TPU v7x, 32 devices: a whole 2x2x4 slice. The times are simulated.
32 devices in a mesh: tok: 16 (over z, y, core), head: 2 (over x).
Axes of the slice: x: 2, y: 2, z: 4, core: 2. Of those that a mesh axis runs over, the one named last changes fastest.
Arguments:
- queries: bfloat16 [4096, 4096], P(('tok', 'head')), may hold values from -60 to 60
- key_states: bfloat16 [4096, 1024], P(('tok', 'head')), may hold values from -60 to 60
- value_states: bfloat16 [4096, 1024], P(('tok', 'head')), may hold values from -6 to 6
- query_gain: float32 [128], replicated, may hold values from 0.5 to 6
- key_gain: float32 [128], replicated, may hold values from 0.5 to 6
- lengths: int32 [8], replicated, may hold values from 1 to 1024, as said below
- slot_order: int32 [16, 24], P('tok'), may hold values from 0 to 23, each once within a row
Outputs:
- attention: bfloat16 [4096, 4096], P('tok', 'head')
- page_pool: bfloat16 [384, 16, 8, 256], P('tok', None, 'head')
Inputs may be any that keep to these rules, and one draw needn't show every extreme that they name: `lengths`: they sum to 4096; the first is 8 and the second exactly 1024. `slot_order`: each row is a permutation of the 24 slots.
All inputs are finite; a program needn't handle non-finite values.
Results may differ from a plain program's by a relative error of at most 0.0044.
The roundings to bfloat16 on the way count: a program that leaves them out, or rounds other values in their place, can miss the bound.
Values may be sent and summed in bfloat16 or wider, within the bound.
No kernel may reach another device: no remote copies, remote signals or barrier semaphores. Data moves between devices by JAX's collectives and lax.ppermute only.
A program may use at most 64 MiB of HBM per device.

v0:
```python
import math

import jax
import jax.numpy as jnp
from jax import lax
from jax.sharding import PartitionSpec as P

HEAD_DIM = 128
REACH = 4
PAGE = 16


def from_behind(x, axis, by):
    peers = lax.axis_size(axis)
    pairs = [(i, i + by) for i in range(peers) if 0 <= i + by < peers]
    return lax.ppermute(x, axis, pairs)


def seg_table(lengths):
    seg_ends = jnp.cumsum(lengths)
    seg_starts = seg_ends - lengths
    return (seg_starts, seg_ends)


def locate(points, seg_starts, seg_ends):
    segment = jnp.sum((points[:, None] >= seg_starts[None, :]).astype(jnp.int32), axis=1) - 1
    onehot = segment[:, None] == jnp.arange(seg_starts.shape[0], dtype=jnp.int32)[None, :]
    first = jnp.sum(jnp.where(onehot, seg_starts[None, :], 0), axis=1)
    finish = jnp.sum(jnp.where(onehot, seg_ends[None, :], 0), axis=1)
    return (segment, first, finish)


def rms_scale(tensor, gain_vec):
    power_mean = jnp.mean(tensor * tensor, axis=-1, keepdims=True)
    return tensor * lax.rsqrt(power_mean + 1e-06) * gain_vec


def rotary(tensor, offset):
    half_dim = tensor.shape[-1] // 2
    frequency = jnp.exp(
        jnp.arange(half_dim, dtype=jnp.float32) * (-2.0 * math.log(1000000.0) / tensor.shape[-1])
    )
    angles = offset.astype(jnp.float32)[:, None] * frequency[None, :]
    cosine = jnp.concatenate([jnp.cos(angles), jnp.cos(angles)], axis=-1)[:, None, :]
    sine_rows = jnp.concatenate([jnp.sin(angles), jnp.sin(angles)], axis=-1)[:, None, :]
    turned = jnp.concatenate([-tensor[..., half_dim:], tensor[..., :half_dim]], axis=-1)
    return tensor * cosine + turned * sine_rows


def on_device(queries, key_states, value_states, query_gain, key_gain, lengths, slot_order):
    q_local, k_local, v_local = (
        lax.all_to_all(queries, "head", split_axis=1, concat_axis=0, tiled=True),
        lax.all_to_all(key_states, "head", split_axis=1, concat_axis=0, tiled=True),
        lax.all_to_all(value_states, "head", split_axis=1, concat_axis=0, tiled=True),
    )
    head_dim = HEAD_DIM
    shard_rows = q_local.shape[0]
    q_heads = q_local.shape[1] // head_dim
    kv_local = k_local.shape[1] // head_dim
    group_size = q_heads // kv_local
    tok_index = lax.axis_index("tok")
    base_row = tok_index * shard_rows
    seg_starts, seg_ends = seg_table(lengths)
    points = base_row + jnp.arange(shard_rows, dtype=jnp.int32)
    segment, first, finish = locate(points, seg_starts, seg_ends)
    offset = points - first
    q_rot = rotary(
        rms_scale(q_local.astype(jnp.float32).reshape(shard_rows, q_heads, head_dim), query_gain),
        offset,
    ).astype(jnp.bfloat16)
    k_rot = rotary(
        rms_scale(k_local.astype(jnp.float32).reshape(shard_rows, kv_local, head_dim), key_gain),
        offset,
    ).astype(jnp.bfloat16)
    paired = jnp.concatenate([k_rot, v_local.reshape(shard_rows, kv_local, head_dim)], axis=-1)
    sources = [(paired, 0)]
    for distance in range(1, REACH + 1):
        sources.append((from_behind(paired, "tok", distance), distance))
    block_rows = min(128, shard_rows)
    blocks = shard_rows // block_rows
    score_scale = 1.0 / math.sqrt(head_dim)
    key_info = []
    for source, distance in sources:
        key_points = base_row - distance * shard_rows + jnp.arange(shard_rows, dtype=jnp.int32)
        key_info.append((source, key_points, locate(key_points, seg_starts, seg_ends)[0]))

    def attend(inputs):
        query_tile, query_pos, query_seg = inputs
        state = (
            jnp.full((kv_local, block_rows, group_size), -1e30, jnp.float32),
            jnp.zeros((kv_local, block_rows, group_size), jnp.float32),
            jnp.zeros((kv_local, block_rows, group_size, head_dim), jnp.float32),
        )
        for source, key_points, key_seg in key_info:
            visible = (query_seg[:, None] == key_seg[None, :]) & (
                key_points[None, :] <= query_pos[:, None]
            )

            def update(current, source=source, visible=visible):
                run_max, run_sum, accum = current
                scores = (
                    jnp.einsum(
                        "qgrd,kgd->gqrk",
                        query_tile,
                        source[..., :head_dim],
                        preferred_element_type=jnp.float32,
                    )
                    * score_scale
                )
                masked = visible[None, :, None, :]
                scores = jnp.where(masked, scores, -1e30)
                new_max = jnp.maximum(run_max, jnp.max(scores, axis=-1))
                expo = jnp.where(masked, jnp.exp(scores - new_max[..., None]), 0.0)
                factor = jnp.exp(run_max - new_max)
                run_sum = run_sum * factor + jnp.sum(expo, axis=-1)
                mixed = jnp.einsum(
                    "gqrk,kgd->gqrd",
                    expo.astype(jnp.bfloat16),
                    source[..., head_dim:],
                    preferred_element_type=jnp.float32,
                )
                accum = accum * factor[..., None] + mixed
                return (new_max, run_sum, accum)

            state = lax.cond(jnp.any(visible), update, lambda current: current, state)
        run_max, run_sum, accum = state
        return accum / run_sum[..., None]

    tiles = q_rot.reshape(blocks, block_rows, kv_local, group_size, head_dim)
    result = lax.map(
        attend, (tiles, points.reshape(blocks, block_rows), segment.reshape(blocks, block_rows))
    )
    attention = (
        jnp.transpose(result, (0, 2, 1, 3, 4))
        .reshape(shard_rows, q_heads * head_dim)
        .astype(jnp.bfloat16)
    )
    tail_rows = from_behind(paired[shard_rows - PAGE :], "tok", 1)
    extended = jnp.concatenate([tail_rows, paired], axis=0)
    ext_points = base_row - PAGE + jnp.arange(PAGE + shard_rows, dtype=jnp.int32)
    ext_segment, ext_first, ext_finish = locate(ext_points, seg_starts, seg_ends)
    ext_offset = ext_points - ext_first
    page_last = jnp.minimum(ext_first + (ext_offset // PAGE + 1) * PAGE, ext_finish) - 1
    owned = (ext_segment >= 0) & (page_last // shard_rows == tok_index)
    page_ends = (offset % PAGE == PAGE - 1) | (points == finish - 1)
    flags = page_ends.astype(jnp.int32)
    before = jnp.cumsum(flags) - flags
    local_last = jnp.clip(page_last - base_row, 0, shard_rows - 1)
    rank_rows = before[local_last]
    pool_pages = slot_order.shape[1]
    slot_ids = jnp.sum(
        jnp.where(
            rank_rows[:, None] == jnp.arange(pool_pages, dtype=jnp.int32)[None, :],
            slot_order[0][None, :],
            0,
        ),
        axis=1,
    )
    target = jnp.where(owned, slot_ids * PAGE + ext_offset % PAGE, pool_pages * PAGE)
    page_pool = (
        jnp.zeros((pool_pages * PAGE, kv_local, 2 * head_dim), jnp.bfloat16)
        .at[target]
        .set(extended, mode="drop")
    )
    page_pool = page_pool.reshape(pool_pages, PAGE, kv_local, 2 * head_dim)
    return (attention, page_pool)


def solution(mesh):
    in_specs = (
        P(("tok", "head"), None),
        P(("tok", "head"), None),
        P(("tok", "head"), None),
        P(),
        P(),
        P(),
        P("tok", None),
    )
    out_specs = (P("tok", "head"), P("tok", None, "head", None))
    return jax.shard_map(
        on_device, mesh=mesh, in_specs=in_specs, out_specs=out_specs, check_vma=False
    )
```

profile of v0, /device:TPU:5, one launch (start us, length us, event | category | flops | bytes accessed | tf_op | source)
XLA Modules:
  0.0 142.8 jit_solution(2072357013520851533)
XLA Ops:
  0.6 1.8 %copy.119 = bf16[16,2,8,512]{3,2,0,1:T(8,128)(2,1)} copy(bf16[16,2,8,512]{3,2,1,0:T(8,128)(2,1)} %bitcast.175) | data formatting | bytes 524288 | tf_op jit(solution)/shard_map/all_to_all | solution.py:53
  2.4 3.4 %all-to-all-start.1 = ((bf16[128,2,512]{2,0,1:T(8,128)(2,1)}), bf16[128,2,512]{2,0,1:T(8,128)(2,1)S(1)}, u32[]{:S(2)}, u32[]{:S(2)}) async-start(bf16[128,2,512]{2,0,1:T(8,128)(2,1)} %bitcast.116), calls=%async_computation.1 | async-start | bytes 524288 | tf_op jit(solution)/shard_map/all_to_all | solution.py:53
  9.9 2.5 %gather_fusion = s32[272]{0:T(512)S(1)} fusion(s32[256]{0:T(256)S(1)} %get-tuple-element.506, s32[1024]{0:T(1024)S(1)} %pad_clamp_fusion), kind=kCustom, calls=%fused_computation | custom fusion | bytes 3264 | tf_op jit(solution)/shard_map/gather | solution.py:149
  17.9 3.4 %all-to-all-start.2 = ((bf16[128,2,512]{2,0,1:T(8,128)(2,1)}), bf16[128,2,512]{2,0,1:T(8,128)(2,1)S(1)}, u32[]{:S(2)}, u32[]{:S(2)}) async-start(bf16[128,2,512]{2,0,1:T(8,128)(2,1)} %bitcast.115), calls=%async_computation.2 | async-start | bytes 524288 | tf_op jit(solution)/shard_map/all_to_all | solution.py:54
  22.7 3.2 %all-to-all-done.2 = bf16[128,2,512]{2,0,1:T(8,128)(2,1)S(1)} async-done(((bf16[128,2,512]{2,0,1:T(8,128)(2,1)}), bf16[128,2,512]{2,0,1:T(8,128)(2,1)S(1)}, u32[]{:S(2)}, u32[]{:S(2)}) %all-to-all-start.2) | async-done | bytes 262176 | tf_op jit(solution)/shard_map/all_to_all | solution.py:54
  25.9 3.6 %all-to-all-start = ((bf16[128,2,2048]{0,2,1:T(8,128)(2,1)}), bf16[128,2,2048]{0,2,1:T(8,128)(2,1)S(1)}, u32[]{:S(2)}, u32[]{:S(2)}) async-start(bf16[128,2,2048]{0,2,1:T(8,128)(2,1)} %bitcast.23), calls=%async_computation | async-start | bytes 2097152 | tf_op jit(solution)/shard_map/all_to_all | solution.py:52
  31.1 4.6 %collective-permute-start.4 = (bf16[16,4,256]{2,1,0:T(4,128)(2,1)S(1)}, bf16[16,4,256]{2,1,0:T(4,128)(2,1)S(1)}, u32[]{:S(2)}, u32[]{:S(2)}) collective-permute-start(bf16[16,4,256]{2,1,0:T(4,128)(2,1)S(1)} %fusion.100), channel_id=1, source_target_pairs={{0,2},{2,4},{4,6},{6,8},{8,10},{10,12},{12,14},{14,16},{16,18},{18... | collective-permute-start | bytes 98312 | tf_op jit(solution)/shard_map/ppermute | solution.py:16
  36.8 1.9 %collective-permute-start = (bf16[256,4,256]{2,1,0:T(4,128)(2,1)}, bf16[256,4,256]{2,1,0:T(4,128)(2,1)}, u32[]{:S(2)}, u32[]{:S(2)}) collective-permute-start(bf16[256,4,256]{2,1,0:T(4,128)(2,1)} %pad_maximum_fusion), channel_id=1, source_target_pairs={{0,2},{2,4},{4,6},{6,8},{8,10},{10,12},{12,14},{14,16},{16,18},{18... | collective-permute-start | bytes 1572872 | tf_op jit(solution)/shard_map/ppermute | solution.py:16
  38.7 3.1 %collective-permute-start.1 = (bf16[256,4,256]{2,1,0:T(4,128)(2,1)}, bf16[256,4,256]{2,1,0:T(4,128)(2,1)}, u32[]{:S(2)}, u32[]{:S(2)}) collective-permute-start(bf16[256,4,256]{2,1,0:T(4,128)(2,1)} %pad_maximum_fusion), channel_id=1, source_target_pairs={{0,4},{2,6},{4,8},{6,10},{8,12},{10,14},{12,16},{14,18},{16,20},{1... | collective-permute-start | bytes 1572872 | tf_op jit(solution)/shard_map/ppermute | solution.py:16
  41.8 3.9 %collective-permute-start.2 = (bf16[256,4,256]{2,1,0:T(4,128)(2,1)}, bf16[256,4,256]{2,1,0:T(4,128)(2,1)}, u32[]{:S(2)}, u32[]{:S(2)}) collective-permute-start(bf16[256,4,256]{2,1,0:T(4,128)(2,1)} %pad_maximum_fusion), channel_id=1, source_target_pairs={{0,6},{2,8},{4,10},{6,12},{8,14},{10,16},{12,18},{14,20},{16,22},{... | collective-permute-start | bytes 1572872 | tf_op jit(solution)/shard_map/ppermute | solution.py:16
  45.7 4.0 %collective-permute-start.3 = (bf16[256,4,256]{2,1,0:T(4,128)(2,1)}, bf16[256,4,256]{2,1,0:T(4,128)(2,1)}, u32[]{:S(2)}, u32[]{:S(2)}) collective-permute-start(bf16[256,4,256]{2,1,0:T(4,128)(2,1)} %pad_maximum_fusion), channel_id=1, source_target_pairs={{0,8},{2,10},{4,12},{6,14},{8,16},{10,18},{12,20},{14,22},{16,24},... | collective-permute-start | bytes 1572872 | tf_op jit(solution)/shard_map/ppermute | solution.py:16
  51.0 8.6 %scatter_fusion = bf16[384,4,256]{2,1,0:T(4,128)(2,1)S(1)} fusion(bf16[384,4,256]{2,1,0:T(4,128)(2,1)S(1)} %broadcast_in_dim.225, s32[272]{0:T(512)S(1)} %fusion.103, bf16[272,4,256]{2,1,0:T(4,128)(2,1)S(1)} %maximum_maximum_fusion), kind=kCustom, calls=%fused_computation.1 | custom fusion | bytes 1672256 | tf_op jit(solution)/shard_map/scatter | solution.py:163
  62.2 1.8 %copy.83 = f32[2,128,2048]{2,1,0:T(8,128)} copy(f32[2,128,2048]{1,2,0:T(8,128)S(1)} %get-tuple-element.499) | data formatting | bytes 4194304 | tf_op jit(solution)/shard_map/convert_element_type | solution.py:68
  64.0 2.0 %copy.114 = f32[32,8,16,128]{3,2,1,0:T(8,128)S(1)} copy(f32[32,8,16,128]{3,1,2,0:T(8,128)} %bitcast.155) | data formatting | bytes 4194304
  66.6 1.8 %copy.86 = f32[256,16,128]{0,2,1:T(8,128)} copy(f32[256,16,128]{2,1,0:T(8,128)S(1)} %bitcast.153) | data formatting | bytes 4194304 | tf_op jit(solution)/shard_map/convert_element_type | solution.py:68
  68.5 1.9 %multiply_multiply_fusion = f32[256,16,128]{0,2,1:T(8,128)S(1)} fusion(f32[256,16,128]{0,2,1:T(8,128)} %copy.86, f32[128]{0:T(128)S(1)} %copy-done.21, f32[256,16]{0,1:T(8,128)S(1)} %add_rsqrt_fusion.1), kind=kLoop, calls=%fused_computation.130 | loop fusion | flops 1048576 | bytes 4211200 | tf_op jit(solution)/shard_map/mul | solution.py:35
  75.0 1.9 %copy.96 = bf16[256,4,256]{2,0,1:T(8,128)(2,1)} copy(bf16[256,4,256]{2,1,0:T(4,128)(2,1)} %collective-permute-done) | data formatting | bytes 1048576
  77.0 1.9 %copy.97 = bf16[256,4,256]{2,0,1:T(8,128)(2,1)} copy(bf16[256,4,256]{2,1,0:T(4,128)(2,1)} %collective-permute-done.1) | data formatting | bytes 1048576
  78.9 1.9 %copy.98 = bf16[256,4,256]{2,0,1:T(8,128)(2,1)} copy(bf16[256,4,256]{2,1,0:T(4,128)(2,1)} %collective-permute-done.2) | data formatting | bytes 1048576
  80.8 1.9 %copy.99 = bf16[256,4,256]{2,0,1:T(8,128)(2,1)} copy(bf16[256,4,256]{2,1,0:T(4,128)(2,1)} %collective-permute-done.3) | data formatting | bytes 1048576
  82.8 56.3 %while.11 = (s32[]{:T(128)}, bf16[2,4,128,4,128]{4,2,3,1,0:T(8,128)(2,1)}, s32[2,128]{1,0:T(2,128)}, s32[256]{0:T(256)S(1)}, s32[2,128]{1,0:T(2,128)}, /*index=5...) while((s32[]{:T(128)}, ...), condition=%wide.region_35.36_spmd.clone, body=%wide.region_9.35_spmd.clone.sunk | while | flops 1379558656 | bytes 61062528 | solution.py:130
  85.6 5.4 %conditional.15 = (f32[4,128,4]{1,2,0:T(4,128)}, f32[4,128,4]{1,2,0:T(4,128)S(1)}, f32[4,128,4,128]{3,1,2,0:T(8,128)S(1)}) conditional(s32[]{:T(128)} %convert_element_type.180, () %tuple.132, (pred[128,256]{1,0:T(8,128)(4,1)S(1)}, bf16[128,4,4,128]{3,0,2,1:T(8,128)(2,1)S(1)}, bf16[256,4,128]{2,0,1:T(8,128)(2,1)S(1)}, ...), branch_computations={%region_15.15_spmd, %region_16.18_spmd} | conditional | flops 275521536 | bytes 8577048 | solution.py:125
  86.8 2.0 %convolution_add_fusion = f32[4,128,4,128]{3,1,2,0:T(8,128)S(1)} fusion(f32[4,128,4,256]{3,1,2,0:T(8,128)S(1)} %get-tuple-element.473, f32[4,128,4]{1,2,0:T(4,128)} %get-tuple-element.716, pred[128,256]{1,0:T(8,128)(4,1)S(1)} %get-tuple-element.162, f32[4,128,4]{1,2,0:T(4,128)S(1)} %get-tuple-element.452, bf16[256,4,128]{2,0,1:T(8,128)(2,1)S(1)} %get-tuple-element.165), kind=kOutput, calls=%fused_computation.12 | convolution fusion | flops 137101312 | bytes 3457024 | tf_op jit(solution)/shard_map/while/body/eval_jaxpr/cond/branch_1_fun/gqrk,kgd->gqrd/dot_general | solution.py:116
  91.6 5.8 %conditional.16 = ((f32[4,128,4]{1,2,0:T(4,128)}, f32[4,128,4]{1,2,0:T(4,128)S(1)}, f32[4,128,4,128]{3,1,2,0:T(8,128)S(1)})) conditional(s32[]{:T(128)} %convert_element_type.179, (f32[4,128,4]{1,2,0:T(4,128)}, f32[4,128,4]{1,2,0:T(4,128)S(1)}, f32[4,128,4,128]{3,1,2,0:T(8,128)S(1)}) %conditional.15, (pred[128,256]{1,0:T(8,128)(4,1)S(1)}, ...), branch_computations={%region_19.19_spmd, %region_20.22_spmd} | conditional | flops 275779584 | bytes 11763772 | solution.py:125
  98.0 4.7 %conditional.17 = ((f32[4,128,4]{1,2,0:T(4,128)}, f32[4,128,4]{1,2,0:T(4,128)S(1)}, f32[4,128,4,128]{3,1,2,0:T(8,128)S(1)})) conditional(s32[]{:T(128)} %convert_element_type.178, (f32[4,128,4]{1,2,0:T(4,128)}, f32[4,128,4]{1,2,0:T(4,128)S(1)}, f32[4,128,4,128]{3,1,2,0:T(8,128)S(1)}) %get-tuple-element.807, (pred[128,256]{1,0:T(8,128)(4,1)S(1)}, ...), branch_computations={%region_23.23_spmd, %region_24.26_spmd} | conditional | flops 275779584 | bytes 9666592 | solution.py:125
  103.4 5.8 %conditional.18 = ((f32[4,128,4]{1,2,0:T(4,128)}, f32[4,128,4]{1,2,0:T(4,128)S(1)}, f32[4,128,4,128]{3,1,2,0:T(8,128)S(1)})) conditional(s32[]{:T(128)} %convert_element_type.177, (f32[4,128,4]{1,2,0:T(4,128)}, f32[4,128,4]{1,2,0:T(4,128)S(1)}, f32[4,128,4,128]{3,1,2,0:T(8,128)S(1)}) %get-tuple-element.808, (pred[128,256]{1,0:T(8,128)(4,1)S(1)}, ...), branch_computations={%region_27.27_spmd, %region_28.30_spmd} | conditional | flops 275779584 | bytes 11763772 | solution.py:125
  113.7 5.4 %conditional.15 = (f32[4,128,4]{1,2,0:T(4,128)}, f32[4,128,4]{1,2,0:T(4,128)S(1)}, f32[4,128,4,128]{3,1,2,0:T(8,128)S(1)}) conditional(s32[]{:T(128)} %convert_element_type.180, () %tuple.132, (pred[128,256]{1,0:T(8,128)(4,1)S(1)}, bf16[128,4,4,128]{3,0,2,1:T(8,128)(2,1)S(1)}, bf16[256,4,128]{2,0,1:T(8,128)(2,1)S(1)}, ...), branch_computations={%region_15.15_spmd, %region_16.18_spmd} | conditional | flops 275521536 | bytes 8577048 | solution.py:125
  114.9 2.0 %convolution_add_fusion = f32[4,128,4,128]{3,1,2,0:T(8,128)S(1)} fusion(f32[4,128,4,256]{3,1,2,0:T(8,128)S(1)} %get-tuple-element.473, f32[4,128,4]{1,2,0:T(4,128)} %get-tuple-element.716, pred[128,256]{1,0:T(8,128)(4,1)S(1)} %get-tuple-element.162, f32[4,128,4]{1,2,0:T(4,128)S(1)} %get-tuple-element.452, bf16[256,4,128]{2,0,1:T(8,128)(2,1)S(1)} %get-tuple-element.165), kind=kOutput, calls=%fused_computation.12 | convolution fusion | flops 137101312 | bytes 3457024 | tf_op jit(solution)/shard_map/while/body/eval_jaxpr/cond/branch_1_fun/gqrk,kgd->gqrd/dot_general | solution.py:116
  119.7 5.8 %conditional.16 = ((f32[4,128,4]{1,2,0:T(4,128)}, f32[4,128,4]{1,2,0:T(4,128)S(1)}, f32[4,128,4,128]{3,1,2,0:T(8,128)S(1)})) conditional(s32[]{:T(128)} %convert_element_type.179, (f32[4,128,4]{1,2,0:T(4,128)}, f32[4,128,4]{1,2,0:T(4,128)S(1)}, f32[4,128,4,128]{3,1,2,0:T(8,128)S(1)}) %conditional.15, (pred[128,256]{1,0:T(8,128)(4,1)S(1)}, ...), branch_computations={%region_19.19_spmd, %region_20.22_spmd} | conditional | flops 275779584 | bytes 11763772 | solution.py:125
  126.1 4.7 %conditional.17 = ((f32[4,128,4]{1,2,0:T(4,128)}, f32[4,128,4]{1,2,0:T(4,128)S(1)}, f32[4,128,4,128]{3,1,2,0:T(8,128)S(1)})) conditional(s32[]{:T(128)} %convert_element_type.178, (f32[4,128,4]{1,2,0:T(4,128)}, f32[4,128,4]{1,2,0:T(4,128)S(1)}, f32[4,128,4,128]{3,1,2,0:T(8,128)S(1)}) %get-tuple-element.807, (pred[128,256]{1,0:T(8,128)(4,1)S(1)}, ...), branch_computations={%region_23.23_spmd, %region_24.26_spmd} | conditional | flops 275779584 | bytes 9666592 | solution.py:125
  131.5 5.7 %conditional.18 = ((f32[4,128,4]{1,2,0:T(4,128)}, f32[4,128,4]{1,2,0:T(4,128)S(1)}, f32[4,128,4,128]{3,1,2,0:T(8,128)S(1)})) conditional(s32[]{:T(128)} %convert_element_type.177, (f32[4,128,4]{1,2,0:T(4,128)}, f32[4,128,4]{1,2,0:T(4,128)S(1)}, f32[4,128,4,128]{3,1,2,0:T(8,128)S(1)}) %get-tuple-element.808, (pred[128,256]{1,0:T(8,128)(4,1)S(1)}, ...), branch_computations={%region_27.27_spmd, %region_28.30_spmd} | conditional | flops 275779584 | bytes 11763772 | solution.py:125
  139.1 2.0 %copy.100 = bf16[2,128,4,4,128]{4,3,2,1,0:T(4,128)(2,1)S(1)} copy(bf16[2,128,4,4,128]{4,1,3,2,0:T(8,128)(2,1)} %bitcast.169) | data formatting | bytes 2097152 | tf_op jit(solution)/shard_map/convert_element_type | solution.py:136
  (194 shorter events, 69.4 us)
Async XLA Ops:
  0.6 11.8 %copy-start.23 = (s32[1,24]{1,0:T(1,128)S(1)}, s32[1,24]{1,0:T(1,128)}, u32[]{:S(2)}) copy-start(s32[1,24]{1,0:T(1,128)} %param.25) | copy-start | bytes 292
  0.6 14.3 %copy-start.6 = (bf16[128,4096]{1,0:T(8,128)(2,1)S(1)}, bf16[128,4096]{1,0:T(8,128)(2,1)}, u32[]{:S(2)}) copy-start(bf16[128,4096]{1,0:T(8,128)(2,1)} %param.19) | copy-start | bytes 3145732
  2.4 15.5 %all-to-all-start.1 = ((bf16[128,2,512]{2,0,1:T(8,128)(2,1)}), bf16[128,2,512]{2,0,1:T(8,128)(2,1)S(1)}, u32[]{:S(2)}, u32[]{:S(2)}) async-start(bf16[128,2,512]{2,0,1:T(8,128)(2,1)} %bitcast.116), calls=%async_computation.1 | async-start | bytes 524288 | tf_op jit(solution)/shard_map/all_to_all | solution.py:53
  9.9 6.3 %copy-start.8 = (bf16[128,1024]{1,0:T(8,128)(2,1)S(1)}, bf16[128,1024]{1,0:T(8,128)(2,1)}, u32[]{:S(2)}) copy-start(bf16[128,1024]{1,0:T(8,128)(2,1)} %param.21) | copy-start | bytes 786436
  16.2 5.7 %copy-start.20 = (f32[128]{0:T(128)S(1)}, f32[128]{0:T(128)}, u32[]{:S(2)}) copy-start(f32[128]{0:T(128)} %param.23) | copy-start | bytes 1540
  17.9 8.0 %all-to-all-start.2 = ((bf16[128,2,512]{2,0,1:T(8,128)(2,1)}), bf16[128,2,512]{2,0,1:T(8,128)(2,1)S(1)}, u32[]{:S(2)}, u32[]{:S(2)}) async-start(bf16[128,2,512]{2,0,1:T(8,128)(2,1)} %bitcast.115), calls=%async_computation.2 | async-start | bytes 524288 | tf_op jit(solution)/shard_map/all_to_all | solution.py:54
  22.3 7.2 %copy-start.7 = (f32[256,128]{1,0:T(8,128)S(1)}, f32[256,128]{1,0:T(8,128)}, u32[]{:S(2)}) copy-start(f32[256,128]{1,0:T(8,128)} %get-tuple-element.516) | copy-start | bytes 393220
  25.9 34.7 %all-to-all-start = ((bf16[128,2,2048]{0,2,1:T(8,128)(2,1)}), bf16[128,2,2048]{0,2,1:T(8,128)(2,1)S(1)}, u32[]{:S(2)}, u32[]{:S(2)}) async-start(bf16[128,2,2048]{0,2,1:T(8,128)(2,1)} %bitcast.23), calls=%async_computation | async-start | bytes 2097152 | tf_op jit(solution)/shard_map/all_to_all | solution.py:52
  31.1 19.4 %collective-permute-start.4 = (bf16[16,4,256]{2,1,0:T(4,128)(2,1)S(1)}, bf16[16,4,256]{2,1,0:T(4,128)(2,1)S(1)}, u32[]{:S(2)}, u32[]{:S(2)}) collective-permute-start(bf16[16,4,256]{2,1,0:T(4,128)(2,1)S(1)} %fusion.100), channel_id=1, source_target_pairs={{0,2},{2,4},{4,6},{6,8},{8,10},{10,12},{12,14},{14,16},{16,18},{18... | collective-permute-start | bytes 98312 | tf_op jit(solution)/shard_map/ppermute | solution.py:16
  36.8 38.3 %collective-permute-start = (bf16[256,4,256]{2,1,0:T(4,128)(2,1)}, bf16[256,4,256]{2,1,0:T(4,128)(2,1)}, u32[]{:S(2)}, u32[]{:S(2)}) collective-permute-start(bf16[256,4,256]{2,1,0:T(4,128)(2,1)} %pad_maximum_fusion), channel_id=1, source_target_pairs={{0,2},{2,4},{4,6},{6,8},{8,10},{10,12},{12,14},{14,16},{16,18},{18... | collective-permute-start | bytes 1572872 | tf_op jit(solution)/shard_map/ppermute | solution.py:16
  38.7 38.3 %collective-permute-start.1 = (bf16[256,4,256]{2,1,0:T(4,128)(2,1)}, bf16[256,4,256]{2,1,0:T(4,128)(2,1)}, u32[]{:S(2)}, u32[]{:S(2)}) collective-permute-start(bf16[256,4,256]{2,1,0:T(4,128)(2,1)} %pad_maximum_fusion), channel_id=1, source_target_pairs={{0,4},{2,6},{4,8},{6,10},{8,12},{10,14},{12,16},{14,18},{16,20},{1... | collective-permute-start | bytes 1572872 | tf_op jit(solution)/shard_map/ppermute | solution.py:16
  41.8 37.1 %collective-permute-start.2 = (bf16[256,4,256]{2,1,0:T(4,128)(2,1)}, bf16[256,4,256]{2,1,0:T(4,128)(2,1)}, u32[]{:S(2)}, u32[]{:S(2)}) collective-permute-start(bf16[256,4,256]{2,1,0:T(4,128)(2,1)} %pad_maximum_fusion), channel_id=1, source_target_pairs={{0,6},{2,8},{4,10},{6,12},{8,14},{10,16},{12,18},{14,20},{16,22},{... | collective-permute-start | bytes 1572872 | tf_op jit(solution)/shard_map/ppermute | solution.py:16
  45.7 35.1 %collective-permute-start.3 = (bf16[256,4,256]{2,1,0:T(4,128)(2,1)}, bf16[256,4,256]{2,1,0:T(4,128)(2,1)}, u32[]{:S(2)}, u32[]{:S(2)}) collective-permute-start(bf16[256,4,256]{2,1,0:T(4,128)(2,1)} %pad_maximum_fusion), channel_id=1, source_target_pairs={{0,8},{2,10},{4,12},{6,14},{8,16},{10,18},{12,20},{14,22},{16,24},... | collective-permute-start | bytes 1572872 | tf_op jit(solution)/shard_map/ppermute | solution.py:16
  66.6 2.0 %copy-start.21 = (f32[128]{0:T(128)S(1)}, f32[128]{0:T(128)}, u32[]{:S(2)}) copy-start(f32[128]{0:T(128)} %param.22) | copy-start | bytes 1540
  71.8 1.6 %copy-start = (f32[128,2,2048]{0,2,1:T(8,128)S(1)}, f32[128,2,2048]{0,2,1:T(8,128)}, u32[]{:S(2)}) copy-start(f32[128,2,2048]{0,2,1:T(8,128)} %get-tuple-element.498) | copy-start | bytes 6291460
  71.8 1.6 %copy-start.22 = (f32[128]{0:T(128)S(1)}, f32[128]{0:T(128)}, u32[]{:S(2)}) copy-start(f32[128]{0:T(128)} %param.22) | copy-start | bytes 1540
  75.0 7.8 %copy-start.9 = (bf16[256,4,128]{2,0,1:T(8,128)(2,1)S(1)}, bf16[256,4,128]{2,0,1:T(8,128)(2,1)}, u32[]{:S(2)}) copy-start(bf16[256,4,128]{2,0,1:T(8,128)(2,1)} %copy.95) | copy-start | bytes 786436
  75.0 7.8 %copy-start.12 = (s32[256]{0:T(256)S(1)}, s32[256]{0:T(256)}, u32[]{:S(2)}) copy-start(s32[256]{0:T(256)} %copy-done.11) | copy-start | bytes 3076
  75.0 7.8 %copy-start.13 = (s32[256]{0:T(256)S(1)}, s32[256]{0:T(256)}, u32[]{:S(2)}) copy-start(s32[256]{0:T(256)} %get-tuple-element.746) | copy-start | bytes 3076
  75.0 7.8 %copy-start.14 = (s32[256]{0:T(256)S(1)}, s32[256]{0:T(256)}, u32[]{:S(2)}) copy-start(s32[256]{0:T(256)} %get-tuple-element.744) | copy-start | bytes 3076
  75.0 7.8 %copy-start.16 = (s32[256]{0:T(256)S(1)}, s32[256]{0:T(256)}, u32[]{:S(2)}) copy-start(s32[256]{0:T(256)} %get-tuple-element.748) | copy-start | bytes 3076
  75.0 7.8 %copy-start.18 = (s32[256]{0:T(256)S(1)}, s32[256]{0:T(256)}, u32[]{:S(2)}) copy-start(s32[256]{0:T(256)} %get-tuple-element.747) | copy-start | bytes 3076
  91.6 5.8 %copy-start.2 = (bf16[256,4,256]{2,0,1:T(8,128)(2,1)S(1)}, bf16[256,4,256]{2,0,1:T(8,128)(2,1)}, u32[]{:S(2)}) copy-start(bf16[256,4,256]{2,0,1:T(8,128)(2,1)} %get-tuple-element.798) | copy-start | bytes 1572868 | tf_op jit(solution)/shard_map/while
  91.6 4.0 %copy-start.1 = (bf16[256,4,256]{2,0,1:T(8,128)(2,1)S(1)}, bf16[256,4,256]{2,0,1:T(8,128)(2,1)}, u32[]{:S(2)}) copy-start(bf16[256,4,256]{2,0,1:T(8,128)(2,1)} %get-tuple-element.169) | copy-start | bytes 1572868 | tf_op jit(solution)/shard_map/while/body/eval_jaxpr/cond
  103.4 4.0 %copy-start.3 = (bf16[256,4,256]{2,0,1:T(8,128)(2,1)S(1)}, bf16[256,4,256]{2,0,1:T(8,128)(2,1)}, u32[]{:S(2)}) copy-start(bf16[256,4,256]{2,0,1:T(8,128)(2,1)} %get-tuple-element.181) | copy-start | bytes 1572868 | tf_op jit(solution)/shard_map/while/body/eval_jaxpr/cond
  109.8 1.2 copy-start.10
  109.9 1.2 copy-start.15
  119.7 5.8 %copy-start.2 = (bf16[256,4,256]{2,0,1:T(8,128)(2,1)S(1)}, bf16[256,4,256]{2,0,1:T(8,128)(2,1)}, u32[]{:S(2)}) copy-start(bf16[256,4,256]{2,0,1:T(8,128)(2,1)} %get-tuple-element.798) | copy-start | bytes 1572868 | tf_op jit(solution)/shard_map/while
  119.7 4.0 %copy-start.1 = (bf16[256,4,256]{2,0,1:T(8,128)(2,1)S(1)}, bf16[256,4,256]{2,0,1:T(8,128)(2,1)}, u32[]{:S(2)}) copy-start(bf16[256,4,256]{2,0,1:T(8,128)(2,1)} %get-tuple-element.169) | copy-start | bytes 1572868 | tf_op jit(solution)/shard_map/while/body/eval_jaxpr/cond
  131.5 3.9 %copy-start.3 = (bf16[256,4,256]{2,0,1:T(8,128)(2,1)S(1)}, bf16[256,4,256]{2,0,1:T(8,128)(2,1)}, u32[]{:S(2)}) copy-start(bf16[256,4,256]{2,0,1:T(8,128)(2,1)} %get-tuple-element.181) | copy-start | bytes 1572868 | tf_op jit(solution)/shard_map/while/body/eval_jaxpr/cond
  137.9 1.2 copy-start.10
  137.9 1.2 copy-start.15
  (6 other events, 6.1 us)
where the time goes:
time: 145 us; the launch traced here: 143 us
  local copies, waits for them, and re-layouts  42.7 us (29%)
  other arithmetic  41 us (28%)
  starting transfers between devices  28 us (19%)
  matrix products  19.8 us (14%)
  loops' own time  6.91 us (5%)
  waiting for transfers between devices  3.24 us (2%)
    ppermute x5, starting transfers between devices, from_behind(): return lax.ppermute(x, axis, pairs)  17.5 us
    unnamed x40, local copies, waits for them, and re-layouts  14.1 us
    dot_general x8, matrix products, update(): jnp.einsum('gqrk,kgd->gqrd', expo.astype(jnp.bfloat16), source[..., head_...  11 us
    dot_general x8, matrix products, update(): jnp.einsum('qgrd,kgd->gqrk', query_tile, source[..., :head_dim], preferre...  8.71 us
    scatter x1, local copies, waits for them, and re-layouts, on_device(): page_pool = jnp.zeros((pool_pages * PAGE, kv_local, 2 * head_dim), jnp.bf...  8.61 us
    reduce_sum x8, other arithmetic, update(): run_sum = run_sum * factor + jnp.sum(expo, axis=-1)  8.6 us
    another operation x1, loops' own time, on_device(): lax.map(attend, (tiles, points.reshape(blocks, block_rows), segment.resha...  6.64 us
    add x8, other arithmetic, update(): run_sum = run_sum * factor + jnp.sum(expo, axis=-1)  5.67 us
  transfers between devices with their start and end apart: 8, of which 1 were waited for; matrix products, arithmetic and copies ran while one was open for 31% of the time, Pallas kernels for 0%

commit v1 on v0

v1 whole, which is shorter than its diff:
```python
import functools
import math

import jax
import jax.numpy as jnp
from jax import lax
from jax.experimental import pallas as pl
from jax.experimental.pallas import tpu as pltpu
from jax.sharding import PartitionSpec as P

D = 128
REACH = 4
PAGE = 16
HIDE = -2e30
FLOOR = -1e30
MIB = 1024 * 1024


def around(x, axis, by):
    peers = lax.axis_size(axis)
    return lax.ppermute(x, axis, [(i, (i + by) % peers) for i in range(peers)])


def core_swap(x):
    peers = lax.axis_size("tok")
    return lax.ppermute(x, "tok", [(i, i ^ 1) for i in range(peers)])


def seg_first(pos, lengths, segs):
    first = jnp.zeros_like(pos)
    start = jnp.int32(0)
    for s in range(segs):
        first = jnp.where(pos >= start, start, first)
        start = start + lengths[s]
    return first


def rotate(x, gain, cosine, sine):
    power = jnp.mean(x * x, axis=-1, keepdims=True)
    x = x * lax.rsqrt(power + 1e-06) * gain
    return x * cosine + pltpu.roll(x, D // 2, 1) * sine


def lanes(ref, index, width):
    return ref[:, pl.ds(pl.multiple_of(index * width, width), width)]


def kv_prep_body(heads, segs, lengths, k_ref, v_ref, gain_ref, cos_ref, sin_ref, *outs):
    rows = k_ref.shape[0]
    kvl = k_ref.shape[1] // D // heads
    x = lax.axis_index("head")
    base = (lax.axis_index("tok") * heads + x) * rows
    pos = base + lax.broadcasted_iota(jnp.int32, (rows, D), 0)
    offset = (pos - seg_first(pos, lengths, segs)).astype(jnp.float32)
    lane = lax.broadcasted_iota(jnp.int32, (rows, D), 1)
    lower = lane < D // 2
    half = jnp.where(lower, lane, lane - D // 2).astype(jnp.float32)
    angles = offset * jnp.exp(half * (-2.0 * math.log(1000000.0) / D))
    cosine = jnp.cos(angles)
    sine = jnp.where(lower, -1.0, 1.0) * jnp.sin(angles)
    cos_ref[...] = cosine
    sin_ref[...] = sine
    gain = gain_ref[...]
    for d in range(heads):
        peer = lax.rem(x + d, heads)
        for j in range(kvl):
            head = peer * kvl + j
            key = lanes(k_ref, head, D).astype(jnp.float32)
            outs[d][:, 2 * j * D : (2 * j + 1) * D] = rotate(key, gain, cosine, sine).astype(
                jnp.bfloat16
            )
            outs[d][:, (2 * j + 1) * D : (2 * j + 2) * D] = lanes(v_ref, head, D)


def q_prep_body(heads, q_ref, gain_ref, cos_ref, sin_ref, *outs):
    ql = q_ref.shape[1] // D // heads
    x = lax.axis_index("head")
    gain, cosine, sine = gain_ref[...], cos_ref[...], sin_ref[...]
    for d in range(heads):
        peer = lax.rem(x + d, heads)
        for j in range(ql):
            query = lanes(q_ref, peer * ql + j, D).astype(jnp.float32)
            outs[d][:, j * D : (j + 1) * D] = rotate(query, gain, cosine, sine).astype(
                jnp.bfloat16
            )


VMEM = pl.BlockSpec(memory_space=pltpu.VMEM)
SMEM = pl.BlockSpec(memory_space=pltpu.SMEM)


def params():
    return pltpu.CompilerParams(vmem_limit_bytes=48 * MIB)


def kv_prep(lengths, keys, values, gain, heads):
    rows, width = keys.shape
    table = jax.ShapeDtypeStruct((rows, D), jnp.float32)
    part = jax.ShapeDtypeStruct((rows, 2 * width // heads), jnp.bfloat16)
    return pl.pallas_call(
        functools.partial(kv_prep_body, heads, lengths.shape[0]),
        out_shape=[table, table] + [part] * heads,
        in_specs=[SMEM, VMEM, VMEM, VMEM],
        out_specs=[VMEM] * (2 + heads),
        compiler_params=params(),
        name="kv_prep",
    )(lengths, keys, values, gain)


def q_prep(queries, gain, cosine, sine, heads):
    rows, width = queries.shape
    part = jax.ShapeDtypeStruct((rows, width // heads), jnp.bfloat16)
    return pl.pallas_call(
        functools.partial(q_prep_body, heads),
        out_shape=[part] * heads,
        in_specs=[VMEM] * 4,
        out_specs=[VMEM] * heads,
        compiler_params=params(),
        name="q_prep",
    )(queries, gain, cosine, sine)


def shard_of(kind, tok):
    core = lax.rem(tok, 2)
    if kind == "own":
        return tok
    if kind == "far":
        return tok - 4
    if kind == "near":
        return tok - 2
    if kind == "near_swap":
        return tok + 1 - 2 * core - 2
    return jnp.where(core == 0, tok - 3, tok - 1)


def attend_body(heads, segs, rows, pieces, first_stage, last_stage, n_q, n_kv, lengths, *refs):
    q_refs, refs = refs[:n_q], refs[n_q:]
    kv_refs, refs = refs[:n_kv], refs[n_kv:]
    if not first_stage:
        m_in, l_in, acc_in = refs[:3]
        refs = refs[3:]
    if last_stage:
        out_ref, refs = refs[0], refs[1:]
    else:
        m_out, l_out, acc_out = refs[:3]
        refs = refs[3:]
    s_scr, bias_scr = refs
    x = lax.axis_index("head")
    tok = lax.axis_index("tok")
    shard_rows = heads * rows
    kvl = kv_refs[0].shape[1] // (2 * D)
    group = q_refs[0].shape[1] // D // kvl
    wide = group * rows
    scale = math.log2(math.e) / math.sqrt(D)
    lane = lax.broadcasted_iota(jnp.int32, (rows, rows), 1)
    sub = lax.broadcasted_iota(jnp.int32, (rows, rows), 0)
    n_piece = len(pieces)

    def one_chunk(d, q_ref, q_row):
        origin = lax.rem(x - d + heads, heads)
        q_pos = tok * shard_rows + origin * rows + lane
        q_first = seg_first(q_pos, lengths, segs)
        for i, (a, row, kind, kd) in enumerate(pieces):
            k_origin = lax.rem(x - kd + heads, heads)
            k_pos = shard_of(kind, tok) * shard_rows + k_origin * rows + sub
            seen = (k_pos >= q_first) & (k_pos <= q_pos)
            bias_scr[i * rows : (i + 1) * rows, :] = jnp.where(seen, 0.0, HIDE)

        def one_group(g, carry):
            q4 = q_ref[pl.ds(q_row, rows), pl.ds(pl.multiple_of(g * group * D, group * D), group * D)]
            q = jnp.concatenate([q4[:, r * D : (r + 1) * D] for r in range(group)], axis=0)
            if first_stage:
                top = jnp.full((8, wide), FLOOR, jnp.float32)
            else:
                top = jnp.broadcast_to(m_in[d, g], (8, wide))
            for i, (a, row, kind, kd) in enumerate(pieces):
                key = kv_refs[a][
                    row * rows : (row + 1) * rows, pl.ds(pl.multiple_of(g * 2 * D, 2 * D), D)
                ]
                score = lax.dot_general(
                    key, q, (((1,), (1,)), ((), ())), preferred_element_type=jnp.float32
                )
                bias = bias_scr[i * rows : (i + 1) * rows, :]
                score = score * scale + jnp.concatenate([bias] * group, axis=1)
                s_scr[i * rows : (i + 1) * rows, :] = score
                top = jnp.maximum(top, jnp.max(score.reshape(rows // 8, 8, wide), axis=0))
            top = jnp.max(top, axis=0, keepdims=True)
            if first_stage:
                total = jnp.zeros((1, wide), jnp.float32)
                acc = jnp.zeros((D, wide), jnp.float32)
            else:
                fade = jnp.exp2(m_in[d, g] - top)
                total = l_in[d, g] * fade
                acc = acc_in[d, g] * fade
            part = jnp.zeros((8, wide), jnp.float32)
            for i, (a, row, kind, kd) in enumerate(pieces):
                value = kv_refs[a][
                    row * rows : (row + 1) * rows, pl.ds(pl.multiple_of(g * 2 * D + D, D), D)
                ]
                expo = jnp.exp2(s_scr[i * rows : (i + 1) * rows, :] - top)
                part = part + jnp.sum(expo.reshape(rows // 8, 8, wide), axis=0)
                acc = acc + lax.dot_general(
                    value,
                    expo.astype(jnp.bfloat16),
                    (((0,), (0,)), ((), ())),
                    preferred_element_type=jnp.float32,
                )
            total = total + jnp.sum(part, axis=0, keepdims=True)
            if last_stage:
                acc = acc * (1.0 / total)
                at = pl.ds(pl.multiple_of(origin * rows, rows), rows)
                for r in range(group):
                    out_ref[at, pl.ds(pl.multiple_of((g * group + r) * D, D), D)] = (
                        acc[:, r * rows : (r + 1) * rows].T.astype(jnp.bfloat16)
                    )
            else:
                m_out[d, g] = top
                l_out[d, g] = total
                acc_out[d, g] = acc
            return carry

        lax.fori_loop(0, kvl, one_group, 0)

    one_chunk(0, q_refs[0], 0)
    if heads == 2:
        one_chunk(1, q_refs[1], 0)
    elif heads > 2:
        def loop_body(d, carry):
            one_chunk(d, q_refs[1], pl.multiple_of((d - 1) * rows, rows))
            return carry

        lax.fori_loop(1, heads, loop_body, 0)


def attend(lengths, qs, kvs, pieces, state, last, heads):
    rows = qs[0].shape[0]
    kvl = kvs[0].shape[1] // (2 * D)
    ql = qs[0].shape[1] // D
    wide = ql // kvl * rows
    if last:
        out_shape = jax.ShapeDtypeStruct((heads * rows, ql * D), jnp.bfloat16)
    else:
        row = jax.ShapeDtypeStruct((heads, kvl, 1, wide), jnp.float32)
        out_shape = [row, row, jax.ShapeDtypeStruct((heads, kvl, D, wide), jnp.float32)]
    inputs = [lengths, *qs, *kvs, *(state or [])]
    work = heads * kvl * wide * len(pieces) * rows
    return pl.pallas_call(
        functools.partial(
            attend_body, heads, lengths.shape[0], rows, pieces, state is None, last,
            len(qs), len(kvs),
        ),
        out_shape=out_shape,
        in_specs=[SMEM] + [VMEM] * (len(inputs) - 1),
        out_specs=VMEM if last else [VMEM] * 3,
        scratch_shapes=[
            pltpu.VMEM((len(pieces) * rows, wide), jnp.float32),
            pltpu.VMEM((len(pieces) * rows, rows), jnp.float32),
        ],
        compiler_params=params(),
        cost_estimate=pl.CostEstimate(
            flops=4 * D * work, bytes_accessed=4 * MIB, transcendentals=work
        ),
        name="attend_last" if last else "attend_part",
    )(*inputs)


def pages_body(heads, segs, pool, lengths, slots, tail_ref, own_ref, rest_ref, out_ref, hot, ends):
    rows = own_ref.shape[0]
    shard_rows = heads * rows
    x = lax.axis_index("head")
    base = lax.axis_index("tok") * shard_rows
    end = jnp.int32(0)
    for s in range(segs):
        end = end + lengths[s]
        ends[s] = end
    hot[...] = jnp.zeros_like(hot)
    width = hot.shape[1]
    lane = lax.broadcasted_iota(jnp.int32, (PAGE, width), 1)
    sub = lax.broadcasted_iota(jnp.int32, (PAGE, width), 0)

    def finish_of(a):
        def look(s, found):
            return jnp.where((found == 0) & (ends[s] > a), ends[s], found)

        return lax.fori_loop(0, segs, look, jnp.int32(0))

    def start_of(a):
        def look(s, found):
            return jnp.where(ends[s] <= a, ends[s], found)

        return lax.fori_loop(0, segs, look, jnp.int32(0))

    first = start_of(base)
    page = first + ((base - first) // PAGE) * PAGE

    def one_page(rank, a):
        stop = jnp.minimum(a + PAGE, finish_of(a))
        owned = (stop > base) & (stop <= base + shard_rows)

        @pl.when(owned)
        def _():
            shift = a - base
            token = sub + shift
            chunk = token // rows
            d = lax.rem(x - chunk + 2 * heads, heads)
            column = jnp.where(token < 0, token + PAGE, 128 + d * rows + token - chunk * rows)
            mark = (lane == column) & (sub < stop - a)
            slot = slots[0, rank]
            hot[pl.ds(pl.multiple_of(slot * PAGE, PAGE), PAGE), :] = mark.astype(hot.dtype)

        return jnp.where(owned, stop, a)

    lax.fori_loop(0, pool, one_page, page)
    mark = hot[...].astype(jnp.bfloat16)
    tail = jnp.concatenate(
        [tail_ref[...], jnp.zeros((128 - PAGE, tail_ref.shape[1]), jnp.bfloat16)], axis=0
    )
    source = jnp.concatenate([tail, own_ref[...], rest_ref[...]], axis=0)
    out_ref[...] = jnp.dot(mark, source, preferred_element_type=jnp.float32).astype(jnp.bfloat16)


def pages(lengths, slots, tail, own, rest, heads):
    rows, width = own.shape
    pool = slots.shape[1]
    return pl.pallas_call(
        functools.partial(pages_body, heads, lengths.shape[0], pool),
        out_shape=jax.ShapeDtypeStruct((pool * PAGE, width), jnp.bfloat16),
        in_specs=[SMEM, SMEM, VMEM, VMEM, VMEM],
        out_specs=VMEM,
        scratch_shapes=[
            pltpu.VMEM((pool * PAGE, 128 + heads * rows), jnp.float32),
            pltpu.SMEM((lengths.shape[0],), jnp.int32),
        ],
        compiler_params=params(),
        name="pages",
    )(lengths, slots, tail, own, rest)


def join(parts):
    return parts[0] if len(parts) == 1 else jnp.concatenate(parts, axis=0)


def on_device(queries, key_states, value_states, query_gain, key_gain, lengths, slot_order):
    heads = lax.axis_size("head")
    rows = queries.shape[0]
    core = lax.rem(lax.axis_index("tok"), 2)
    x = lax.axis_index("head")

    cosine, sine, own, *away = kv_prep(
        lengths, key_states, value_states, key_gain.reshape(1, D), heads
    )
    rest = join([around(part, "head", d) for d, part in enumerate(away, 1)])
    own4, own2 = around(own, "tok", 4), around(own, "tok", 2)
    q_own, *q_away = q_prep(queries, query_gain.reshape(1, D), cosine, sine, heads)
    q_rest = join([around(part, "head", d) for d, part in enumerate(q_away, 1)])
    rest4, rest2 = around(rest, "tok", 4), around(rest, "tok", 2)

    tail_at = lax.rem(x + 1, heads)
    rest_tail = lax.dynamic_slice_in_dim(
        rest, jnp.maximum(tail_at, 1) * rows - PAGE, PAGE, axis=0
    )
    tail = around(jnp.where(tail_at == 0, own[rows - PAGE :], rest_tail), "tok", 1)
    pool2d = pages(lengths, slot_order, tail, own, rest, heads)
    kvl = own.shape[1] // (2 * D)
    page_pool = pool2d.reshape(slot_order.shape[1], PAGE, kvl, 2 * D)

    own_s = core_swap(jnp.concatenate([jnp.where(core == 0, own, own4), own2], axis=0))
    rest_s = core_swap(jnp.concatenate([jnp.where(core == 0, rest, rest4), rest2], axis=0))

    others = range(1, heads)
    many = heads - 1
    early = [own, rest, own4, own2, own_s]
    pieces = [(0, 0, "own", 0)] + [(1, d - 1, "own", d) for d in others]
    pieces += [(2, 0, "far", 0), (3, 0, "near", 0), (4, 0, "mix_swap", 0), (4, 1, "near_swap", 0)]
    state = attend(lengths, [q_own, q_rest], early, tuple(pieces), None, False, heads)
    late = [rest4, rest2, rest_s]
    pieces = [(0, d - 1, "far", d) for d in others]
    pieces += [(1, d - 1, "near", d) for d in others]
    pieces += [(2, d - 1, "mix_swap", d) for d in others]
    pieces += [(2, many + d - 1, "near_swap", d) for d in others]
    attention = attend(lengths, [q_own, q_rest], late, tuple(pieces), state, True, heads)
    return (attention, page_pool)


def solution(mesh):
    in_specs = (
        P(("tok", "head"), None),
        P(("tok", "head"), None),
        P(("tok", "head"), None),
        P(),
        P(),
        P(),
        P("tok", None),
    )
    out_specs = (P("tok", "head"), P("tok", None, "head", None))
    return jax.shard_map(
        on_device, mesh=mesh, in_specs=in_specs, out_specs=out_specs, check_vma=False
    )
```

time: 145 us -> 64.3 us (0.44)
  the two profiles are of different devices: /device:TPU:5 before, /device:TPU:0 now
where the time goes in v1:
time: 64.3 us; the launch traced here: 63.9 us
  Pallas kernels  23.8 us (37%)
  waiting for transfers between devices  18.9 us (29%)
  starting transfers between devices  10.3 us (16%)
  local copies, waits for them, and re-layouts  8.45 us (13%)
  other arithmetic  1.81 us (3%)
  between operations  0.7 us (1%)
    ppermute x7, waiting for transfers between devices, around(): return lax.ppermute(x, axis, [(i, (i + by) % peers) for i in range(peers)])  18.9 us
    pallas_call x2, Pallas kernels, attend(): pl.pallas_call(functools.partial(attend_body, heads, lengths.shape[0], ro...  14.7 us
    ppermute x7, starting transfers between devices, around(): return lax.ppermute(x, axis, [(i, (i + by) % peers) for i in range(peers)])  10.3 us
    unnamed x24, local copies, waits for them, and re-layouts  6.99 us
    pallas_call x1, Pallas kernels, q_prep(): pl.pallas_call(functools.partial(q_prep_body, heads), out_shape=[part] *...  4.5 us
    pallas_call x1, Pallas kernels, pages(): pl.pallas_call(functools.partial(pages_body, heads, lengths.shape[0], poo...  3.13 us
    pallas_call x1, Pallas kernels, kv_prep(): pl.pallas_call(functools.partial(kv_prep_body, heads, lengths.shape[0]),...  1.47 us
    reshape x1, local copies, waits for them, and re-layouts, on_device(): page_pool = pool2d.reshape(slot_order.shape[1], PAGE, kvl, 2 * D)  1.45 us
  transfers between devices with their start and end apart: 9, of which 4 were waited for; matrix products, arithmetic and copies ran while one was open for 5% of the time, Pallas kernels for 23%

profile of v1, /device:TPU:0, one launch (start us, length us, event | category | flops | bytes accessed | tf_op | source)
XLA Modules:
  0.0 63.9 jit_solution(8396590227970725465)
XLA Ops:
  0.6 0.9 %copy-done.1 = bf16[128,1024]{1,0:T(8,128)(2,1)S(1)} copy-done((bf16[128,1024]{1,0:T(8,128)(2,1)S(1)}, bf16[128,1024]{1,0:T(8,128)(2,1)}, u32[]{:S(2)}) %copy-start.1) | copy-done | bytes 262168
  1.6 0.9 %copy-done.2 = bf16[128,1024]{1,0:T(8,128)(2,1)S(1)} copy-done((bf16[128,1024]{1,0:T(8,128)(2,1)S(1)}, bf16[128,1024]{1,0:T(8,128)(2,1)}, u32[]{:S(2)}) %copy-start.2) | copy-done | bytes 262168
  2.5 0.7 %copy-done.7 = s32[8]{0:T(128)S(1)} copy-done((s32[8]{0:T(128)S(1)}, s32[8]{0:T(128)}, u32[]{:S(2)}) %copy-start.7) | copy-done | bytes 56
  3.2 0.7 %copy-done.11 = f32[128]{0:T(128)S(1)} copy-done((f32[128]{0:T(128)S(1)}, f32[128]{0:T(128)}, u32[]{:S(2)}) %copy-start.11) | copy-done | bytes 536
  3.8 1.5 %kv_prep.1 = (f32[128,128]{1,0:T(8,128)S(1)}, f32[128,128]{1,0:T(8,128)S(1)}, bf16[128,1024]{1,0:T(8,128)(2,1)S(1)}, bf16[128,1024]{1,0:T(8,128)(2,1)S(1)}) custom-call(s32[8]{0:T(128)S(1)} %copy-done.7, bf16[128,1024]{1,0:T(8,128)(2,1)S(1)} %copy-done.1, bf16[128,1024]{1,0:T(8,128)(2,1)S(1)} %copy-done.2, f32[1,128]{1,0:T(1,128)S(1)} %bitcast.3), custom_call_target="tpu_custom_call" | custom-call | tf_op jit(solution)/shard_map/kv_prep/pallas_call | solution.py:100
  5.3 3.0 %collective-permute-start.1 = (bf16[128,1024]{1,0:T(8,128)(2,1)S(1)}, bf16[128,1024]{1,0:T(8,128)(2,1)S(1)}, u32[]{:S(2)}, u32[]{:S(2)}) collective-permute-start(bf16[128,1024]{1,0:T(8,128)(2,1)S(1)} %get-tuple-element.15), channel_id=1, source_target_pairs={{0,1},{1,0},{2,3},{3,2},{4,5},{5,4},{6,7},{7,6},{8,9},{9,8},{10,11... | collective-permute-start | bytes 786440 | tf_op jit(solution)/shard_map/ppermute | solution.py:21
  8.3 1.6 %collective-permute-start.5 = (bf16[128,1024]{1,0:T(8,128)(2,1)S(1)}, bf16[128,1024]{1,0:T(8,128)(2,1)S(1)}, u32[]{:S(2)}, u32[]{:S(2)}) collective-permute-start(bf16[128,1024]{1,0:T(8,128)(2,1)S(1)} %get-tuple-element.16.refs_2_.own_ref), channel_id=1, source_target_pairs={{0,8},{2,10},{4,12},{6,14},{8,16},{10,18},{12,20},{14,22},{16,24},... | collective-permute-start | bytes 786440 | tf_op jit(solution)/shard_map/ppermute | solution.py:21
  9.9 1.5 %collective-permute-start.6 = (bf16[128,1024]{1,0:T(8,128)(2,1)S(1)}, bf16[128,1024]{1,0:T(8,128)(2,1)S(1)}, u32[]{:S(2)}, u32[]{:S(2)}) collective-permute-start(bf16[128,1024]{1,0:T(8,128)(2,1)S(1)} %get-tuple-element.16.refs_2_.own_ref), channel_id=1, source_target_pairs={{0,4},{2,6},{4,8},{6,10},{8,12},{10,14},{12,16},{14,18},{16,20},{1... | collective-permute-start | bytes 786440 | tf_op jit(solution)/shard_map/ppermute | solution.py:21
  11.4 1.2 %copy-done = bf16[128,4096]{1,0:T(8,128)(2,1)S(1)} copy-done((bf16[128,4096]{1,0:T(8,128)(2,1)S(1)}, bf16[128,4096]{1,0:T(8,128)(2,1)}, u32[]{:S(2)}) %copy-start) | copy-done | bytes 1048600
  12.7 0.7 %copy-done.9 = f32[128]{0:T(128)S(1)} copy-done((f32[128]{0:T(128)S(1)}, f32[128]{0:T(128)}, u32[]{:S(2)}) %copy-start.9) | copy-done | bytes 536
  13.3 4.5 %q_prep.1 = (bf16[128,2048]{1,0:T(8,128)(2,1)S(1)}, bf16[128,2048]{1,0:T(8,128)(2,1)}) custom-call(bf16[128,4096]{1,0:T(8,128)(2,1)S(1)} %copy-done, f32[1,128]{1,0:T(1,128)S(1)} %bitcast.2, f32[128,128]{1,0:T(8,128)S(1)} %get-tuple-element.11.cos_ref, f32[128,128]{1,0:T(8,128)S(1)} %get-tuple-element.12.sin_ref), custom_call_target="tpu_custom_call" | custom-call | tf_op jit(solution)/shard_map/q_prep/pallas_call | solution.py:113
  17.8 0.5 collective-permute-start
  18.3 0.0 collective-permute-done.1.refs_3_.rest_ref
  18.4 1.6 %collective-permute-start.2 = (bf16[128,1024]{1,0:T(8,128)(2,1)S(1)}, bf16[128,1024]{1,0:T(8,128)(2,1)S(1)}, u32[]{:S(2)}, u32[]{:S(2)}) collective-permute-start(bf16[128,1024]{1,0:T(8,128)(2,1)S(1)} %collective-permute-done.1.refs_3_.rest_ref), channel_id=1, source_target_pairs={{0,8},{2,10},{4,12},{6,14},{8,16},{10,18},{12,20},{14,22},{16,24},... | collective-permute-start | bytes 786440 | tf_op jit(solution)/shard_map/ppermute | solution.py:21
  19.9 1.5 %collective-permute-start.3 = (bf16[128,1024]{1,0:T(8,128)(2,1)S(1)}, bf16[128,1024]{1,0:T(8,128)(2,1)S(1)}, u32[]{:S(2)}, u32[]{:S(2)}) collective-permute-start(bf16[128,1024]{1,0:T(8,128)(2,1)S(1)} %collective-permute-done.1.refs_3_.rest_ref), channel_id=1, source_target_pairs={{0,4},{2,6},{4,8},{6,10},{8,12},{10,14},{12,16},{14,18},{16,20},{1... | collective-permute-start | bytes 786440 | tf_op jit(solution)/shard_map/ppermute | solution.py:21
  21.5 4.4 %collective-permute-done.6.refs_5_ = bf16[128,1024]{1,0:T(8,128)(2,1)S(1)} collective-permute-done((bf16[128,1024]{1,0:T(8,128)(2,1)S(1)}, bf16[128,1024]{1,0:T(8,128)(2,1)S(1)}, u32[]{:S(2)}, u32[]{:S(2)}) %collective-permute-start.6) | collective-permute-done | bytes 262176 | tf_op jit(solution)/shard_map/ppermute | solution.py:21
  25.9 0.9 %pad_maximum_fusion.1 = bf16[256,1024]{1,0:T(8,128)(2,1)} fusion(bf16[128,1024]{1,0:T(8,128)(2,1)S(1)} %collective-permute-done.6.refs_5_, bf16[128,1024]{1,0:T(8,128)(2,1)S(1)} %broadcast_select_fusion), kind=kLoop, calls=%fused_computation.1 | loop fusion | flops 1048576 | bytes 1048576 | tf_op jit(solution)/shard_map/concatenate | solution.py:367
  26.8 0.2 collective-permute-done.2.refs_2_
  27.1 8.7 %collective-permute-done.3.refs_3_ = bf16[128,1024]{1,0:T(8,128)(2,1)S(1)} collective-permute-done((bf16[128,1024]{1,0:T(8,128)(2,1)S(1)}, bf16[128,1024]{1,0:T(8,128)(2,1)S(1)}, u32[]{:S(2)}, u32[]{:S(2)}) %collective-permute-start.3) | collective-permute-done | bytes 262176 | tf_op jit(solution)/shard_map/ppermute | solution.py:21
  35.8 0.8 %pad_maximum_fusion = bf16[256,1024]{1,0:T(8,128)(2,1)} fusion(bf16[128,1024]{1,0:T(8,128)(2,1)S(1)} %collective-permute-done.3.refs_3_, bf16[128,1024]{1,0:T(8,128)(2,1)S(1)} %broadcast_select_fusion.1), kind=kLoop, calls=%fused_computation | loop fusion | flops 1048576 | bytes 1048576 | tf_op jit(solution)/shard_map/concatenate | solution.py:368
  36.6 0.0 collective-permute-start.4
  36.6 0.6 collective-permute-start.8
  37.2 5.5 %collective-permute-done.8.tail_ref = bf16[16,1024]{1,0:T(8,128)(2,1)S(1)} collective-permute-done((bf16[16,1024]{1,0:T(8,128)(2,1)S(1)}, bf16[16,1024]{1,0:T(8,128)(2,1)S(1)}, u32[]{:S(2)}, u32[]{:S(2)}) %collective-permute-start.8) | collective-permute-done | bytes 32800 | tf_op jit(solution)/shard_map/ppermute | solution.py:21
  42.7 3.1 %pages.1 = bf16[384,1024]{1,0:T(8,128)(2,1)S(1)} custom-call(s32[8]{0:T(128)S(1)} %copy-done.8, s32[1,24]{1,0:T(1,128)S(1)} %copy-done.10, bf16[16,1024]{1,0:T(8,128)(2,1)S(1)} %collective-permute-done.8.tail_ref, bf16[128,1024]{1,0:T(8,128)(2,1)S(1)} %get-tuple-element.16.refs_2_.own_ref, bf16[128,1024]{1,0:T(8,128)(2,1)S(1)} %collective-permute-done.1.refs_3_.rest_ref), custom_call_target="tpu_custom_call" | custom-call | tf_op jit(solution)/shard_map/pages/pallas_call | solution.py:325
  45.8 1.5 %reshape.15 = bf16[24,16,4,256]{3,2,1,0:T(4,128)(2,1)} reshape(bf16[384,1024]{1,0:T(8,128)(2,1)S(1)} %pages.1) | data formatting | bytes 1572864 | tf_op jit(solution)/shard_map/reshape | solution.py:365
  47.3 0.0 collective-permute-done.refs_1_
  47.3 0.0 collective-permute-done.7.refs_6_
  47.3 0.9 %copy-done.4 = bf16[128,1024]{1,0:T(8,128)(2,1)S(1)} copy-done((bf16[128,1024]{1,0:T(8,128)(2,1)S(1)}, bf16[128,1024]{1,0:T(8,128)(2,1)}, u32[]{:S(2)}) %copy-start.4) | copy-done | bytes 262168
  48.3 0.9 %copy-done.6 = bf16[128,1024]{1,0:T(8,128)(2,1)S(1)} copy-done((bf16[128,1024]{1,0:T(8,128)(2,1)S(1)}, bf16[128,1024]{1,0:T(8,128)(2,1)}, u32[]{:S(2)}) %copy-start.6) | copy-done | bytes 262168
  49.2 7.3 %attend_part.1 = (f32[2,4,1,512]{3,2,1,0:T(1,128)S(1)}, f32[2,4,1,512]{3,2,1,0:T(1,128)S(1)}, f32[2,4,128,512]{3,2,1,0:T(8,128)S(1)}) custom-call(s32[8]{0:T(128)S(1)} %copy-done.8, bf16[128,2048]{1,0:T(8,128)(2,1)S(1)} %get-tuple-element.13.refs_0_, bf16[128,2048]{1,0:T(8,128)(2,1)S(1)} %collective-permute-done.refs_1_, ...), custom_call_target="tpu_custom_call" | custom-call | flops 1610612736 | bytes 4194304 | tf_op jit(solution)/shard_map/attend_part/pallas_call | solution.py:247
  56.5 0.0 collective-permute-done.4.refs_4_
  56.5 7.4 %attend_last.1 = bf16[256,2048]{1,0:T(8,128)(2,1)} custom-call(s32[8]{0:T(128)S(1)} %copy-done.8, bf16[128,2048]{1,0:T(8,128)(2,1)S(1)} %get-tuple-element.13.refs_0_, bf16[128,2048]{1,0:T(8,128)(2,1)S(1)} %collective-permute-done.refs_1_, bf16[128,1024]{1,0:T(8,128)(2,1)S(1)} %collective-permute-done.2.refs_2_, ...), custom_call_target="tpu_custom_call" | custom-call | flops 1073741824 | bytes 4194304 | tf_op jit(solution)/shard_map/attend_last/pallas_call | solution.py:247
  (21 shorter events, 0.1 us)
Async XLA Ops:
  0.6 1.0 %copy-start.1 = (bf16[128,1024]{1,0:T(8,128)(2,1)S(1)}, bf16[128,1024]{1,0:T(8,128)(2,1)}, u32[]{:S(2)}) copy-start(bf16[128,1024]{1,0:T(8,128)(2,1)} %k_ref.1) | copy-start | bytes 786436
  1.6 0.9 %copy-start.2 = (bf16[128,1024]{1,0:T(8,128)(2,1)S(1)}, bf16[128,1024]{1,0:T(8,128)(2,1)}, u32[]{:S(2)}) copy-start(bf16[128,1024]{1,0:T(8,128)(2,1)} %v_ref.1) | copy-start | bytes 786436
  2.5 0.7 %copy-start.7 = (s32[8]{0:T(128)S(1)}, s32[8]{0:T(128)}, u32[]{:S(2)}) copy-start(s32[8]{0:T(128)} %lengths.7) | copy-start | bytes 100
  3.2 0.7 %copy-start.11 = (f32[128]{0:T(128)S(1)}, f32[128]{0:T(128)}, u32[]{:S(2)}) copy-start(f32[128]{0:T(128)} %param.11) | copy-start | bytes 1540
  5.3 13.0 %collective-permute-start.1 = (bf16[128,1024]{1,0:T(8,128)(2,1)S(1)}, bf16[128,1024]{1,0:T(8,128)(2,1)S(1)}, u32[]{:S(2)}, u32[]{:S(2)}) collective-permute-start(bf16[128,1024]{1,0:T(8,128)(2,1)S(1)} %get-tuple-element.15), channel_id=1, source_target_pairs={{0,1},{1,0},{2,3},{3,2},{4,5},{5,4},{6,7},{7,6},{8,9},{9,8},{10,11... | collective-permute-start | bytes 786440 | tf_op jit(solution)/shard_map/ppermute | solution.py:21
  8.3 13.1 %collective-permute-start.5 = (bf16[128,1024]{1,0:T(8,128)(2,1)S(1)}, bf16[128,1024]{1,0:T(8,128)(2,1)S(1)}, u32[]{:S(2)}, u32[]{:S(2)}) collective-permute-start(bf16[128,1024]{1,0:T(8,128)(2,1)S(1)} %get-tuple-element.16.refs_2_.own_ref), channel_id=1, source_target_pairs={{0,8},{2,10},{4,12},{6,14},{8,16},{10,18},{12,20},{14,22},{16,24},... | collective-permute-start | bytes 786440 | tf_op jit(solution)/shard_map/ppermute | solution.py:21
  9.9 16.0 %collective-permute-start.6 = (bf16[128,1024]{1,0:T(8,128)(2,1)S(1)}, bf16[128,1024]{1,0:T(8,128)(2,1)S(1)}, u32[]{:S(2)}, u32[]{:S(2)}) collective-permute-start(bf16[128,1024]{1,0:T(8,128)(2,1)S(1)} %get-tuple-element.16.refs_2_.own_ref), channel_id=1, source_target_pairs={{0,4},{2,6},{4,8},{6,10},{8,12},{10,14},{12,16},{14,18},{16,20},{1... | collective-permute-start | bytes 786440 | tf_op jit(solution)/shard_map/ppermute | solution.py:21
  11.4 1.2 %copy-start = (bf16[128,4096]{1,0:T(8,128)(2,1)S(1)}, bf16[128,4096]{1,0:T(8,128)(2,1)}, u32[]{:S(2)}) copy-start(bf16[128,4096]{1,0:T(8,128)(2,1)} %q_ref.1) | copy-start | bytes 3145732
  12.6 0.7 %copy-start.9 = (f32[128]{0:T(128)S(1)}, f32[128]{0:T(128)}, u32[]{:S(2)}) copy-start(f32[128]{0:T(128)} %param.10) | copy-start | bytes 1540
  17.8 24.9 %copy-start.8 = (s32[8]{0:T(128)S(1)}, s32[8]{0:T(128)}, u32[]{:S(2)}) copy-start(s32[8]{0:T(128)} %lengths.7) | copy-start | bytes 100
  17.8 24.9 %copy-start.10 = (s32[1,24]{1,0:T(1,128)S(1)}, s32[1,24]{1,0:T(1,128)}, u32[]{:S(2)}) copy-start(s32[1,24]{1,0:T(1,128)} %slots.1) | copy-start | bytes 292
  17.8 29.5 %collective-permute-start = (bf16[128,2048]{1,0:T(8,128)(2,1)}, bf16[128,2048]{1,0:T(8,128)(2,1)S(1)}, u32[]{:S(2)}, u32[]{:S(2)}) collective-permute-start(bf16[128,2048]{1,0:T(8,128)(2,1)} %get-tuple-element.14), channel_id=1, source_target_pairs={{0,1},{1,0},{2,3},{3,2},{4,5},{5,4},{6,7},{7,6},{8,9},{9,8},{10,11... | collective-permute-start | bytes 1572872 | tf_op jit(solution)/shard_map/ppermute | solution.py:21
  18.4 8.7 %collective-permute-start.2 = (bf16[128,1024]{1,0:T(8,128)(2,1)S(1)}, bf16[128,1024]{1,0:T(8,128)(2,1)S(1)}, u32[]{:S(2)}, u32[]{:S(2)}) collective-permute-start(bf16[128,1024]{1,0:T(8,128)(2,1)S(1)} %collective-permute-done.1.refs_3_.rest_ref), channel_id=1, source_target_pairs={{0,8},{2,10},{4,12},{6,14},{8,16},{10,18},{12,20},{14,22},{16,24},... | collective-permute-start | bytes 786440 | tf_op jit(solution)/shard_map/ppermute | solution.py:21
  19.9 15.8 %collective-permute-start.3 = (bf16[128,1024]{1,0:T(8,128)(2,1)S(1)}, bf16[128,1024]{1,0:T(8,128)(2,1)S(1)}, u32[]{:S(2)}, u32[]{:S(2)}) collective-permute-start(bf16[128,1024]{1,0:T(8,128)(2,1)S(1)} %collective-permute-done.1.refs_3_.rest_ref), channel_id=1, source_target_pairs={{0,4},{2,6},{4,8},{6,10},{8,12},{10,14},{12,16},{14,18},{16,20},{1... | collective-permute-start | bytes 786440 | tf_op jit(solution)/shard_map/ppermute | solution.py:21
  21.5 15.7 %copy-start.3 = (bf16[128,1024]{1,0:T(8,128)(2,1)}, bf16[128,1024]{1,0:T(8,128)(2,1)S(1)}, u32[]{:S(2)}) copy-start(bf16[128,1024]{1,0:T(8,128)(2,1)S(1)} %collective-permute-done.5.refs_4_) | copy-start | bytes 786436
  25.9 11.3 %copy-start.5 = (bf16[128,1024]{1,0:T(8,128)(2,1)}, bf16[128,1024]{1,0:T(8,128)(2,1)S(1)}, u32[]{:S(2)}) copy-start(bf16[128,1024]{1,0:T(8,128)(2,1)S(1)} %collective-permute-done.6.refs_5_) | copy-start | bytes 786436
  26.8 20.5 %collective-permute-start.7 = (bf16[256,1024]{1,0:T(8,128)(2,1)}, bf16[256,1024]{1,0:T(8,128)(2,1)}, u32[]{:S(2)}, u32[]{:S(2)}) collective-permute-start(bf16[256,1024]{1,0:T(8,128)(2,1)} %pad_maximum_fusion.1), channel_id=1, source_target_pairs={{0,2},{2,0},{4,6},{6,4},{8,10},{10,8},{12,14},{14,12},{16,18},{18,... | collective-permute-start | bytes 1572872 | tf_op jit(solution)/shard_map/ppermute | solution.py:26
  36.6 19.9 %collective-permute-start.4 = (bf16[256,1024]{1,0:T(8,128)(2,1)}, bf16[256,1024]{1,0:T(8,128)(2,1)S(1)}, u32[]{:S(2)}, u32[]{:S(2)}) collective-permute-start(bf16[256,1024]{1,0:T(8,128)(2,1)} %pad_maximum_fusion), channel_id=1, source_target_pairs={{0,2},{2,0},{4,6},{6,4},{8,10},{10,8},{12,14},{14,12},{16,18},{18,... | collective-permute-start | bytes 1572872 | tf_op jit(solution)/shard_map/ppermute | solution.py:26
  36.6 6.1 %collective-permute-start.8 = (bf16[16,1024]{1,0:T(8,128)(2,1)S(1)}, bf16[16,1024]{1,0:T(8,128)(2,1)S(1)}, u32[]{:S(2)}, u32[]{:S(2)}) collective-permute-start(bf16[16,1024]{1,0:T(8,128)(2,1)S(1)} %dynamic-slice_select_fusion), channel_id=1, source_target_pairs={{0,2},{2,4},{4,6},{6,8},{8,10},{10,12},{12,14},{14,16},{16,18},{18... | collective-permute-start | bytes 98312 | tf_op jit(solution)/shard_map/ppermute | solution.py:21
  47.3 1.0 %copy-start.4 = (bf16[128,1024]{1,0:T(8,128)(2,1)S(1)}, bf16[128,1024]{1,0:T(8,128)(2,1)}, u32[]{:S(2)}) copy-start(bf16[128,1024]{1,0:T(8,128)(2,1)} %copy-done.3) | copy-start | bytes 786436
  48.3 0.9 %copy-start.6 = (bf16[128,1024]{1,0:T(8,128)(2,1)S(1)}, bf16[128,1024]{1,0:T(8,128)(2,1)}, u32[]{:S(2)}) copy-start(bf16[128,1024]{1,0:T(8,128)(2,1)} %copy-done.5) | copy-start | bytes 786436

commit v2 on v1

v2 whole, which is shorter than its diff:
```python
import functools
import math

import jax
import jax.numpy as jnp
from jax import lax
from jax.experimental import pallas as pl
from jax.experimental.pallas import tpu as pltpu
from jax.sharding import PartitionSpec as P

D = 128
PAGE = 16
HIDE = -2e30
FLOOR = -1e30
MIB = 1024 * 1024
SCALE = math.log2(math.e) / math.sqrt(D)

VMEM = pl.BlockSpec(memory_space=pltpu.VMEM)
SMEM = pl.BlockSpec(memory_space=pltpu.SMEM)
TOKEN = jax.ShapeDtypeStruct((8, D), jnp.float32)
ANY = pl.BlockSpec(memory_space=pl.ANY)
HBM = pl.BlockSpec(memory_space=pltpu.HBM)


def cost(us):
    return pl.CostEstimate(flops=int(us * 1.15e9), bytes_accessed=0, transcendentals=0)


def params(mib=32):
    return pltpu.CompilerParams(vmem_limit_bytes=mib * MIB)


def around(x, axis, by):
    peers = lax.axis_size(axis)
    return lax.ppermute(x, axis, [(i, (i + by) % peers) for i in range(peers)])


def swap(x, bit):
    peers = lax.axis_size("tok")
    return lax.ppermute(x, "tok", [(i, i ^ bit) for i in range(peers)])


def join(parts):
    return parts[0] if len(parts) == 1 else jnp.concatenate(parts, axis=0)


def at(index):
    return pl.ds(index, D) if isinstance(index, int) else pl.ds(pl.multiple_of(index, D), D)


def seg_first(pos, lengths, segs):
    first = jnp.zeros_like(pos)
    start = jnp.int32(0)
    for s in range(segs):
        first = jnp.where(pos >= start, start, first)
        start = start + lengths[s]
    return first


def seg_bounds(axis, lengths, segs):
    index = lax.broadcasted_iota(jnp.int32, (D, D), axis)
    begin = jnp.where(index == segs, -(2**30), 2**30)
    end = jnp.zeros((D, D), jnp.int32)
    here = jnp.int32(0)
    for s in range(segs):
        begin = jnp.where(index == s, here, begin)
        here = here + lengths[s]
        end = jnp.where(index == s, here, end)
    return begin, end


def rotate(x, cos_gain, sin_gain):
    power = jnp.mean(x * x, axis=0, keepdims=True)
    half = D // 2
    turned = jnp.concatenate([x[half:], x[:half]], axis=0)
    return (x * cos_gain + turned * sin_gain) * lax.rsqrt(power + 1e-06)


def gain_tables(cosine, sine, gain_row):
    gain = jnp.broadcast_to(gain_row, (D, D)).T
    half = D // 2
    turned = jnp.concatenate([gain[half:], gain[:half]], axis=0)
    cos_gain = jnp.concatenate([cosine, cosine], axis=0) * gain
    sin_gain = jnp.concatenate([-sine, sine], axis=0) * turned
    return cos_gain, sin_gain


def kv_prep_body(heads, segs, lengths_in, k_in, v_in, gain_in, cos_ref, sin_ref, *refs):
    outs, (lengths, k_ref, v_ref, gain_ref, sems) = refs[:heads], refs[heads:]
    pairs = [(lengths_in, lengths), (gain_in, gain_ref), (k_in, k_ref), (v_in, v_ref)]
    copies = [pltpu.make_async_copy(a, b, sems.at[i]) for i, (a, b) in enumerate(pairs)]
    for copy in copies:
        copy.start()
    rows = k_ref.shape[0]
    kvl = k_ref.shape[1] // D // heads
    x = lax.axis_index("head")
    base = (lax.axis_index("tok") * heads + x) * rows
    half = D // 2
    pos = base + lax.broadcasted_iota(jnp.int32, (half, rows), 1)
    step = lax.broadcasted_iota(jnp.int32, (half, rows), 0).astype(jnp.float32)
    frequency = jnp.exp(step * (-2.0 * math.log(1000000.0) / D))
    copies[0].wait()
    offset = (pos - seg_first(pos, lengths, segs)).astype(jnp.float32)
    angles = offset * frequency
    cosine, sine = jnp.cos(angles), jnp.sin(angles)
    cos_ref[...] = cosine
    sin_ref[...] = sine
    copies[1].wait()
    cos_gain, sin_gain = gain_tables(cosine, sine, gain_ref[...])
    copies[2].wait()
    copies[3].wait()
    for d in reversed(range(heads)):
        peer = lax.rem(x + d, heads)
        for j in range(kvl):
            head = peer * kvl + j
            key = k_ref[:, at(head * D)].astype(jnp.float32).T
            key = rotate(key, cos_gain, sin_gain).T
            outs[d][:, 2 * j * D : (2 * j + 1) * D] = key.astype(jnp.bfloat16)
            value = v_ref[:, at(head * D)]
            outs[d][:, (2 * j + 1) * D : (2 * j + 2) * D] = value.T


def kv_prep(lengths, keys, values, gain, heads):
    rows, width = keys.shape
    table = jax.ShapeDtypeStruct((D // 2, rows), jnp.float32)
    part = jax.ShapeDtypeStruct((rows, 2 * width // heads), jnp.bfloat16)
    return pl.pallas_call(
        functools.partial(kv_prep_body, heads, lengths.shape[0]),
        out_shape=[table, table] + [part] * heads,
        in_specs=[HBM] * 4,
        out_specs=[VMEM] * (2 + heads),
        scratch_shapes=[
            pltpu.SMEM(lengths.shape, jnp.int32),
            pltpu.VMEM(keys.shape, jnp.bfloat16),
            pltpu.VMEM(values.shape, jnp.bfloat16),
            pltpu.VMEM(gain.shape, jnp.float32),
            pltpu.SemaphoreType.DMA((4,)),
        ],
        compiler_params=params(62),
        cost_estimate=cost(0.01),
        name="kv_prep",
    )(lengths, keys, values, gain)


def q_prep_body(heads, q_in, gain_in, cos_in, sin_in, *refs):
    outs, (token, q_ref, gain_ref, cos_ref, sin_ref, sems) = refs[:heads], refs[heads:]
    token[...] = jnp.zeros_like(token)
    ql = q_ref.shape[1] // D // heads
    x = lax.axis_index("head")
    tables = [(gain_in, gain_ref), (cos_in, cos_ref), (sin_in, sin_ref)]
    tables = [
        pltpu.make_async_copy(a, b, sems.at[heads + i]) for i, (a, b) in enumerate(tables)
    ]
    for copy in tables:
        copy.start()
    copies = []
    for d in reversed(range(heads)):
        part = pl.ds(pl.multiple_of(lax.rem(x + d, heads) * ql * D, D), ql * D)
        copy = pltpu.make_async_copy(q_in.at[:, part], q_ref.at[:, part], sems.at[d])
        copy.start()
        copies.append(copy)
    for copy in tables:
        copy.wait()
    cos_gain, sin_gain = gain_tables(cos_ref[...], sin_ref[...], gain_ref[...])
    for d in reversed(range(heads)):
        copies[heads - 1 - d].wait()
        peer = lax.rem(x + d, heads)
        for j in range(ql):
            query = q_ref[:, at((peer * ql + j) * D)].astype(jnp.float32).T
            outs[d][j * D : (j + 1) * D, :] = rotate(query, cos_gain, sin_gain).astype(
                jnp.bfloat16
            )


def q_prep(queries, gain, cosine, sine, heads):
    rows, width = queries.shape
    part = jax.ShapeDtypeStruct((width // heads, rows), jnp.bfloat16)
    return pl.pallas_call(
        functools.partial(q_prep_body, heads),
        out_shape=[part] * heads + [TOKEN],
        in_specs=[HBM] * 4,
        out_specs=[VMEM] * (heads + 1),
        scratch_shapes=[
            pltpu.VMEM(queries.shape, jnp.bfloat16),
            pltpu.VMEM(gain.shape, jnp.float32),
            pltpu.VMEM(cosine.shape, jnp.float32),
            pltpu.VMEM(sine.shape, jnp.float32),
            pltpu.SemaphoreType.DMA((heads + 3,)),
        ],
        compiler_params=params(),
        cost_estimate=cost(0.01),
        name="q_prep",
    )(queries, gain, cosine, sine)


def shard_of(kind, tok):
    core = lax.rem(tok, 2)
    if kind == "own":
        return tok
    if kind == "far":
        return tok - 4
    if kind == "near":
        return tok - 2
    if kind == "near_swap":
        return tok - 1 - 2 * core
    return jnp.where(core == 0, tok - 3, tok - 1)


def attend_body(heads, segs, jobs, last, counts, lengths, *refs):
    n_q, n_kv, n_state, n_earlier = counts
    q_refs, refs = refs[:n_q], refs[n_q:]
    kv_refs, refs = refs[:n_kv], refs[n_kv:]
    states, refs = refs[: 3 * n_state], refs[3 * n_state :]
    earlier, refs = refs[:n_earlier], refs[n_earlier:]
    n_out = 2 if last else 3 * len(jobs)
    outs, (s_scr, p_scr, e_scr, f_scr, *page) = refs[:n_out], refs[n_out:]
    bufs = s_scr.shape[0]
    x = lax.axis_index("head")
    tok = lax.axis_index("tok")
    rows = D
    kvl = kv_refs[0].shape[1] // (2 * D)
    ql = f_scr.shape[2] // D * kvl
    group = ql // kvl
    wide = group * rows
    lane = lax.broadcasted_iota(jnp.int32, (rows, rows), 1)
    sub = lax.broadcasted_iota(jnp.int32, (rows, rows), 0)
    key_begin, key_end = seg_bounds(1, lengths, segs)
    query_begin, query_end = seg_bounds(0, lengths, segs)

    def key_block(pieces, g, side, axis):
        cols = at((2 * g + side) * D)
        return jnp.concatenate(
            [kv_refs[a][row * rows : (row + 1) * rows, cols] for a, row, _, _ in pieces],
            axis=axis,
        )

    def prepare(slot, job, c):
        _, first, _, _, pieces = jobs[job]
        d = first + c
        origin = lax.rem(x - d + heads, heads)
        q_chunk = tok * heads + origin
        q_pos = q_chunk * rows + lane
        outside = jnp.where((q_pos >= query_begin) & (q_pos < query_end), 0.0, HIDE)
        f_scr[slot] = jnp.concatenate([outside.astype(jnp.bfloat16)] * group, axis=1)
        for i, (a, row, kind, kd) in enumerate(pieces):
            k_chunk = shard_of(kind, tok) * heads + lax.rem(x - kd + heads, heads)
            k_pos = jnp.where(k_chunk <= q_chunk, k_chunk * rows + sub, -1)
            inside = (k_pos >= key_begin) & (k_pos < key_end)
            e_scr[slot, i * rows : (i + 1) * rows, :] = jnp.where(inside, 1.0, 0.0).astype(
                jnp.bfloat16
            )
        return origin

    def scores(buf, slot, job, c, g):
        q, first, _, s, pieces = jobs[job]
        d = first + c
        n = len(pieces)
        query = jnp.concatenate(
            [q_refs[q][at((c * ql + g * group + r) * D), :] for r in range(group)], axis=1
        )
        query = jnp.concatenate([query, f_scr[slot]], axis=0)
        keys = jnp.concatenate([key_block(pieces, g, 0, 0), e_scr[slot, : n * rows, :]], axis=1)
        score = jnp.dot(keys, query, preferred_element_type=jnp.float32)
        if s is None:
            top = jnp.full((8, wide), FLOOR, jnp.float32)
        else:
            top = jnp.broadcast_to(states[3 * s][c, g], (8, wide))
        for i, (a, row, kind, kd) in enumerate(pieces):
            block = score[i * rows : (i + 1) * rows]
            if kind == "own" and (not isinstance(d, int) or kd == d):
                late = jnp.where((sub > lane) & (kd == d), HIDE, 0.0)
                block = block + jnp.concatenate([late] * group, axis=1)
            s_scr[buf, i * rows : (i + 1) * rows, :] = block
            top = jnp.maximum(top, jnp.max(block.reshape(rows // 8, 8, wide), axis=0))
        return jnp.max(top, axis=0, keepdims=True)

    def weigh(buf, job, top):
        part = jnp.zeros((8, wide), jnp.float32)
        for i in range(len(jobs[job][4])):
            expo = jnp.exp2((s_scr[buf, i * rows : (i + 1) * rows, :] - top) * SCALE)
            part = part + jnp.sum(expo.reshape(rows // 8, 8, wide), axis=0)
            p_scr[buf, i * rows : (i + 1) * rows, :] = expo.astype(jnp.bfloat16)
        return jnp.sum(part, axis=0, keepdims=True)

    def mix(buf, job, c, g, origin, top, total):
        _, _, _, s, pieces = jobs[job]
        acc = jnp.dot(
            key_block(pieces, g, 1, 1),
            p_scr[buf, : len(pieces) * rows, :],
            preferred_element_type=jnp.float32,
        )
        if s is not None:
            fade = jnp.exp2((states[3 * s][c, g] - top) * SCALE)
            total = total + states[3 * s + 1][c, g] * fade
            acc = acc + states[3 * s + 2][c, g] * fade
        if last:
            acc = (acc * (1.0 / total)).astype(jnp.bfloat16)
            for r in range(group):
                outs[0][at(origin * rows), (g * group + r) * D : (g * group + r + 1) * D] = acc[
                    :, r * rows : (r + 1) * rows
                ].T
        else:
            outs[3 * job][c, g] = top
            outs[3 * job + 1][c, g] = total
            outs[3 * job + 2][c, g] = acc

    def sweep(chunks):
        origins = [prepare(slot, job, c) for slot, (job, c) in enumerate(chunks)]
        units = [(slot, g) for slot in range(len(chunks)) for g in range(kvl)]
        tops, totals = {}, {}
        for i in range(len(units) + 2):
            if i < len(units):
                slot, g = units[i]
                tops[i] = scores(i % bufs, slot, *chunks[slot], g)
            if 0 <= i - 1 < len(units):
                slot, g = units[i - 1]
                totals[i - 1] = weigh((i - 1) % bufs, chunks[slot][0], tops[i - 1])
            if 0 <= i - 2 < len(units):
                slot, g = units[i - 2]
                job, c = chunks[slot]
                mix((i - 2) % bufs, job, c, g, origins[slot], tops[i - 2], totals[i - 2])

    if last:
        slots, own_s, head_ref, _ = earlier
        first_page = (slots, own_s, kv_refs[0], head_ref, outs[1], *page)
        send = partial_page(heads, segs, lengths, *first_page)
    if max(job[2] for job in jobs) == 1:
        sweep([(job, 0) for job in range(len(jobs))])
    else:
        for job in range(len(jobs)):
            def body(c, carry, job=job):
                sweep([(job, c)])
                return carry

            lax.fori_loop(0, jobs[job][2], body, 0)
    if last:
        send()


def partial_page(heads, segs, lengths, slots, own_s, rest_s, head_ref, pool_ref, page, sem):
    x = lax.axis_index("head")
    tok = lax.axis_index("tok")
    core = lax.rem(tok, 2)
    base = tok * heads * D
    first = jnp.int32(0)
    end = jnp.int32(0)
    for s in range(segs):
        end = end + lengths[s]
        first = jnp.where(end <= base, end, first)
    before = lax.rem(base - first, PAGE)
    kvl = head_ref.shape[1]
    d = lax.rem(x + 1, heads)
    lane = lax.broadcasted_iota(jnp.int32, (PAGE, PAGE), 1)
    sub = lax.broadcasted_iota(jnp.int32, (PAGE, PAGE), 0)
    move = jnp.where((lane == sub + PAGE - before) & (sub < before), 1.0, 0.0).astype(jnp.bfloat16)
    copy = pltpu.make_async_copy(page, pool_ref.at[slots[0, 0]], sem)

    def write(ref, row):
        moved = []
        for g in range(kvl):
            at_row = pl.ds(pl.multiple_of(row + D - PAGE, PAGE), PAGE)
            key = ref[at_row, 2 * g * D : (2 * g + 1) * D]
            value = ref[at(row), (2 * g + 1) * D : (2 * g + 2) * D].T[D - PAGE :]
            both = jnp.concatenate([key, value], axis=1)
            moved.append(jnp.dot(move, both, preferred_element_type=jnp.float32))
        moved = jnp.stack(moved, axis=1)
        index = lax.broadcasted_iota(jnp.int32, moved.shape, 0)
        page[...] = jnp.where(index < before, moved, head_ref[...].astype(jnp.float32)).astype(
            jnp.bfloat16
        )
        copy.start()

    @pl.when((before > 0) & (d == 0))
    def _():
        write(own_s, (1 - core) * D)

    @pl.when((before > 0) & (d > 0))
    def _():
        write(rest_s, jnp.maximum(d - 1, 0) * D + (1 - core) * (heads - 1) * D)

    def finish():
        @pl.when(before > 0)
        def _():
            copy.wait()

    return finish


def attend(lengths, qs, kvs, jobs, last, heads, *earlier):
    kvl = kvs[0].shape[1] // (2 * D)
    states, plan = [], []
    for q, first, state, pieces in jobs:
        many = 1 if first == 0 else heads - 1
        plan.append((q, first, many, None if state is None else len(states), tuple(pieces)))
        if state is not None:
            states.append(state)
    ql = qs[plan[0][0]].shape[0] // D // plan[0][2]
    wide = ql // kvl * D
    if last:
        pool = earlier[3]
        out_shape = [jax.ShapeDtypeStruct((heads * D, ql * D), jnp.bfloat16)]
        out_shape += [jax.ShapeDtypeStruct(pool.shape, pool.dtype)]
    else:
        out_shape = []
        for _, _, many, _, _ in plan:
            row = jax.ShapeDtypeStruct((many, kvl, 1, wide), jnp.float32)
            out_shape += [row, row, jax.ShapeDtypeStruct((many, kvl, D, wide), jnp.float32)]
    inputs = [lengths, *qs, *kvs, *[part for state in states for part in state], *earlier]
    more = [SMEM, VMEM, VMEM, ANY] if last else [ANY] * len(earlier)
    keys = max(len(job[4]) for job in plan) * D
    together = len(plan) if heads == 2 else 1
    bufs = min(3, kvl * together)
    result = pl.pallas_call(
        functools.partial(
            attend_body, heads, lengths.shape[0], tuple(plan), last,
            (len(qs), len(kvs), len(states), len(earlier)),
        ),
        out_shape=out_shape,
        in_specs=[SMEM] + [VMEM] * (len(inputs) - 1 - len(earlier)) + more,
        out_specs=[VMEM, ANY] if last else [VMEM] * len(out_shape),
        input_output_aliases={len(inputs) - 1: 1} if last else {},
        scratch_shapes=[
            pltpu.VMEM((bufs, keys, wide), jnp.float32),
            pltpu.VMEM((bufs, keys, wide), jnp.bfloat16),
            pltpu.VMEM((together, keys, D), jnp.bfloat16),
            pltpu.VMEM((together, D, wide), jnp.bfloat16),
        ]
        + ([pltpu.VMEM(pool.shape[1:], pool.dtype), pltpu.SemaphoreType.DMA] if last else []),
        compiler_params=params(),
        cost_estimate=cost(0.01),
        name="attend_last" if last else "attend_part",
    )(*inputs)
    return result if last else [result[i : i + 3] for i in range(0, len(result), 3)]


def pages_body(heads, segs, pool, lengths, slots, own_ref, rest_ref, out_ref, head_ref, hot, ends):
    rows = D
    shard_rows = heads * rows
    x = lax.axis_index("head")
    base = lax.axis_index("tok") * shard_rows
    end = jnp.int32(0)
    for s in range(segs):
        end = end + lengths[s]
        ends[s] = end
    hot[...] = jnp.zeros_like(hot)
    width = hot.shape[1]
    lane = lax.broadcasted_iota(jnp.int32, (PAGE, width), 1)
    sub = lax.broadcasted_iota(jnp.int32, (PAGE, width), 0)

    def finish_of(a):
        found = jnp.int32(0)
        for s in reversed(range(segs)):
            found = jnp.where(ends[s] > a, ends[s], found)
        return found

    first = jnp.int32(0)
    for s in range(segs):
        first = jnp.where(ends[s] <= base, ends[s], first)
    page = first + ((base - first) // PAGE) * PAGE

    def one_page(rank, a):
        stop = jnp.minimum(a + PAGE, finish_of(a))
        owned = (stop > base) & (stop <= base + shard_rows)

        @pl.when(owned)
        def _():
            token = sub + (a - base)
            piece = token // rows
            d = lax.rem(x - piece + 2 * heads, heads)
            column = jnp.where(token < 0, -1, (d - piece) * rows + token)
            mark = (lane == column) & (sub < stop - a)
            slot = slots[0, rank]
            hot[pl.ds(pl.multiple_of(slot * PAGE, PAGE), PAGE), :] = mark.astype(hot.dtype)

        return jnp.where(owned, stop, a)

    lax.fori_loop(0, pool, one_page, page)
    mark = hot[...].astype(jnp.bfloat16)
    kvl = own_ref.shape[1] // (2 * D)
    moved = []
    for g in range(kvl):
        key_at, value_at = at(2 * g * D), at((2 * g + 1) * D)
        others = [rest_ref[i * D : (i + 1) * D, value_at].T for i in range(heads - 1)]
        key = jnp.concatenate([own_ref[:, key_at], rest_ref[:, key_at]], axis=0)
        value = jnp.concatenate([own_ref[:, value_at].T, *others], axis=0)
        both = jnp.concatenate([key, value], axis=1)
        moved.append(jnp.dot(mark, both, preferred_element_type=jnp.float32))
    out_ref[...] = jnp.stack(moved, axis=1).astype(jnp.bfloat16).reshape(out_ref.shape)
    head_ref[...] = out_ref[slots[0, 0]]


def pages(lengths, slots, own, rest, heads):
    pool = slots.shape[1]
    kvl = own.shape[1] // (2 * D)
    return pl.pallas_call(
        functools.partial(pages_body, heads, lengths.shape[0], pool),
        out_shape=[
            jax.ShapeDtypeStruct((pool, PAGE, kvl, 2 * D), jnp.bfloat16),
            jax.ShapeDtypeStruct((PAGE, kvl, 2 * D), jnp.bfloat16),
        ],
        in_specs=[SMEM, SMEM, VMEM, VMEM],
        out_specs=[VMEM, VMEM],
        scratch_shapes=[
            pltpu.VMEM((pool * PAGE, heads * D), jnp.float32),
            pltpu.SMEM((lengths.shape[0],), jnp.int32),
        ],
        compiler_params=params(),
        cost_estimate=cost(0.01),
        name="pages",
    )(lengths, slots, own, rest)


def pick_body(bit, plan, *refs):
    *ins, out = refs
    side = lax.rem(lax.axis_index("tok") // bit, 2)
    row = 0
    for part in plan:
        rows = ins[part[0]].shape[0]
        to = pl.ds(row, rows)
        if len(part) == 1:
            out[to, :] = ins[part[0]][...]
        else:
            for value, index in enumerate(part):
                @pl.when(side == value)
                def _(index=index, to=to):
                    out[to, :] = ins[index][...]
        row += rows


def pick(bit, plan, *arrays):
    rows = sum(arrays[part[0]].shape[0] for part in plan)
    last = max(max(part) for part in plan)
    return pl.pallas_call(
        functools.partial(pick_body, bit, plan),
        out_shape=jax.ShapeDtypeStruct((rows, arrays[0].shape[1]), jnp.bfloat16),
        in_specs=[ANY if i > last else VMEM for i in range(len(arrays))],
        out_specs=VMEM,
        compiler_params=params(8),
        cost_estimate=cost(0.01),
        name="pick",
    )(*arrays)


def after_body(*refs):
    del refs


def after(x, *earlier):
    return pl.pallas_call(
        after_body,
        out_shape=jax.ShapeDtypeStruct(x.shape, x.dtype),
        in_specs=[ANY] * (1 + len(earlier)),
        out_specs=ANY,
        input_output_aliases={0: 0},
        compiler_params=params(1),
        cost_estimate=cost(0.01),
        name="after",
    )(x, *earlier)


def on_device(queries, key_states, value_states, query_gain, key_gain, lengths, slot_order):
    heads = lax.axis_size("head")
    others = range(1, heads)

    cosine, sine, own, *away = kv_prep(
        lengths, key_states, value_states, key_gain.reshape(1, D), heads
    )
    rest = join([around(part, "head", d) for d, part in enumerate(away, 1)])
    own4 = around(own, "tok", 4)
    q_own, *q_away, turned = q_prep(queries, query_gain.reshape(1, D), cosine, sine, heads)
    q_rest = join([around(part, "head", d) for d, part in enumerate(q_away, 1)])
    qs = [q_own, q_rest]
    rest = after(rest, turned)
    rest4, rest2 = around(rest, "tok", 4), around(rest, "tok", 2)
    own4 = after(own4, rest)
    near = pick(2, ((0, 1),), own, own4)
    own2 = swap(near, 2)

    base = [(0, 0, "own", 0)] + [(1, d - 1, "own", d) for d in others]
    [own_state] = attend(
        lengths, [q_own], [own, rest], [(0, 0, None, base)], False, heads, near
    )
    page_pool, head_page = pages(lengths, slot_order, own, rest, heads)
    own_mixed = pick(1, ((0, 1), (2,)), own, own4, own2, own_state[0], head_page)
    own_s = swap(own_mixed, 1)

    qs = [q_own, q_rest]
    pieces = [(2, 0, "far", 0), (3, 0, "near", 0)]
    own_state, rest_state = attend(
        lengths, qs, [own, rest, own4, own2],
        [(0, 0, own_state, pieces), (1, 1, None, base + pieces)], False, heads, own_mixed,
    )

    rest_mixed = pick(1, ((0, 1), (2,)), rest, rest4, rest2, own_state[0])
    rest_s = swap(rest_mixed, 1)
    pieces = [(0, 0, "mix_swap", 0), (0, 1, "near_swap", 0)]
    pieces += [(1, d - 1, "far", d) for d in others]
    pieces += [(2, d - 1, "near", d) for d in others]
    own_state, rest_state = attend(
        lengths, qs, [own_s, rest4, rest2],
        [(0, 0, own_state, pieces), (1, 1, rest_state, pieces)], False, heads, rest_mixed,
    )
    pieces = [(0, d - 1, "mix_swap", d) for d in others]
    pieces += [(0, heads + d - 2, "near_swap", d) for d in others]
    attention, page_pool = attend(
        lengths, qs, [rest_s],
        [(0, 0, own_state, pieces), (1, 1, rest_state, pieces)], True, heads,
        slot_order, own_s, head_page, page_pool,
    )
    return (attention, page_pool)


def solution(mesh):
    in_specs = (
        P(("tok", "head"), None),
        P(("tok", "head"), None),
        P(("tok", "head"), None),
        P(),
        P(),
        P(),
        P("tok", None),
    )
    out_specs = (P("tok", "head"), P("tok", None, "head", None))
    return jax.shard_map(
        on_device, mesh=mesh, in_specs=in_specs, out_specs=out_specs, check_vma=False
    )
```

time: 64.3 us -> 40.4 us (0.63)
  the two profiles are of different devices: /device:TPU:0 before, /device:TPU:1 now
where the time goes in v2:
time: 40.4 us; the launch traced here: 40.1 us
  Pallas kernels  20.5 us (51%)
  starting transfers between devices  11.7 us (29%)
  waiting for transfers between devices  3.7 us (9%)
  local copies, waits for them, and re-layouts  3.41 us (8%)
  between operations  0.73 us (2%)
    pallas_call x4, Pallas kernels, attend(): pl.pallas_call(functools.partial(attend_body, heads, lengths.shape[0], tu...  13 us
    ppermute x3, starting transfers between devices, swap(): return lax.ppermute(x, 'tok', [(i, i ^ bit) for i in range(peers)])  7.74 us
    ppermute x5, starting transfers between devices, around(): return lax.ppermute(x, axis, [(i, (i + by) % peers) for i in range(peers)])  3.96 us
    ppermute x5, waiting for transfers between devices, around(): return lax.ppermute(x, axis, [(i, (i + by) % peers) for i in range(peers)])  3.69 us
    pallas_call x1, Pallas kernels, pages(): pl.pallas_call(functools.partial(pages_body, heads, lengths.shape[0], poo...  3.65 us
    unnamed x14, local copies, waits for them, and re-layouts  3.41 us
    pallas_call x1, Pallas kernels, kv_prep(): pl.pallas_call(functools.partial(kv_prep_body, heads, lengths.shape[0]),...  2.74 us
    pallas_call x1, Pallas kernels, q_prep(): pl.pallas_call(functools.partial(q_prep_body, heads), out_shape=[part] *...  1.1 us
  transfers between devices with their start and end apart: 8, of which 3 were waited for; matrix products, arithmetic and copies ran while one was open for 0% of the time, Pallas kernels for 35%

profile of v2, /device:TPU:1, one launch (start us, length us, event | category | flops | bytes accessed | tf_op | source)
XLA Modules:
  0.0 40.1 jit_solution(9405624233946301283)
XLA Ops:
  0.6 2.7 %kv_prep.1 = (f32[64,128]{1,0:T(8,128)}, f32[64,128]{1,0:T(8,128)}, bf16[128,1024]{1,0:T(8,128)(2,1)}, bf16[128,1024]{1,0:T(8,128)(2,1)}) custom-call(s32[8]{0:T(128)} %lengths.9, bf16[128,1024]{1,0:T(8,128)(2,1)} %k_in.1, bf16[128,1024]{1,0:T(8,128)(2,1)} %v_in.1, f32[1,128]{1,0:T(1,128)} %bitcast.3), custom_call_target="tpu_custom_call" | custom-call | flops 11500000 | tf_op jit(solution)/shard_map/kv_prep/pallas_call | solution.py:127
  3.4 2.1 %collective-permute-start.1 = (bf16[128,1024]{1,0:T(8,128)(2,1)}, bf16[128,1024]{1,0:T(8,128)(2,1)S(1)}, u32[]{:S(2)}, u32[]{:S(2)}) collective-permute-start(bf16[128,1024]{1,0:T(8,128)(2,1)} %get-tuple-element.30), channel_id=1, source_target_pairs={{0,1},{1,0},{2,3},{3,2},{4,5},{5,4},{6,7},{7,6},{8,9},{9,8},{10,11... | collective-permute-start | bytes 786440 | tf_op jit(solution)/shard_map/ppermute | solution.py:35
  5.5 1.3 %collective-permute-start.4 = (bf16[128,1024]{1,0:T(8,128)(2,1)}, bf16[128,1024]{1,0:T(8,128)(2,1)S(1)}, u32[]{:S(2)}, u32[]{:S(2)}) collective-permute-start(bf16[128,1024]{1,0:T(8,128)(2,1)} %get-tuple-element.32.refs_0_.refs_1_.own_ref.refs_2_), channel_id=1, source_target_pairs={{0,8},{2,10},{4,12},{6,14},{8,16},{10,18},{12,20},{14,22},{16,24},... | collective-permute-start | bytes 786440 | tf_op jit(solution)/shard_map/ppermute | solution.py:35
  6.8 0.0 copy-start.6
  6.8 0.7 %copy-done.6 = f32[128]{0:T(128)S(1)} copy-done((f32[128]{0:T(128)S(1)}, f32[128]{0:T(128)}, u32[]{:S(2)}) %copy-start.6) | copy-done | bytes 536
  7.4 1.2 %copy-done.1 = bf16[128,4096]{1,0:T(8,128)(2,1)S(1)} copy-done((bf16[128,4096]{1,0:T(8,128)(2,1)S(1)}, bf16[128,4096]{1,0:T(8,128)(2,1)}, u32[]{:S(2)}) %copy-start.1) | copy-done | bytes 1048600
  8.7 0.8 %copy-done.2 = f32[64,128]{1,0:T(8,128)S(1)} copy-done((f32[64,128]{1,0:T(8,128)S(1)}, f32[64,128]{1,0:T(8,128)}, u32[]{:S(2)}) %copy-start.2) | copy-done | bytes 32792
  9.4 0.8 %copy-done.3 = f32[64,128]{1,0:T(8,128)S(1)} copy-done((f32[64,128]{1,0:T(8,128)S(1)}, f32[64,128]{1,0:T(8,128)}, u32[]{:S(2)}) %copy-start.3) | copy-done | bytes 32792
  10.2 1.1 %q_prep.1 = (bf16[2048,128]{1,0:T(8,128)(2,1)S(1)}, bf16[2048,128]{1,0:T(8,128)(2,1)S(1)}, f32[8,128]{1,0:T(8,128)S(1)}) custom-call(bf16[128,4096]{1,0:T(8,128)(2,1)S(1)} %copy-done.1, f32[1,128]{1,0:T(1,128)S(1)} %bitcast.2, f32[64,128]{1,0:T(8,128)S(1)} %copy-done.2, f32[64,128]{1,0:T(8,128)S(1)} %copy-done.3), custom_call_target="tpu_custom_call" | custom-call | flops 11500000 | tf_op jit(solution)/shard_map/q_prep/pallas_call | solution.py:178
  11.3 0.3 collective-permute-start
  11.6 0.1 collective-permute-done.1.refs_0_
  11.7 2.7 %collective-permute-done.4.refs_0_ = bf16[128,1024]{1,0:T(8,128)(2,1)S(1)} collective-permute-done((bf16[128,1024]{1,0:T(8,128)(2,1)}, bf16[128,1024]{1,0:T(8,128)(2,1)S(1)}, u32[]{:S(2)}, u32[]{:S(2)}) %collective-permute-start.4) | collective-permute-done | bytes 262176 | tf_op jit(solution)/shard_map/ppermute | solution.py:35
  14.5 0.0 copy-done
  14.5 0.0 copy-start.4
  14.5 1.3 %collective-permute-start.5 = (bf16[128,1024]{1,0:T(8,128)(2,1)S(1)}, bf16[128,1024]{1,0:T(8,128)(2,1)S(1)}, u32[]{:S(2)}, u32[]{:S(2)}) collective-permute-start(bf16[128,1024]{1,0:T(8,128)(2,1)S(1)} %pick.3.refs_3_), channel_id=1, source_target_pairs={{0,4},{2,6},{4,0},{6,2},{8,12},{10,14},{12,8},{14,10},{16,20},{18,... | collective-permute-start | bytes 786440 | tf_op jit(solution)/shard_map/ppermute | solution.py:40
  15.8 0.0 collective-permute-start.2
  15.8 0.2 collective-permute-start.3
  16.1 0.0 copy-done.4
  16.1 1.6 %attend_part.3 = (f32[1,4,1,512]{3,2,1,0:T(1,128)S(1)}, f32[1,4,1,512]{3,2,1,0:T(1,128)S(1)}, f32[1,4,128,512]{3,2,1,0:T(8,128)S(1)}) custom-call(s32[8]{0:T(128)S(1)} %copy-done.4, bf16[2048,128]{1,0:T(8,128)(2,1)S(1)} %get-tuple-element.28.refs_0_, bf16[128,1024]{1,0:T(8,128)(2,1)S(1)} %copy-done, ...), custom_call_target="tpu_custom_call" | custom-call | flops 11500000 | tf_op jit(solution)/shard_map/attend_part/pallas_call | solution.py:413
  17.7 0.0 copy-done.5
  17.7 3.7 %pages.1 = (bf16[24,16,4,256]{3,2,1,0:T(4,128)(2,1)}, bf16[16,4,256]{2,1,0:T(4,128)(2,1)S(1)}) custom-call(s32[8]{0:T(128)S(1)} %copy-done.4, s32[1,24]{1,0:T(1,128)S(1)} %copy-done.5, bf16[128,1024]{1,0:T(8,128)(2,1)S(1)} %copy-done, bf16[128,1024]{1,0:T(8,128)(2,1)S(1)} %after.2.refs_1_.refs_2_.rest_ref.refs_3_.refs_0_), custom_call_target="tpu_custom_call" | custom-call | flops 11500000 | tf_op jit(solution)/shard_map/pages/pallas_call | solution.py:495
  21.4 0.0 collective-permute-done.5.refs_2_.refs_5_
  21.4 3.4 %collective-permute-start.7 = (bf16[256,1024]{1,0:T(8,128)(2,1)S(1)}, bf16[256,1024]{1,0:T(8,128)(2,1)S(1)}, u32[]{:S(2)}, u32[]{:S(2)}) collective-permute-start(bf16[256,1024]{1,0:T(8,128)(2,1)S(1)} %pick.4.refs_9_), channel_id=1, source_target_pairs={{0,2},{2,0},{4,6},{6,4},{8,10},{10,8},{12,14},{14,12},{16,18},{18,... | collective-permute-start | bytes 1572872 | tf_op jit(solution)/shard_map/ppermute | solution.py:40
  24.8 0.0 collective-permute-done.refs_1_
  24.8 3.3 %attend_part.4 = (f32[1,4,1,512]{3,2,1,0:T(1,128)S(1)}, f32[1,4,1,512]{3,2,1,0:T(1,128)S(1)}, f32[1,4,128,512]{3,2,1,0:T(8,128)S(1)}, f32[1,4,1,512]{3,2,1,0:T(1...) custom-call(s32[8]{0:T(128)S(1)} %copy-done.4, bf16[2048,128]{1,0:T(8,128)(2,1)S(1)} %get-tuple-element.28.refs_0_, ...), custom_call_target="tpu_custom_call" | custom-call | flops 11500000 | tf_op jit(solution)/shard_map/attend_part/pallas_call | solution.py:413
  28.1 0.0 collective-permute-done.2.refs_1_.refs_3_
  28.1 0.8 %collective-permute-done.3.refs_2_.refs_4_ = bf16[128,1024]{1,0:T(8,128)(2,1)S(1)} collective-permute-done((bf16[128,1024]{1,0:T(8,128)(2,1)S(1)}, bf16[128,1024]{1,0:T(8,128)(2,1)S(1)}, u32[]{:S(2)}, u32[]{:S(2)}) %collective-permute-start.3) | collective-permute-done | bytes 262176 | tf_op jit(solution)/shard_map/ppermute | solution.py:35
  28.9 3.1 %collective-permute-start.6 = (bf16[256,1024]{1,0:T(8,128)(2,1)S(1)}, bf16[256,1024]{1,0:T(8,128)(2,1)S(1)}, u32[]{:S(2)}, u32[]{:S(2)}) collective-permute-start(bf16[256,1024]{1,0:T(8,128)(2,1)S(1)} %pick.5.refs_11_), channel_id=1, source_target_pairs={{0,2},{2,0},{4,6},{6,4},{8,10},{10,8},{12,14},{14,12},{16,18},{18,... | collective-permute-start | bytes 1572872 | tf_op jit(solution)/shard_map/ppermute | solution.py:40
  32.0 0.0 collective-permute-done.7.refs_2_.refs_10_
  32.0 4.1 %attend_part.5 = (f32[1,4,1,512]{3,2,1,0:T(1,128)S(1)}, f32[1,4,1,512]{3,2,1,0:T(1,128)S(1)}, f32[1,4,128,512]{3,2,1,0:T(8,128)S(1)}, f32[1,4,1,512]{3,2,1,0:T(1...) custom-call(s32[8]{0:T(128)S(1)} %copy-done.4, bf16[2048,128]{1,0:T(8,128)(2,1)S(1)} %get-tuple-element.28.refs_0_, ...), custom_call_target="tpu_custom_call" | custom-call | flops 11500000 | tf_op jit(solution)/shard_map/attend_part/pallas_call | solution.py:413
  36.1 0.0 collective-permute-done.6.refs_2_
  36.1 4.0 %attend_last.1 = (bf16[256,2048]{1,0:T(8,128)(2,1)}, bf16[24,16,4,256]{3,2,1,0:T(4,128)(2,1)}) custom-call(s32[8]{0:T(128)S(1)} %copy-done.4, bf16[2048,128]{1,0:T(8,128)(2,1)S(1)} %get-tuple-element.28.refs_0_, bf16[2048,128]{1,0:T(8,128)(2,1)S(1)} %collective-permute-done.refs_1_, ...), custom_call_target="tpu_custom_call", output_to_operand_aliasing={{1}: (13, {})} | custom-call | flops 11500000 | tf_op jit(solution)/shard_map/attend_last/pallas_call | solution.py:413
  (10 shorter events, 0.1 us)
Async XLA Ops:
  3.4 8.3 %collective-permute-start.1 = (bf16[128,1024]{1,0:T(8,128)(2,1)}, bf16[128,1024]{1,0:T(8,128)(2,1)S(1)}, u32[]{:S(2)}, u32[]{:S(2)}) collective-permute-start(bf16[128,1024]{1,0:T(8,128)(2,1)} %get-tuple-element.30), channel_id=1, source_target_pairs={{0,1},{1,0},{2,3},{3,2},{4,5},{5,4},{6,7},{7,6},{8,9},{9,8},{10,11... | collective-permute-start | bytes 786440 | tf_op jit(solution)/shard_map/ppermute | solution.py:35
  5.5 9.0 %collective-permute-start.4 = (bf16[128,1024]{1,0:T(8,128)(2,1)}, bf16[128,1024]{1,0:T(8,128)(2,1)S(1)}, u32[]{:S(2)}, u32[]{:S(2)}) collective-permute-start(bf16[128,1024]{1,0:T(8,128)(2,1)} %get-tuple-element.32.refs_0_.refs_1_.own_ref.refs_2_), channel_id=1, source_target_pairs={{0,8},{2,10},{4,12},{6,14},{8,16},{10,18},{12,20},{14,22},{16,24},... | collective-permute-start | bytes 786440 | tf_op jit(solution)/shard_map/ppermute | solution.py:35
  6.8 0.7 %copy-start.6 = (f32[128]{0:T(128)S(1)}, f32[128]{0:T(128)}, u32[]{:S(2)}) copy-start(f32[128]{0:T(128)} %param.10) | copy-start | bytes 1540
  7.4 1.2 %copy-start.1 = (bf16[128,4096]{1,0:T(8,128)(2,1)S(1)}, bf16[128,4096]{1,0:T(8,128)(2,1)}, u32[]{:S(2)}) copy-start(bf16[128,4096]{1,0:T(8,128)(2,1)} %q_in.1) | copy-start | bytes 3145732
  8.7 0.8 %copy-start.2 = (f32[64,128]{1,0:T(8,128)S(1)}, f32[64,128]{1,0:T(8,128)}, u32[]{:S(2)}) copy-start(f32[64,128]{1,0:T(8,128)} %get-tuple-element.26.cos_in) | copy-start | bytes 98308
  9.4 0.8 %copy-start.3 = (f32[64,128]{1,0:T(8,128)S(1)}, f32[64,128]{1,0:T(8,128)}, u32[]{:S(2)}) copy-start(f32[64,128]{1,0:T(8,128)} %get-tuple-element.27.sin_in) | copy-start | bytes 98308
  11.3 13.5 %collective-permute-start = (bf16[2048,128]{1,0:T(8,128)(2,1)S(1)}, bf16[2048,128]{1,0:T(8,128)(2,1)S(1)}, u32[]{:S(2)}, u32[]{:S(2)}) collective-permute-start(bf16[2048,128]{1,0:T(8,128)(2,1)S(1)} %get-tuple-element.29), channel_id=1, source_target_pairs={{0,1},{1,0},{2,3},{3,2},{4,5},{5,4},{6,7},{7,6},{8,9},{9,8},{10,11... | collective-permute-start | bytes 1572872 | tf_op jit(solution)/shard_map/ppermute | solution.py:35
  11.7 2.8 %copy-start = (bf16[128,1024]{1,0:T(8,128)(2,1)S(1)}, bf16[128,1024]{1,0:T(8,128)(2,1)}, u32[]{:S(2)}) copy-start(bf16[128,1024]{1,0:T(8,128)(2,1)} %get-tuple-element.32.refs_0_.refs_1_.own_ref.refs_2_) | copy-start | bytes 786436
  14.5 1.5 %copy-start.4 = (s32[8]{0:T(128)S(1)}, s32[8]{0:T(128)}, u32[]{:S(2)}) copy-start(s32[8]{0:T(128)} %lengths.9) | copy-start | bytes 100
  14.5 6.8 %collective-permute-start.5 = (bf16[128,1024]{1,0:T(8,128)(2,1)S(1)}, bf16[128,1024]{1,0:T(8,128)(2,1)S(1)}, u32[]{:S(2)}, u32[]{:S(2)}) collective-permute-start(bf16[128,1024]{1,0:T(8,128)(2,1)S(1)} %pick.3.refs_3_), channel_id=1, source_target_pairs={{0,4},{2,6},{4,0},{6,2},{8,12},{10,14},{12,8},{14,10},{16,20},{18,... | collective-permute-start | bytes 786440 | tf_op jit(solution)/shard_map/ppermute | solution.py:40
  15.8 12.3 %collective-permute-start.2 = (bf16[128,1024]{1,0:T(8,128)(2,1)S(1)}, bf16[128,1024]{1,0:T(8,128)(2,1)S(1)}, u32[]{:S(2)}, u32[]{:S(2)}) collective-permute-start(bf16[128,1024]{1,0:T(8,128)(2,1)S(1)} %after.2.refs_1_.refs_2_.rest_ref.refs_3_.refs_0_), channel_id=1, source_target_pairs={{0,8},{2,10},{4,12},{6,14},{8,16},{10,18},{12,20},{14,22},{16,24},... | collective-permute-start | bytes 786440 | tf_op jit(solution)/shard_map/ppermute | solution.py:35
  15.8 13.1 %collective-permute-start.3 = (bf16[128,1024]{1,0:T(8,128)(2,1)S(1)}, bf16[128,1024]{1,0:T(8,128)(2,1)S(1)}, u32[]{:S(2)}, u32[]{:S(2)}) collective-permute-start(bf16[128,1024]{1,0:T(8,128)(2,1)S(1)} %after.2.refs_1_.refs_2_.rest_ref.refs_3_.refs_0_), channel_id=1, source_target_pairs={{0,4},{2,6},{4,8},{6,10},{8,12},{10,14},{12,16},{14,18},{16,20},{1... | collective-permute-start | bytes 786440 | tf_op jit(solution)/shard_map/ppermute | solution.py:35
  16.1 1.6 %copy-start.5 = (s32[1,24]{1,0:T(1,128)S(1)}, s32[1,24]{1,0:T(1,128)}, u32[]{:S(2)}) copy-start(s32[1,24]{1,0:T(1,128)} %refs_9_.1) | copy-start | bytes 292
  21.4 10.6 %collective-permute-start.7 = (bf16[256,1024]{1,0:T(8,128)(2,1)S(1)}, bf16[256,1024]{1,0:T(8,128)(2,1)S(1)}, u32[]{:S(2)}, u32[]{:S(2)}) collective-permute-start(bf16[256,1024]{1,0:T(8,128)(2,1)S(1)} %pick.4.refs_9_), channel_id=1, source_target_pairs={{0,2},{2,0},{4,6},{6,4},{8,10},{10,8},{12,14},{14,12},{16,18},{18,... | collective-permute-start | bytes 1572872 | tf_op jit(solution)/shard_map/ppermute | solution.py:40
  28.9 7.1 %collective-permute-start.6 = (bf16[256,1024]{1,0:T(8,128)(2,1)S(1)}, bf16[256,1024]{1,0:T(8,128)(2,1)S(1)}, u32[]{:S(2)}, u32[]{:S(2)}) collective-permute-start(bf16[256,1024]{1,0:T(8,128)(2,1)S(1)} %pick.5.refs_11_), channel_id=1, source_target_pairs={{0,2},{2,0},{4,6},{6,4},{8,10},{10,8},{12,14},{14,12},{16,18},{18,... | collective-permute-start | bytes 1572872 | tf_op jit(solution)/shard_map/ppermute | solution.py:40

commit v3 on v2

--- a/solution.py
+++ b/solution.py
@@ -33,6 +33,11 @@
 def around(x, axis, by):
     peers = lax.axis_size(axis)
     return lax.ppermute(x, axis, [(i, (i + by) % peers) for i in range(peers)])
+
+
+def onward(x, axis, by):
+    peers = lax.axis_size(axis)
+    return lax.ppermute(x, axis, [(i, i + by) for i in range(peers - by)])
 
 
 def swap(x, bit):
@@ -57,10 +62,10 @@
     return first
 
 
-def seg_bounds(axis, lengths, segs):
-    index = lax.broadcasted_iota(jnp.int32, (D, D), axis)
+def seg_bounds(shape, axis, lengths, segs):
+    index = lax.broadcasted_iota(jnp.int32, shape, axis)
     begin = jnp.where(index == segs, -(2**30), 2**30)
-    end = jnp.zeros((D, D), jnp.int32)
+    end = jnp.zeros(shape, jnp.int32)
     here = jnp.int32(0)
     for s in range(segs):
         begin = jnp.where(index == s, here, begin)
@@ -85,7 +90,7 @@
     return cos_gain, sin_gain
 
 
-def kv_prep_body(heads, segs, lengths_in, k_in, v_in, gain_in, cos_ref, sin_ref, *refs):
+def kv_prep_body(heads, segs, lengths_in, k_in, v_in, gain_in, table_ref, *refs):
     outs, (lengths, k_ref, v_ref, gain_ref, sems) = refs[:heads], refs[heads:]
     pairs = [(lengths_in, lengths), (gain_in, gain_ref), (k_in, k_ref), (v_in, v_ref)]
     copies = [pltpu.make_async_copy(a, b, sems.at[i]) for i, (a, b) in enumerate(pairs)]
@@ -103,8 +108,8 @@
     offset = (pos - seg_first(pos, lengths, segs)).astype(jnp.float32)
     angles = offset * frequency
     cosine, sine = jnp.cos(angles), jnp.sin(angles)
-    cos_ref[...] = cosine
-    sin_ref[...] = sine
+    table_ref[:half] = cosine
+    table_ref[half:] = sine
     copies[1].wait()
     cos_gain, sin_gain = gain_tables(cosine, sine, gain_ref[...])
     copies[2].wait()
@@ -122,13 +127,13 @@
 
 def kv_prep(lengths, keys, values, gain, heads):
     rows, width = keys.shape
-    table = jax.ShapeDtypeStruct((D // 2, rows), jnp.float32)
+    table = jax.ShapeDtypeStruct((D, rows), jnp.float32)
     part = jax.ShapeDtypeStruct((rows, 2 * width // heads), jnp.bfloat16)
     return pl.pallas_call(
         functools.partial(kv_prep_body, heads, lengths.shape[0]),
-        out_shape=[table, table] + [part] * heads,
+        out_shape=[table] + [part] * heads,
         in_specs=[HBM] * 4,
-        out_specs=[VMEM] * (2 + heads),
+        out_specs=[VMEM] * (1 + heads),
         scratch_shapes=[
             pltpu.SMEM(lengths.shape, jnp.int32),
             pltpu.VMEM(keys.shape, jnp.bfloat16),
@@ -142,28 +147,14 @@
     )(lengths, keys, values, gain)
 
 
-def q_prep_body(heads, q_in, gain_in, cos_in, sin_in, *refs):
-    outs, (token, q_ref, gain_ref, cos_ref, sin_ref, sems) = refs[:heads], refs[heads:]
+def q_prep_body(heads, q_ref, gain_ref, table_ref, *refs):
+    *outs, token = refs
     token[...] = jnp.zeros_like(token)
     ql = q_ref.shape[1] // D // heads
     x = lax.axis_index("head")
-    tables = [(gain_in, gain_ref), (cos_in, cos_ref), (sin_in, sin_ref)]
-    tables = [
-        pltpu.make_async_copy(a, b, sems.at[heads + i]) for i, (a, b) in enumerate(tables)
-    ]
-    for copy in tables:
-        copy.start()
-    copies = []
+    half = D // 2
+    cos_gain, sin_gain = gain_tables(table_ref[:half], table_ref[half:], gain_ref[...])
     for d in reversed(range(heads)):
-        part = pl.ds(pl.multiple_of(lax.rem(x + d, heads) * ql * D, D), ql * D)
-        copy = pltpu.make_async_copy(q_in.at[:, part], q_ref.at[:, part], sems.at[d])
-        copy.start()
-        copies.append(copy)
-    for copy in tables:
-        copy.wait()
-    cos_gain, sin_gain = gain_tables(cos_ref[...], sin_ref[...], gain_ref[...])
-    for d in reversed(range(heads)):
-        copies[heads - 1 - d].wait()
         peer = lax.rem(x + d, heads)
         for j in range(ql):
             query = q_ref[:, at((peer * ql + j) * D)].astype(jnp.float32).T
@@ -172,25 +163,18 @@
             )
 
 
-def q_prep(queries, gain, cosine, sine, heads):
+def q_prep(queries, gain, table, heads):
     rows, width = queries.shape
     part = jax.ShapeDtypeStruct((width // heads, rows), jnp.bfloat16)
     return pl.pallas_call(
         functools.partial(q_prep_body, heads),
         out_shape=[part] * heads + [TOKEN],
-        in_specs=[HBM] * 4,
+        in_specs=[VMEM] * 3,
         out_specs=[VMEM] * (heads + 1),
-        scratch_shapes=[
-            pltpu.VMEM(queries.shape, jnp.bfloat16),
-            pltpu.VMEM(gain.shape, jnp.float32),
-            pltpu.VMEM(cosine.shape, jnp.float32),
-            pltpu.VMEM(sine.shape, jnp.float32),
-            pltpu.SemaphoreType.DMA((heads + 3,)),
-        ],
         compiler_params=params(),
         cost_estimate=cost(0.01),
         name="q_prep",
-    )(queries, gain, cosine, sine)
+    )(queries, gain, table)
 
 
 def shard_of(kind, tok):
@@ -214,6 +198,8 @@
     earlier, refs = refs[:n_earlier], refs[n_earlier:]
     n_out = 2 if last else 3 * len(jobs)
     outs, (s_scr, p_scr, e_scr, f_scr, *page) = refs[:n_out], refs[n_out:]
+    if last:
+        out_scr, out_sems, *page = page
     bufs = s_scr.shape[0]
     x = lax.axis_index("head")
     tok = lax.axis_index("tok")
@@ -224,8 +210,9 @@
     wide = group * rows
     lane = lax.broadcasted_iota(jnp.int32, (rows, rows), 1)
     sub = lax.broadcasted_iota(jnp.int32, (rows, rows), 0)
-    key_begin, key_end = seg_bounds(1, lengths, segs)
-    query_begin, query_end = seg_bounds(0, lengths, segs)
+    key_begin, key_end = seg_bounds((1, D), 1, lengths, segs)
+    used = (segs + 16) // 16 * 16
+    query_begin, query_end = seg_bounds((used, D), 0, lengths, segs)
 
     def key_block(pieces, g, side, axis):
         cols = at((2 * g + side) * D)
@@ -234,15 +221,28 @@
             axis=axis,
         )
 
-    def prepare(slot, job, c):
+    def out_part(origin, g):
+        part = at(origin * rows), pl.ds(g * group * D, group * D)
+        sem = out_sems.at[origin, g]
+        return pltpu.make_async_copy(out_scr.at[part], outs[0].at[part], sem)
+
+    def prepare(slot, job, c, known):
         _, first, _, _, pieces = jobs[job]
         d = first + c
         origin = lax.rem(x - d + heads, heads)
         q_chunk = tok * heads + origin
-        q_pos = q_chunk * rows + lane
+        q_pos = q_chunk * rows + lane[:used]
         outside = jnp.where((q_pos >= query_begin) & (q_pos < query_end), 0.0, HIDE)
+        outside = jnp.concatenate([outside, jnp.zeros((D - used, D), jnp.float32)], axis=0)
         f_scr[slot] = jnp.concatenate([outside.astype(jnp.bfloat16)] * group, axis=1)
         for i, (a, row, kind, kd) in enumerate(pieces):
+            if kind != "own" and (a, row, kind, kd) in known:
+                from_slot, j = known[a, row, kind, kd]
+                e_scr[slot, i * rows : (i + 1) * rows, :] = e_scr[
+                    from_slot, j * rows : (j + 1) * rows, :
+                ]
+                continue
+            known[a, row, kind, kd] = (slot, i)
             k_chunk = shard_of(kind, tok) * heads + lax.rem(x - kd + heads, heads)
             k_pos = jnp.where(k_chunk <= q_chunk, k_chunk * rows + sub, -1)
             inside = (k_pos >= key_begin) & (k_pos < key_end)
@@ -296,16 +296,19 @@
         if last:
             acc = (acc * (1.0 / total)).astype(jnp.bfloat16)
             for r in range(group):
-                outs[0][at(origin * rows), (g * group + r) * D : (g * group + r + 1) * D] = acc[
+                out_scr[at(origin * rows), (g * group + r) * D : (g * group + r + 1) * D] = acc[
                     :, r * rows : (r + 1) * rows
                 ].T
+            part = out_part(origin, g)
+            part.start()
         else:
             outs[3 * job][c, g] = top
             outs[3 * job + 1][c, g] = total
             outs[3 * job + 2][c, g] = acc
 
     def sweep(chunks):
-        origins = [prepare(slot, job, c) for slot, (job, c) in enumerate(chunks)]
+        known = {}
+        origins = [prepare(slot, job, c, known) for slot, (job, c) in enumerate(chunks)]
         units = [(slot, g) for slot in range(len(chunks)) for g in range(kvl)]
         tops, totals = {}, {}
         for i in range(len(units) + 2):
@@ -334,6 +337,9 @@
 
             lax.fori_loop(0, jobs[job][2], body, 0)
     if last:
+        for origin in range(heads):
+            for g in range(kvl):
+                out_part(origin, g).wait()
         send()
 
 
@@ -417,7 +423,7 @@
         ),
         out_shape=out_shape,
         in_specs=[SMEM] + [VMEM] * (len(inputs) - 1 - len(earlier)) + more,
-        out_specs=[VMEM, ANY] if last else [VMEM] * len(out_shape),
+        out_specs=[ANY, ANY] if last else [VMEM] * len(out_shape),
         input_output_aliases={len(inputs) - 1: 1} if last else {},
         scratch_shapes=[
             pltpu.VMEM((bufs, keys, wide), jnp.float32),
@@ -425,7 +431,16 @@
             pltpu.VMEM((together, keys, D), jnp.bfloat16),
             pltpu.VMEM((together, D, wide), jnp.bfloat16),
         ]
-        + ([pltpu.VMEM(pool.shape[1:], pool.dtype), pltpu.SemaphoreType.DMA] if last else []),
+        + (
+            [
+                pltpu.VMEM(out_shape[0].shape, jnp.bfloat16),
+                pltpu.SemaphoreType.DMA((heads, kvl)),
+                pltpu.VMEM(pool.shape[1:], pool.dtype),
+                pltpu.SemaphoreType.DMA,
+            ]
+            if last
+            else []
+        ),
         compiler_params=params(),
         cost_estimate=cost(0.01),
         name="attend_last" if last else "attend_part",
@@ -433,7 +448,10 @@
     return result if last else [result[i : i + 3] for i in range(0, len(result), 3)]
 
 
-def pages_body(heads, segs, pool, lengths, slots, own_ref, rest_ref, out_ref, head_ref, hot, ends):
+def pages_body(
+    heads, segs, pool, lengths, slots, own_ref, rest_ref, pool_ref, head_ref, hot, ends,
+    wide_scr, out_scr, sems,
+):
     rows = D
     shard_rows = heads * rows
     x = lax.axis_index("head")
@@ -475,18 +493,29 @@
         return jnp.where(owned, stop, a)
 
     lax.fori_loop(0, pool, one_page, page)
-    mark = hot[...].astype(jnp.bfloat16)
     kvl = own_ref.shape[1] // (2 * D)
-    moved = []
+    both = []
     for g in range(kvl):
         key_at, value_at = at(2 * g * D), at((2 * g + 1) * D)
         others = [rest_ref[i * D : (i + 1) * D, value_at].T for i in range(heads - 1)]
         key = jnp.concatenate([own_ref[:, key_at], rest_ref[:, key_at]], axis=0)
         value = jnp.concatenate([own_ref[:, value_at].T, *others], axis=0)
-        both = jnp.concatenate([key, value], axis=1)
-        moved.append(jnp.dot(mark, both, preferred_element_type=jnp.float32))
-    out_ref[...] = jnp.stack(moved, axis=1).astype(jnp.bfloat16).reshape(out_ref.shape)
-    head_ref[...] = out_ref[slots[0, 0]]
+        both.append(jnp.concatenate([key, value], axis=1))
+    step = 8
+    copies = []
+    for i, page in enumerate(range(0, pool, step)):
+        mark = hot[page * PAGE : (page + step) * PAGE, :].astype(jnp.bfloat16)
+        for g in range(kvl):
+            wide_scr[i % 2, :, g, :] = jnp.dot(mark, both[g], preferred_element_type=jnp.float32)
+        block = pl.ds(page, step)
+        out_scr[block] = (
+            wide_scr[i % 2].astype(jnp.bfloat16).reshape(step, PAGE, kvl, 2 * D)
+        )
+        copies.append(pltpu.make_async_copy(out_scr.at[block], pool_ref.at[block], sems.at[i]))
+        copies[-1].start()
+    head_ref[...] = out_scr[slots[0, 0]]
+    for copy in copies:
+        copy.wait()
 
 
 def pages(lengths, slots, own, rest, heads):
@@ -499,10 +528,13 @@
             jax.ShapeDtypeStruct((PAGE, kvl, 2 * D), jnp.bfloat16),
         ],
         in_specs=[SMEM, SMEM, VMEM, VMEM],
-        out_specs=[VMEM, VMEM],
+        out_specs=[ANY, VMEM],
         scratch_shapes=[
             pltpu.VMEM((pool * PAGE, heads * D), jnp.float32),
             pltpu.SMEM((lengths.shape[0],), jnp.int32),
+            pltpu.VMEM((2, 8 * PAGE, kvl, 2 * D), jnp.float32),
+            pltpu.VMEM((pool, PAGE, kvl, 2 * D), jnp.bfloat16),
+            pltpu.SemaphoreType.DMA((pool // 8,)),
         ],
         compiler_params=params(),
         cost_estimate=cost(0.01),
@@ -562,42 +594,38 @@
     heads = lax.axis_size("head")
     others = range(1, heads)
 
-    cosine, sine, own, *away = kv_prep(
+    table, own, *away = kv_prep(
         lengths, key_states, value_states, key_gain.reshape(1, D), heads
     )
     rest = join([around(part, "head", d) for d, part in enumerate(away, 1)])
     own4 = around(own, "tok", 4)
-    q_own, *q_away, turned = q_prep(queries, query_gain.reshape(1, D), cosine, sine, heads)
+    q_own, *q_away, turned = q_prep(queries, query_gain.reshape(1, D), table, heads)
     q_rest = join([around(part, "head", d) for d, part in enumerate(q_away, 1)])
+    rest = after(rest, turned)
+    rest4, rest2 = around(rest, "tok", 4), onward(rest, "tok", 2)
+    base = [(0, 0, "own", 0)] + [(1, d - 1, "own", d) for d in others]
+    [own_state] = attend(lengths, [q_own], [own, rest], [(0, 0, None, base)], False, heads)
+
+    own4 = after(own4, own_state[0])
+    own2 = swap(pick(2, ((0, 1),), own, own4), 2)
+    page_pool, head_page = pages(lengths, slot_order, own, rest, heads)
+    own_mixed = pick(1, ((0, 1), (2,)), own, own4, own2, head_page)
+    own_s = swap(own_mixed, 1)
+
     qs = [q_own, q_rest]
-    rest = after(rest, turned)
-    rest4, rest2 = around(rest, "tok", 4), around(rest, "tok", 2)
-    own4 = after(own4, rest)
-    near = pick(2, ((0, 1),), own, own4)
-    own2 = swap(near, 2)
-
-    base = [(0, 0, "own", 0)] + [(1, d - 1, "own", d) for d in others]
-    [own_state] = attend(
-        lengths, [q_own], [own, rest], [(0, 0, None, base)], False, heads, near
-    )
-    page_pool, head_page = pages(lengths, slot_order, own, rest, heads)
-    own_mixed = pick(1, ((0, 1), (2,)), own, own4, own2, own_state[0], head_page)
-    own_s = swap(own_mixed, 1)
-
-    qs = [q_own, q_rest]
-    pieces = [(2, 0, "far", 0), (3, 0, "near", 0)]
+    near = [(2, 0, "far", 0), (3, 0, "near", 0)]
     own_state, rest_state = attend(
         lengths, qs, [own, rest, own4, own2],
-        [(0, 0, own_state, pieces), (1, 1, None, base + pieces)], False, heads, own_mixed,
+        [(0, 0, own_state, near), (1, 1, None, base + near)], False, heads,
+        own_mixed,
     )
 
     rest_mixed = pick(1, ((0, 1), (2,)), rest, rest4, rest2, own_state[0])
     rest_s = swap(rest_mixed, 1)
-    pieces = [(0, 0, "mix_swap", 0), (0, 1, "near_swap", 0)]
-    pieces += [(1, d - 1, "far", d) for d in others]
-    pieces += [(2, d - 1, "near", d) for d in others]
+    pieces = [(2, 0, "mix_swap", 0), (2, 1, "near_swap", 0)]
+    pieces += [(0, d - 1, "far", d) for d in others] + [(1, d - 1, "near", d) for d in others]
     own_state, rest_state = attend(
-        lengths, qs, [own_s, rest4, rest2],
+        lengths, qs, [rest4, rest2, own_s],
         [(0, 0, own_state, pieces), (1, 1, rest_state, pieces)], False, heads, rest_mixed,
     )
     pieces = [(0, d - 1, "mix_swap", d) for d in others]

time: 40.4 us -> 37.6 us (0.931)
  the two profiles are of different devices: /device:TPU:1 before, /device:TPU:15 now
where the time goes in v3:
time: 37.6 us; the launch traced here: 37.3 us
  Pallas kernels  19.4 us (52%)
  starting transfers between devices  12.3 us (33%)
  local copies, waits for them, and re-layouts  3.67 us (10%)
  waiting for transfers between devices  1.07 us (3%)
  between operations  0.78 us (2%)
    pallas_call x4, Pallas kernels, attend(): pl.pallas_call(functools.partial(attend_body, heads, lengths.shape[0], tu...  12.6 us
    ppermute x4, starting transfers between devices, around(): return lax.ppermute(x, axis, [(i, (i + by) % peers) for i in range(peers)])  4.2 us
    ppermute x1, starting transfers between devices, onward(): return lax.ppermute(x, axis, [(i, i + by) for i in range(peers - by)])  4.15 us
    ppermute x3, starting transfers between devices, swap(): return lax.ppermute(x, 'tok', [(i, i ^ bit) for i in range(peers)])  3.98 us
    unnamed x12, local copies, waits for them, and re-layouts  3.67 us
    pallas_call x1, Pallas kernels, pages(): pl.pallas_call(functools.partial(pages_body, heads, lengths.shape[0], poo...  3.1 us
    pallas_call x1, Pallas kernels, kv_prep(): pl.pallas_call(functools.partial(kv_prep_body, heads, lengths.shape[0]),...  2.82 us
    ppermute x4, waiting for transfers between devices, around(): return lax.ppermute(x, axis, [(i, (i + by) % peers) for i in range(peers)])  1.06 us
  transfers between devices with their start and end apart: 8, of which 1 were waited for; matrix products, arithmetic and copies ran while one was open for 0% of the time, Pallas kernels for 35%

profile of v3, /device:TPU:15, one launch (start us, length us, event | category | flops | bytes accessed | tf_op | source)
XLA Modules:
  0.0 37.3 jit_solution(15410725791425880171)
XLA Ops:
  0.6 2.8 %kv_prep.1 = (f32[128,128]{1,0:T(8,128)}, bf16[128,1024]{1,0:T(8,128)(2,1)}, bf16[128,1024]{1,0:T(8,128)(2,1)}) custom-call(s32[8]{0:T(128)} %lengths.9, bf16[128,1024]{1,0:T(8,128)(2,1)} %k_in.1, bf16[128,1024]{1,0:T(8,128)(2,1)} %v_in.1, f32[1,128]{1,0:T(1,128)} %bitcast.3), custom_call_target="tpu_custom_call" | custom-call | flops 11500000 | tf_op jit(solution)/shard_map/kv_prep/pallas_call | solution.py:132
  3.5 0.3 collective-permute-start.1
  3.8 1.3 %collective-permute-start.4 = (bf16[128,1024]{1,0:T(8,128)(2,1)}, bf16[128,1024]{1,0:T(8,128)(2,1)S(1)}, u32[]{:S(2)}, u32[]{:S(2)}) collective-permute-start(bf16[128,1024]{1,0:T(8,128)(2,1)} %get-tuple-element.30.refs_1_.refs_0_.own_ref.refs_2_), channel_id=1, source_target_pairs={{0,8},{2,10},{4,12},{6,14},{8,16},{10,18},{12,20},{14,22},{16,24},... | collective-permute-start | bytes 786440 | tf_op jit(solution)/shard_map/ppermute | solution.py:35
  5.1 0.7 %copy-done.5 = f32[128]{0:T(128)S(1)} copy-done((f32[128]{0:T(128)S(1)}, f32[128]{0:T(128)}, u32[]{:S(2)}) %copy-start.5) | copy-done | bytes 536
  5.7 1.2 %copy-done.1 = bf16[128,4096]{1,0:T(8,128)(2,1)S(1)} copy-done((bf16[128,4096]{1,0:T(8,128)(2,1)S(1)}, bf16[128,4096]{1,0:T(8,128)(2,1)}, u32[]{:S(2)}) %copy-start.1) | copy-done | bytes 1048600
  7.0 0.8 %copy-done.2 = f32[128,128]{1,0:T(8,128)S(1)} copy-done((f32[128,128]{1,0:T(8,128)S(1)}, f32[128,128]{1,0:T(8,128)}, u32[]{:S(2)}) %copy-start.2) | copy-done | bytes 65560
  7.8 0.8 %q_prep.1 = (bf16[2048,128]{1,0:T(8,128)(2,1)S(1)}, bf16[2048,128]{1,0:T(8,128)(2,1)S(1)}, f32[8,128]{1,0:T(8,128)S(1)}) custom-call(bf16[128,4096]{1,0:T(8,128)(2,1)S(1)} %copy-done.1, f32[1,128]{1,0:T(1,128)S(1)} %bitcast.2, f32[128,128]{1,0:T(8,128)S(1)} %copy-done.2), custom_call_target="tpu_custom_call" | custom-call | flops 11500000 | tf_op jit(solution)/shard_map/q_prep/pallas_call | solution.py:169
  8.6 1.3 %collective-permute-start = (bf16[2048,128]{1,0:T(8,128)(2,1)S(1)}, bf16[2048,128]{1,0:T(8,128)(2,1)S(1)}, u32[]{:S(2)}, u32[]{:S(2)}) collective-permute-start(bf16[2048,128]{1,0:T(8,128)(2,1)S(1)} %get-tuple-element.27), channel_id=1, source_target_pairs={{0,1},{1,0},{2,3},{3,2},{4,5},{5,4},{6,7},{7,6},{8,9},{9,8},{10,11... | collective-permute-start | bytes 1572872 | tf_op jit(solution)/shard_map/ppermute | solution.py:35
  9.9 1.0 %collective-permute-done.1.refs_0_ = bf16[128,1024]{1,0:T(8,128)(2,1)S(1)} collective-permute-done((bf16[128,1024]{1,0:T(8,128)(2,1)}, bf16[128,1024]{1,0:T(8,128)(2,1)S(1)}, u32[]{:S(2)}, u32[]{:S(2)}) %collective-permute-start.1) | collective-permute-done | bytes 262176 | tf_op jit(solution)/shard_map/ppermute | solution.py:35
  10.9 0.9 %copy-done = bf16[128,1024]{1,0:T(8,128)(2,1)S(1)} copy-done((bf16[128,1024]{1,0:T(8,128)(2,1)S(1)}, bf16[128,1024]{1,0:T(8,128)(2,1)}, u32[]{:S(2)}) %copy-start) | copy-done | bytes 262168
  11.9 0.0 copy-done.3
  11.9 1.6 %attend_part.3 = (f32[1,4,1,512]{3,2,1,0:T(1,128)S(1)}, f32[1,4,1,512]{3,2,1,0:T(1,128)S(1)}, f32[1,4,128,512]{3,2,1,0:T(8,128)S(1)}) custom-call(s32[8]{0:T(128)S(1)} %copy-done.3, bf16[2048,128]{1,0:T(8,128)(2,1)S(1)} %get-tuple-element.26.refs_0_, bf16[128,1024]{1,0:T(8,128)(2,1)S(1)} %copy-done, bf16[128,1024]{1,0:T(8,128)(2,1)S(1)} %after.2.refs_2_.rest_ref.refs_3_.refs_0_), custom_call_target="tpu_custom_call" | custom-call | flops 11500000 | tf_op jit(solution)/shard_map/attend_part/pallas_call | solution.py:419
  13.5 0.0 collective-permute-done.4.refs_0_
  13.5 0.0 copy-start.4
  13.6 0.3 collective-permute-start.5
  13.9 1.3 %collective-permute-start.2 = (bf16[128,1024]{1,0:T(8,128)(2,1)S(1)}, bf16[128,1024]{1,0:T(8,128)(2,1)S(1)}, u32[]{:S(2)}, u32[]{:S(2)}) collective-permute-start(bf16[128,1024]{1,0:T(8,128)(2,1)S(1)} %after.2.refs_2_.rest_ref.refs_3_.refs_0_), channel_id=1, source_target_pairs={{0,8},{2,10},{4,12},{6,14},{8,16},{10,18},{12,20},{14,22},{16,24},... | collective-permute-start | bytes 786440 | tf_op jit(solution)/shard_map/ppermute | solution.py:35
  15.2 4.1 %collective-permute-start.3 = (bf16[128,1024]{1,0:T(8,128)(2,1)S(1)}, bf16[128,1024]{1,0:T(8,128)(2,1)S(1)}, u32[]{:S(2)}, u32[]{:S(2)}) collective-permute-start(bf16[128,1024]{1,0:T(8,128)(2,1)S(1)} %after.2.refs_2_.rest_ref.refs_3_.refs_0_), channel_id=1, source_target_pairs={{0,4},{2,6},{4,8},{6,10},{8,12},{10,14},{12,16},{14,18},{16,20},{1... | collective-permute-start | bytes 786440 | tf_op jit(solution)/shard_map/ppermute | solution.py:40
  19.3 0.0 copy-done.4
  19.3 3.1 %pages.1 = (bf16[24,16,4,256]{3,2,1,0:T(4,128)(2,1)}, bf16[16,4,256]{2,1,0:T(4,128)(2,1)S(1)}) custom-call(s32[8]{0:T(128)S(1)} %copy-done.3, s32[1,24]{1,0:T(1,128)S(1)} %copy-done.4, bf16[128,1024]{1,0:T(8,128)(2,1)S(1)} %copy-done, bf16[128,1024]{1,0:T(8,128)(2,1)S(1)} %after.2.refs_2_.rest_ref.refs_3_.refs_0_), custom_call_target="tpu_custom_call" | custom-call | flops 11500000 | tf_op jit(solution)/shard_map/pages/pallas_call | solution.py:524
  22.4 0.0 collective-permute-done.5.refs_2_.refs_5_
  22.5 0.1 pick.4.refs_9_
  22.5 3.6 %collective-permute-start.7 = (bf16[256,1024]{1,0:T(8,128)(2,1)S(1)}, bf16[256,1024]{1,0:T(8,128)(2,1)S(1)}, u32[]{:S(2)}, u32[]{:S(2)}) collective-permute-start(bf16[256,1024]{1,0:T(8,128)(2,1)S(1)} %pick.4.refs_9_), channel_id=1, source_target_pairs={{0,2},{2,0},{4,6},{6,4},{8,10},{10,8},{12,14},{14,12},{16,18},{18,... | collective-permute-start | bytes 1572872 | tf_op jit(solution)/shard_map/ppermute | solution.py:45
  26.1 0.0 collective-permute-done.refs_1_
  26.1 3.3 %attend_part.4 = (f32[1,4,1,512]{3,2,1,0:T(1,128)S(1)}, f32[1,4,1,512]{3,2,1,0:T(1,128)S(1)}, f32[1,4,128,512]{3,2,1,0:T(8,128)S(1)}, f32[1,4,1,512]{3,2,1,0:T(1...) custom-call(s32[8]{0:T(128)S(1)} %copy-done.3, bf16[2048,128]{1,0:T(8,128)(2,1)S(1)} %get-tuple-element.26.refs_0_, ...), custom_call_target="tpu_custom_call" | custom-call | flops 11500000 | tf_op jit(solution)/shard_map/attend_part/pallas_call | solution.py:419
  29.4 0.0 collective-permute-done.2.refs_1_.refs_2_
  29.4 0.0 collective-permute-done.3.refs_2_.refs_3_
  29.4 0.1 pick.5.refs_11_
  29.5 0.1 collective-permute-start.6
  29.6 0.0 collective-permute-done.7.refs_4_.refs_10_
  29.6 4.0 %attend_part.5 = (f32[1,4,1,512]{3,2,1,0:T(1,128)S(1)}, f32[1,4,1,512]{3,2,1,0:T(1,128)S(1)}, f32[1,4,128,512]{3,2,1,0:T(8,128)S(1)}, f32[1,4,1,512]{3,2,1,0:T(1...) custom-call(s32[8]{0:T(128)S(1)} %copy-done.3, bf16[2048,128]{1,0:T(8,128)(2,1)S(1)} %get-tuple-element.26.refs_0_, ...), custom_call_target="tpu_custom_call" | custom-call | flops 11500000 | tf_op jit(solution)/shard_map/attend_part/pallas_call | solution.py:419
  33.5 0.0 collective-permute-done.6.refs_2_
  33.6 3.7 %attend_last.1 = (bf16[256,2048]{1,0:T(8,128)(2,1)}, bf16[24,16,4,256]{3,2,1,0:T(4,128)(2,1)}) custom-call(s32[8]{0:T(128)S(1)} %copy-done.3, bf16[2048,128]{1,0:T(8,128)(2,1)S(1)} %get-tuple-element.26.refs_0_, bf16[2048,128]{1,0:T(8,128)(2,1)S(1)} %collective-permute-done.refs_1_, ...), custom_call_target="tpu_custom_call", output_to_operand_aliasing={{1}: (13, {})} | custom-call | flops 11500000 | tf_op jit(solution)/shard_map/attend_last/pallas_call | solution.py:419
  (8 shorter events, 0.1 us)
Async XLA Ops:
  3.5 7.5 %collective-permute-start.1 = (bf16[128,1024]{1,0:T(8,128)(2,1)}, bf16[128,1024]{1,0:T(8,128)(2,1)S(1)}, u32[]{:S(2)}, u32[]{:S(2)}) collective-permute-start(bf16[128,1024]{1,0:T(8,128)(2,1)} %get-tuple-element.28), channel_id=1, source_target_pairs={{0,1},{1,0},{2,3},{3,2},{4,5},{5,4},{6,7},{7,6},{8,9},{9,8},{10,11... | collective-permute-start | bytes 786440 | tf_op jit(solution)/shard_map/ppermute | solution.py:35
  3.8 9.7 %collective-permute-start.4 = (bf16[128,1024]{1,0:T(8,128)(2,1)}, bf16[128,1024]{1,0:T(8,128)(2,1)S(1)}, u32[]{:S(2)}, u32[]{:S(2)}) collective-permute-start(bf16[128,1024]{1,0:T(8,128)(2,1)} %get-tuple-element.30.refs_1_.refs_0_.own_ref.refs_2_), channel_id=1, source_target_pairs={{0,8},{2,10},{4,12},{6,14},{8,16},{10,18},{12,20},{14,22},{16,24},... | collective-permute-start | bytes 786440 | tf_op jit(solution)/shard_map/ppermute | solution.py:35
  5.1 0.7 %copy-start.5 = (f32[128]{0:T(128)S(1)}, f32[128]{0:T(128)}, u32[]{:S(2)}) copy-start(f32[128]{0:T(128)} %param.10) | copy-start | bytes 1540
  5.7 1.2 %copy-start.1 = (bf16[128,4096]{1,0:T(8,128)(2,1)S(1)}, bf16[128,4096]{1,0:T(8,128)(2,1)}, u32[]{:S(2)}) copy-start(bf16[128,4096]{1,0:T(8,128)(2,1)} %q_ref.1) | copy-start | bytes 3145732
  7.0 0.8 %copy-start.2 = (f32[128,128]{1,0:T(8,128)S(1)}, f32[128,128]{1,0:T(8,128)}, u32[]{:S(2)}) copy-start(f32[128,128]{1,0:T(8,128)} %get-tuple-element.25.table_ref) | copy-start | bytes 196612
  8.6 17.5 %collective-permute-start = (bf16[2048,128]{1,0:T(8,128)(2,1)S(1)}, bf16[2048,128]{1,0:T(8,128)(2,1)S(1)}, u32[]{:S(2)}, u32[]{:S(2)}) collective-permute-start(bf16[2048,128]{1,0:T(8,128)(2,1)S(1)} %get-tuple-element.27), channel_id=1, source_target_pairs={{0,1},{1,0},{2,3},{3,2},{4,5},{5,4},{6,7},{7,6},{8,9},{9,8},{10,11... | collective-permute-start | bytes 1572872 | tf_op jit(solution)/shard_map/ppermute | solution.py:35
  10.9 1.0 %copy-start = (bf16[128,1024]{1,0:T(8,128)(2,1)S(1)}, bf16[128,1024]{1,0:T(8,128)(2,1)}, u32[]{:S(2)}) copy-start(bf16[128,1024]{1,0:T(8,128)(2,1)} %get-tuple-element.30.refs_1_.refs_0_.own_ref.refs_2_) | copy-start | bytes 786436
  10.9 0.9 %copy-start.3 = (s32[8]{0:T(128)S(1)}, s32[8]{0:T(128)}, u32[]{:S(2)}) copy-start(s32[8]{0:T(128)} %lengths.9) | copy-start | bytes 100
  13.5 5.8 %copy-start.4 = (s32[1,24]{1,0:T(1,128)S(1)}, s32[1,24]{1,0:T(1,128)}, u32[]{:S(2)}) copy-start(s32[1,24]{1,0:T(1,128)} %refs_9_.1) | copy-start | bytes 292
  13.6 8.9 %collective-permute-start.5 = (bf16[128,1024]{1,0:T(8,128)(2,1)S(1)}, bf16[128,1024]{1,0:T(8,128)(2,1)S(1)}, u32[]{:S(2)}, u32[]{:S(2)}) collective-permute-start(bf16[128,1024]{1,0:T(8,128)(2,1)S(1)} %pick.3), channel_id=1, source_target_pairs={{0,4},{2,6},{4,0},{6,2},{8,12},{10,14},{12,8},{14,10},{16,20},{18,... | collective-permute-start | bytes 786440 | tf_op jit(solution)/shard_map/ppermute | solution.py:45
  13.9 15.5 %collective-permute-start.2 = (bf16[128,1024]{1,0:T(8,128)(2,1)S(1)}, bf16[128,1024]{1,0:T(8,128)(2,1)S(1)}, u32[]{:S(2)}, u32[]{:S(2)}) collective-permute-start(bf16[128,1024]{1,0:T(8,128)(2,1)S(1)} %after.2.refs_2_.rest_ref.refs_3_.refs_0_), channel_id=1, source_target_pairs={{0,8},{2,10},{4,12},{6,14},{8,16},{10,18},{12,20},{14,22},{16,24},... | collective-permute-start | bytes 786440 | tf_op jit(solution)/shard_map/ppermute | solution.py:35
  15.2 14.2 %collective-permute-start.3 = (bf16[128,1024]{1,0:T(8,128)(2,1)S(1)}, bf16[128,1024]{1,0:T(8,128)(2,1)S(1)}, u32[]{:S(2)}, u32[]{:S(2)}) collective-permute-start(bf16[128,1024]{1,0:T(8,128)(2,1)S(1)} %after.2.refs_2_.rest_ref.refs_3_.refs_0_), channel_id=1, source_target_pairs={{0,4},{2,6},{4,8},{6,10},{8,12},{10,14},{12,16},{14,18},{16,20},{1... | collective-permute-start | bytes 786440 | tf_op jit(solution)/shard_map/ppermute | solution.py:40
  22.5 7.1 %collective-permute-start.7 = (bf16[256,1024]{1,0:T(8,128)(2,1)S(1)}, bf16[256,1024]{1,0:T(8,128)(2,1)S(1)}, u32[]{:S(2)}, u32[]{:S(2)}) collective-permute-start(bf16[256,1024]{1,0:T(8,128)(2,1)S(1)} %pick.4.refs_9_), channel_id=1, source_target_pairs={{0,2},{2,0},{4,6},{6,4},{8,10},{10,8},{12,14},{14,12},{16,18},{18,... | collective-permute-start | bytes 1572872 | tf_op jit(solution)/shard_map/ppermute | solution.py:45
  29.5 4.1 %collective-permute-start.6 = (bf16[256,1024]{1,0:T(8,128)(2,1)S(1)}, bf16[256,1024]{1,0:T(8,128)(2,1)S(1)}, u32[]{:S(2)}, u32[]{:S(2)}) collective-permute-start(bf16[256,1024]{1,0:T(8,128)(2,1)S(1)} %pick.5.refs_11_), channel_id=1, source_target_pairs={{0,2},{2,0},{4,6},{6,4},{8,10},{10,8},{12,14},{14,12},{16,18},{18,... | collective-permute-start | bytes 1572872 | tf_op jit(solution)/shard_map/ppermute | solution.py:45

commit v4 on v3

--- a/solution.py
+++ b/solution.py
@@ -90,9 +90,18 @@
     return cos_gain, sin_gain
 
 
-def kv_prep_body(heads, segs, lengths_in, k_in, v_in, gain_in, table_ref, *refs):
-    outs, (lengths, k_ref, v_ref, gain_ref, sems) = refs[:heads], refs[heads:]
+def table_rows(segs):
+    used = (segs + 16) // 16 * 16
+    starts = [D]
+    for rows in (used, used, 8, 8, 8):
+        starts.append(starts[-1] + rows)
+    return starts
+
+
+def kv_prep_body(heads, segs, lengths_in, k_in, v_in, gain_in, q_gain_in, table_ref, *refs):
+    outs, (lengths, k_ref, v_ref, gain_ref, q_gain_ref, sems) = refs[:heads], refs[heads:]
     pairs = [(lengths_in, lengths), (gain_in, gain_ref), (k_in, k_ref), (v_in, v_ref)]
+    pairs += [(q_gain_in, q_gain_ref)]
     copies = [pltpu.make_async_copy(a, b, sems.at[i]) for i, (a, b) in enumerate(pairs)]
     for copy in copies:
         copy.start()
@@ -109,7 +118,16 @@
     angles = offset * frequency
     cosine, sine = jnp.cos(angles), jnp.sin(angles)
     table_ref[:half] = cosine
-    table_ref[half:] = sine
+    table_ref[half:D] = sine
+    down, down_end, along, along_end, gain_at, stop = table_rows(segs)
+    begin, end = seg_bounds((down_end - down, D), 0, lengths, segs)
+    table_ref[down:down_end] = begin.astype(jnp.float32)
+    table_ref[down_end:along] = end.astype(jnp.float32)
+    begin, end = seg_bounds((8, D), 1, lengths, segs)
+    table_ref[along:along_end] = begin.astype(jnp.float32)
+    table_ref[along_end:gain_at] = end.astype(jnp.float32)
+    copies[4].wait()
+    table_ref[gain_at:stop] = jnp.broadcast_to(q_gain_ref[...], (8, D))
     copies[1].wait()
     cos_gain, sin_gain = gain_tables(cosine, sine, gain_ref[...])
     copies[2].wait()
@@ -125,35 +143,37 @@
             outs[d][:, (2 * j + 1) * D : (2 * j + 2) * D] = value.T
 
 
-def kv_prep(lengths, keys, values, gain, heads):
+def kv_prep(lengths, keys, values, gain, q_gain, heads):
     rows, width = keys.shape
-    table = jax.ShapeDtypeStruct((D, rows), jnp.float32)
+    table = jax.ShapeDtypeStruct((table_rows(lengths.shape[0])[-1], rows), jnp.float32)
     part = jax.ShapeDtypeStruct((rows, 2 * width // heads), jnp.bfloat16)
     return pl.pallas_call(
         functools.partial(kv_prep_body, heads, lengths.shape[0]),
         out_shape=[table] + [part] * heads,
-        in_specs=[HBM] * 4,
+        in_specs=[HBM] * 5,
         out_specs=[VMEM] * (1 + heads),
         scratch_shapes=[
             pltpu.SMEM(lengths.shape, jnp.int32),
             pltpu.VMEM(keys.shape, jnp.bfloat16),
             pltpu.VMEM(values.shape, jnp.bfloat16),
             pltpu.VMEM(gain.shape, jnp.float32),
-            pltpu.SemaphoreType.DMA((4,)),
+            pltpu.VMEM(gain.shape, jnp.float32),
+            pltpu.SemaphoreType.DMA((5,)),
         ],
         compiler_params=params(62),
         cost_estimate=cost(0.01),
         name="kv_prep",
-    )(lengths, keys, values, gain)
-
-
-def q_prep_body(heads, q_ref, gain_ref, table_ref, *refs):
+    )(lengths, keys, values, gain, q_gain)
+
+
+def q_prep_body(heads, segs, q_ref, table_ref, own_ref, *refs):
+    del own_ref
     *outs, token = refs
     token[...] = jnp.zeros_like(token)
     ql = q_ref.shape[1] // D // heads
     x = lax.axis_index("head")
     half = D // 2
-    cos_gain, sin_gain = gain_tables(table_ref[:half], table_ref[half:], gain_ref[...])
+    cos_gain, sin_gain = gain_tables(table_ref[:half], table_ref[half:D], table_ref[pl.ds(table_rows(segs)[4], 1), :])
     for d in reversed(range(heads)):
         peer = lax.rem(x + d, heads)
         for j in range(ql):
@@ -163,18 +183,18 @@
             )
 
 
-def q_prep(queries, gain, table, heads):
+def q_prep(queries, table, own, heads, segs):
     rows, width = queries.shape
     part = jax.ShapeDtypeStruct((width // heads, rows), jnp.bfloat16)
     return pl.pallas_call(
-        functools.partial(q_prep_body, heads),
+        functools.partial(q_prep_body, heads, segs),
         out_shape=[part] * heads + [TOKEN],
         in_specs=[VMEM] * 3,
         out_specs=[VMEM] * (heads + 1),
         compiler_params=params(),
         cost_estimate=cost(0.01),
         name="q_prep",
-    )(queries, gain, table)
+    )(queries, table, own)
 
 
 def shard_of(kind, tok):
@@ -190,7 +210,7 @@
     return jnp.where(core == 0, tok - 3, tok - 1)
 
 
-def attend_body(heads, segs, jobs, last, counts, lengths, *refs):
+def attend_body(heads, segs, jobs, last, counts, table, *refs):
     n_q, n_kv, n_state, n_earlier = counts
     q_refs, refs = refs[:n_q], refs[n_q:]
     kv_refs, refs = refs[:n_kv], refs[n_kv:]
@@ -210,9 +230,12 @@
     wide = group * rows
     lane = lax.broadcasted_iota(jnp.int32, (rows, rows), 1)
     sub = lax.broadcasted_iota(jnp.int32, (rows, rows), 0)
-    key_begin, key_end = seg_bounds((1, D), 1, lengths, segs)
-    used = (segs + 16) // 16 * 16
-    query_begin, query_end = seg_bounds((used, D), 0, lengths, segs)
+    down, down_end, along, along_end, _, _ = table_rows(segs)
+    used = down_end - down
+    query_begin = table[down:down_end].astype(jnp.int32)
+    query_end = table[down_end:along].astype(jnp.int32)
+    key_begin = table[along : along + 1].astype(jnp.int32)
+    key_end = table[along_end : along_end + 1].astype(jnp.int32)
 
     def key_block(pieces, g, side, axis):
         cols = at((2 * g + side) * D)
@@ -323,10 +346,6 @@
                 job, c = chunks[slot]
                 mix((i - 2) % bufs, job, c, g, origins[slot], tops[i - 2], totals[i - 2])
 
-    if last:
-        slots, own_s, head_ref, _ = earlier
-        first_page = (slots, own_s, kv_refs[0], head_ref, outs[1], *page)
-        send = partial_page(heads, segs, lengths, *first_page)
     if max(job[2] for job in jobs) == 1:
         sweep([(job, 0) for job in range(len(jobs))])
     else:
@@ -337,29 +356,30 @@
 
             lax.fori_loop(0, jobs[job][2], body, 0)
     if last:
+        slots, own_s, head_ref, _ = earlier
+        first_page = (slots, own_s, kv_refs[0], head_ref, outs[1], *page)
+        finish = partial_page(heads, query_begin, query_end, *first_page)
         for origin in range(heads):
             for g in range(kvl):
                 out_part(origin, g).wait()
-        send()
-
-
-def partial_page(heads, segs, lengths, slots, own_s, rest_s, head_ref, pool_ref, page, sem):
+        finish()
+
+
+def partial_page(heads, begins, ends, slots, own_s, rest_s, head_ref, pool_ref, page, sem):
     x = lax.axis_index("head")
     tok = lax.axis_index("tok")
     core = lax.rem(tok, 2)
     base = tok * heads * D
-    first = jnp.int32(0)
-    end = jnp.int32(0)
-    for s in range(segs):
-        end = end + lengths[s]
-        first = jnp.where(end <= base, end, first)
+    here = (begins <= base) & (base < ends)
+    first = jnp.max(jnp.where(here, begins.astype(jnp.float32), 0.0)).astype(jnp.int32)
     before = lax.rem(base - first, PAGE)
+    slot = jnp.max(slots[:, :1].astype(jnp.float32)).astype(jnp.int32)
     kvl = head_ref.shape[1]
     d = lax.rem(x + 1, heads)
     lane = lax.broadcasted_iota(jnp.int32, (PAGE, PAGE), 1)
     sub = lax.broadcasted_iota(jnp.int32, (PAGE, PAGE), 0)
     move = jnp.where((lane == sub + PAGE - before) & (sub < before), 1.0, 0.0).astype(jnp.bfloat16)
-    copy = pltpu.make_async_copy(page, pool_ref.at[slots[0, 0]], sem)
+    copy = pltpu.make_async_copy(page, pool_ref.at[slot], sem)
 
     def write(ref, row):
         moved = []
@@ -392,7 +412,7 @@
     return finish
 
 
-def attend(lengths, qs, kvs, jobs, last, heads, *earlier):
+def attend(table, qs, kvs, jobs, last, heads, segs, *earlier):
     kvl = kvs[0].shape[1] // (2 * D)
     states, plan = [], []
     for q, first, state, pieces in jobs:
@@ -411,18 +431,18 @@
         for _, _, many, _, _ in plan:
             row = jax.ShapeDtypeStruct((many, kvl, 1, wide), jnp.float32)
             out_shape += [row, row, jax.ShapeDtypeStruct((many, kvl, D, wide), jnp.float32)]
-    inputs = [lengths, *qs, *kvs, *[part for state in states for part in state], *earlier]
-    more = [SMEM, VMEM, VMEM, ANY] if last else [ANY] * len(earlier)
+    inputs = [table, *qs, *kvs, *[part for state in states for part in state], *earlier]
+    more = [VMEM, VMEM, VMEM, ANY] if last else [ANY] * len(earlier)
     keys = max(len(job[4]) for job in plan) * D
     together = len(plan) if heads == 2 else 1
     bufs = min(3, kvl * together)
     result = pl.pallas_call(
         functools.partial(
-            attend_body, heads, lengths.shape[0], tuple(plan), last,
+            attend_body, heads, segs, tuple(plan), last,
             (len(qs), len(kvs), len(states), len(earlier)),
         ),
         out_shape=out_shape,
-        in_specs=[SMEM] + [VMEM] * (len(inputs) - 1 - len(earlier)) + more,
+        in_specs=[VMEM] * (len(inputs) - len(earlier)) + more,
         out_specs=[ANY, ANY] if last else [VMEM] * len(out_shape),
         input_output_aliases={len(inputs) - 1: 1} if last else {},
         scratch_shapes=[
@@ -449,50 +469,49 @@
 
 
 def pages_body(
-    heads, segs, pool, lengths, slots, own_ref, rest_ref, pool_ref, head_ref, hot, ends,
-    wide_scr, out_scr, sems,
+    heads, segs, pool, table, slots, own_ref, rest_ref, pool_ref, head_ref,
+    slot_scr, wide_scr, out_scr, sems,
 ):
-    rows = D
-    shard_rows = heads * rows
     x = lax.axis_index("head")
-    base = lax.axis_index("tok") * shard_rows
-    end = jnp.int32(0)
-    for s in range(segs):
-        end = end + lengths[s]
-        ends[s] = end
-    hot[...] = jnp.zeros_like(hot)
-    width = hot.shape[1]
-    lane = lax.broadcasted_iota(jnp.int32, (PAGE, width), 1)
-    sub = lax.broadcasted_iota(jnp.int32, (PAGE, width), 0)
-
-    def finish_of(a):
-        found = jnp.int32(0)
-        for s in reversed(range(segs)):
-            found = jnp.where(ends[s] > a, ends[s], found)
-        return found
-
-    first = jnp.int32(0)
-    for s in range(segs):
-        first = jnp.where(ends[s] <= base, ends[s], first)
-    page = first + ((base - first) // PAGE) * PAGE
-
-    def one_page(rank, a):
-        stop = jnp.minimum(a + PAGE, finish_of(a))
-        owned = (stop > base) & (stop <= base + shard_rows)
-
-        @pl.when(owned)
-        def _():
-            token = sub + (a - base)
-            piece = token // rows
-            d = lax.rem(x - piece + 2 * heads, heads)
-            column = jnp.where(token < 0, -1, (d - piece) * rows + token)
-            mark = (lane == column) & (sub < stop - a)
-            slot = slots[0, rank]
-            hot[pl.ds(pl.multiple_of(slot * PAGE, PAGE), PAGE), :] = mark.astype(hot.dtype)
-
-        return jnp.where(owned, stop, a)
-
-    lax.fori_loop(0, pool, one_page, page)
+    base = lax.axis_index("tok") * heads * D
+    down, down_end, along, _, _, _ = table_rows(segs)
+    begins, ends = table[down:down_end], table[down_end:along]
+    lane = lax.broadcasted_iota(jnp.int32, (1, D), 1)
+    sub = lax.broadcasted_iota(jnp.int32, (D, D), 0)
+    starts = [base + lax.rem(x - d + heads, heads) * D for d in range(heads)]
+    flags, rows, owned = [], [], []
+    for start in starts:
+        pos = start + lane
+        point = pos.astype(jnp.float32)
+        here = (point >= begins) & (point < ends)
+        first = jnp.sum(jnp.where(here, begins, 0.0), axis=0, keepdims=True).astype(jnp.int32)
+        finish = jnp.sum(jnp.where(here, ends, 0.0), axis=0, keepdims=True).astype(jnp.int32)
+        offset = pos - first
+        rows.append(lax.rem(offset, PAGE))
+        page_last = jnp.minimum(pos - rows[-1] + PAGE, finish) - 1
+        owned.append(page_last < base + heads * D)
+        flags.append(jnp.where(pos == page_last, 1.0, 0.0))
+    flags = jnp.broadcast_to(jnp.concatenate(flags, axis=1), (16, heads * D)).astype(jnp.bfloat16)
+    slot_scr[...] = jnp.zeros_like(slot_scr)
+    slot_scr[0:1, 0:pool] = slots[...].astype(jnp.float32)
+    slot_row = slot_scr[...].astype(jnp.bfloat16)
+    ranks, targets = [], []
+    for d, start in enumerate(starts):
+        ahead = [jnp.where(other + sub < start + lane, 1.0, 0.0) for other in starts]
+        ahead = jnp.concatenate(ahead, axis=0).astype(jnp.bfloat16)
+        rank = jnp.dot(flags, ahead, preferred_element_type=jnp.float32)[:1].astype(jnp.int32)
+        pick_slot = jnp.where(sub == rank, 1.0, 0.0).astype(jnp.bfloat16)
+        slot = jnp.dot(slot_row, pick_slot, preferred_element_type=jnp.float32)[:1]
+        row = slot.astype(jnp.int32) * PAGE + rows[d]
+        targets.append(jnp.where(owned[d], row, -1))
+        ranks.append(jnp.where(owned[d] & (rank == 0), rows[d], -1))
+    target = jnp.concatenate(targets, axis=1)
+    head_target = jnp.concatenate(ranks, axis=1)
+
+    def marks(first_row, rows, target):
+        row = first_row + lax.broadcasted_iota(jnp.int32, (rows, heads * D), 0)
+        return jnp.where(row == target, 1.0, 0.0).astype(jnp.bfloat16)
+
     kvl = own_ref.shape[1] // (2 * D)
     both = []
     for g in range(kvl):
@@ -504,7 +523,7 @@
     step = 8
     copies = []
     for i, page in enumerate(range(0, pool, step)):
-        mark = hot[page * PAGE : (page + step) * PAGE, :].astype(jnp.bfloat16)
+        mark = marks(page * PAGE, step * PAGE, target)
         for g in range(kvl):
             wide_scr[i % 2, :, g, :] = jnp.dot(mark, both[g], preferred_element_type=jnp.float32)
         block = pl.ds(page, step)
@@ -513,25 +532,26 @@
         )
         copies.append(pltpu.make_async_copy(out_scr.at[block], pool_ref.at[block], sems.at[i]))
         copies[-1].start()
-    head_ref[...] = out_scr[slots[0, 0]]
+    mark = marks(0, PAGE, head_target)
+    head = [jnp.dot(mark, part, preferred_element_type=jnp.float32) for part in both]
+    head_ref[...] = jnp.stack(head, axis=1).astype(jnp.bfloat16)
     for copy in copies:
         copy.wait()
 
 
-def pages(lengths, slots, own, rest, heads):
+def pages(table, slots, own, rest, heads, segs):
     pool = slots.shape[1]
     kvl = own.shape[1] // (2 * D)
     return pl.pallas_call(
-        functools.partial(pages_body, heads, lengths.shape[0], pool),
+        functools.partial(pages_body, heads, segs, pool),
         out_shape=[
             jax.ShapeDtypeStruct((pool, PAGE, kvl, 2 * D), jnp.bfloat16),
             jax.ShapeDtypeStruct((PAGE, kvl, 2 * D), jnp.bfloat16),
         ],
-        in_specs=[SMEM, SMEM, VMEM, VMEM],
+        in_specs=[VMEM] * 4,
         out_specs=[ANY, VMEM],
         scratch_shapes=[
-            pltpu.VMEM((pool * PAGE, heads * D), jnp.float32),
-            pltpu.SMEM((lengths.shape[0],), jnp.int32),
+            pltpu.VMEM((16, D), jnp.float32),
             pltpu.VMEM((2, 8 * PAGE, kvl, 2 * D), jnp.float32),
             pltpu.VMEM((pool, PAGE, kvl, 2 * D), jnp.bfloat16),
             pltpu.SemaphoreType.DMA((pool // 8,)),
@@ -539,7 +559,7 @@
         compiler_params=params(),
         cost_estimate=cost(0.01),
         name="pages",
-    )(lengths, slots, own, rest)
+    )(table, slots, own, rest)
 
 
 def pick_body(bit, plan, *refs):
@@ -595,28 +615,29 @@
     others = range(1, heads)
 
     table, own, *away = kv_prep(
-        lengths, key_states, value_states, key_gain.reshape(1, D), heads
+        lengths, key_states, value_states, key_gain.reshape(1, D), query_gain.reshape(1, D), heads
     )
+    segs = lengths.shape[0]
     rest = join([around(part, "head", d) for d, part in enumerate(away, 1)])
     own4 = around(own, "tok", 4)
-    q_own, *q_away, turned = q_prep(queries, query_gain.reshape(1, D), table, heads)
+    q_own, *q_away, turned = q_prep(queries, table, own, heads, segs)
     q_rest = join([around(part, "head", d) for d, part in enumerate(q_away, 1)])
     rest = after(rest, turned)
     rest4, rest2 = around(rest, "tok", 4), onward(rest, "tok", 2)
     base = [(0, 0, "own", 0)] + [(1, d - 1, "own", d) for d in others]
-    [own_state] = attend(lengths, [q_own], [own, rest], [(0, 0, None, base)], False, heads)
+    [own_state] = attend(table, [q_own], [own, rest], [(0, 0, None, base)], False, heads, segs)
 
     own4 = after(own4, own_state[0])
     own2 = swap(pick(2, ((0, 1),), own, own4), 2)
-    page_pool, head_page = pages(lengths, slot_order, own, rest, heads)
+    page_pool, head_page = pages(table, slot_order, own, rest, heads, segs)
     own_mixed = pick(1, ((0, 1), (2,)), own, own4, own2, head_page)
     own_s = swap(own_mixed, 1)
 
     qs = [q_own, q_rest]
     near = [(2, 0, "far", 0), (3, 0, "near", 0)]
     own_state, rest_state = attend(
-        lengths, qs, [own, rest, own4, own2],
-        [(0, 0, own_state, near), (1, 1, None, base + near)], False, heads,
+        table, qs, [own, rest, own4, own2],
+        [(0, 0, own_state, near), (1, 1, None, base + near)], False, heads, segs,
         own_mixed,
     )
 
@@ -625,14 +646,14 @@
     pieces = [(2, 0, "mix_swap", 0), (2, 1, "near_swap", 0)]
     pieces += [(0, d - 1, "far", d) for d in others] + [(1, d - 1, "near", d) for d in others]
     own_state, rest_state = attend(
-        lengths, qs, [rest4, rest2, own_s],
-        [(0, 0, own_state, pieces), (1, 1, rest_state, pieces)], False, heads, rest_mixed,
+        table, qs, [rest4, rest2, own_s],
+        [(0, 0, own_state, pieces), (1, 1, rest_state, pieces)], False, heads, segs, rest_mixed,
     )
     pieces = [(0, d - 1, "mix_swap", d) for d in others]
     pieces += [(0, heads + d - 2, "near_swap", d) for d in others]
     attention, page_pool = attend(
-        lengths, qs, [rest_s],
-        [(0, 0, own_state, pieces), (1, 1, rest_state, pieces)], True, heads,
+        table, qs, [rest_s],
+        [(0, 0, own_state, pieces), (1, 1, rest_state, pieces)], True, heads, segs,
         slot_order, own_s, head_page, page_pool,
     )
     return (attention, page_pool)

time: 37.6 us -> 35.2 us (0.936)
  the two profiles are of different devices: /device:TPU:15 before, /device:TPU:5 now
where the time goes in v4:
time: 35.2 us; the launch traced here: 34.8 us
  Pallas kernels  16.1 us (46%)
  starting transfers between devices  12.5 us (36%)
  local copies, waits for them, and re-layouts  3.1 us (9%)
  waiting for transfers between devices  2.41 us (7%)
  between operations  0.75 us (2%)
    pallas_call x4, Pallas kernels, attend(): pl.pallas_call(functools.partial(attend_body, heads, segs, tuple(plan), l...  10.4 us
    ppermute x3, starting transfers between devices, swap(): return lax.ppermute(x, 'tok', [(i, i ^ bit) for i in range(peers)])  5.8 us
    ppermute x1, starting transfers between devices, onward(): return lax.ppermute(x, axis, [(i, i + by) for i in range(peers - by)])  3.76 us
    unnamed x8, local copies, waits for them, and re-layouts  3.1 us
    ppermute x4, starting transfers between devices, around(): return lax.ppermute(x, axis, [(i, (i + by) % peers) for i in range(peers)])  2.9 us
    pallas_call x1, Pallas kernels, kv_prep(): pl.pallas_call(functools.partial(kv_prep_body, heads, lengths.shape[0]),...  2.83 us
    ppermute x4, waiting for transfers between devices, around(): return lax.ppermute(x, axis, [(i, (i + by) % peers) for i in range(peers)])  2.4 us
    pallas_call x1, Pallas kernels, pages(): pl.pallas_call(functools.partial(pages_body, heads, segs, pool), out_shap...  2.02 us
  transfers between devices with their start and end apart: 8, of which 2 were waited for; matrix products, arithmetic and copies ran while one was open for 0% of the time, Pallas kernels for 29%

profile of v4, /device:TPU:5, one launch (start us, length us, event | category | flops | bytes accessed | tf_op | source)
XLA Modules:
  0.0 34.8 jit_solution(2497436132356066334)
XLA Ops:
  0.6 2.8 %kv_prep.1 = (f32[184,128]{1,0:T(8,128)}, bf16[128,1024]{1,0:T(8,128)(2,1)}, bf16[128,1024]{1,0:T(8,128)(2,1)}) custom-call(s32[8]{0:T(128)} %lengths_in.1, bf16[128,1024]{1,0:T(8,128)(2,1)} %k_in.1, bf16[128,1024]{1,0:T(8,128)(2,1)} %v_in.1, f32[1,128]{1,0:T(1,128)} %bitcast.2, f32[1,128]{1,0:T(1,128)} %bitcast.3), custom_call_target="tpu_custom_call" | custom-call | flops 11500000 | tf_op jit(solution)/shard_map/kv_prep/pallas_call | solution.py:150
  3.5 1.3 %collective-permute-start.1 = (bf16[128,1024]{1,0:T(8,128)(2,1)}, bf16[128,1024]{1,0:T(8,128)(2,1)S(1)}, u32[]{:S(2)}, u32[]{:S(2)}) collective-permute-start(bf16[128,1024]{1,0:T(8,128)(2,1)} %get-tuple-element.29), channel_id=1, source_target_pairs={{0,1},{1,0},{2,3},{3,2},{4,5},{5,4},{6,7},{7,6},{8,9},{9,8},{10,11... | collective-permute-start | bytes 786440 | tf_op jit(solution)/shard_map/ppermute | solution.py:35
  4.7 1.3 %collective-permute-start.4 = (bf16[128,1024]{1,0:T(8,128)(2,1)}, bf16[128,1024]{1,0:T(8,128)(2,1)S(1)}, u32[]{:S(2)}, u32[]{:S(2)}) collective-permute-start(bf16[128,1024]{1,0:T(8,128)(2,1)} %get-tuple-element.26.own_ref.refs_1_.refs_0_.refs_2_), channel_id=1, source_target_pairs={{0,8},{2,10},{4,12},{6,14},{8,16},{10,18},{12,20},{14,22},{16,24},... | collective-permute-start | bytes 786440 | tf_op jit(solution)/shard_map/ppermute | solution.py:35
  6.0 0.0 copy-start
  6.0 1.0 %copy-done = bf16[128,1024]{1,0:T(8,128)(2,1)S(1)} copy-done((bf16[128,1024]{1,0:T(8,128)(2,1)S(1)}, bf16[128,1024]{1,0:T(8,128)(2,1)}, u32[]{:S(2)}) %copy-start) | copy-done | bytes 262168
  7.0 0.0 copy-start.1
  7.0 0.9 %copy-done.1 = f32[184,128]{1,0:T(8,128)S(1)} copy-done((f32[184,128]{1,0:T(8,128)S(1)}, f32[184,128]{1,0:T(8,128)}, u32[]{:S(2)}) %copy-start.1) | copy-done | bytes 94232
  7.9 0.0 copy-start.2
  7.9 1.2 %copy-done.2 = bf16[128,4096]{1,0:T(8,128)(2,1)S(1)} copy-done((bf16[128,4096]{1,0:T(8,128)(2,1)S(1)}, bf16[128,4096]{1,0:T(8,128)(2,1)}, u32[]{:S(2)}) %copy-start.2) | copy-done | bytes 1048600
  9.1 0.8 %q_prep.1 = (bf16[2048,128]{1,0:T(8,128)(2,1)S(1)}, bf16[2048,128]{1,0:T(8,128)(2,1)S(1)}, f32[8,128]{1,0:T(8,128)S(1)}) custom-call(bf16[128,4096]{1,0:T(8,128)(2,1)S(1)} %copy-done.2, f32[184,128]{1,0:T(8,128)S(1)} %copy-done.1, bf16[128,1024]{1,0:T(8,128)(2,1)S(1)} %copy-done), custom_call_target="tpu_custom_call" | custom-call | flops 11500000 | tf_op jit(solution)/shard_map/q_prep/pallas_call | solution.py:189
  9.9 0.3 collective-permute-start
  10.3 0.7 %collective-permute-done.1.refs_0_ = bf16[128,1024]{1,0:T(8,128)(2,1)S(1)} collective-permute-done((bf16[128,1024]{1,0:T(8,128)(2,1)}, bf16[128,1024]{1,0:T(8,128)(2,1)S(1)}, u32[]{:S(2)}, u32[]{:S(2)}) %collective-permute-start.1) | collective-permute-done | bytes 262176 | tf_op jit(solution)/shard_map/ppermute | solution.py:35
  10.9 1.1 %attend_part.3 = (f32[1,4,1,512]{3,2,1,0:T(1,128)S(1)}, f32[1,4,1,512]{3,2,1,0:T(1,128)S(1)}, f32[1,4,128,512]{3,2,1,0:T(8,128)S(1)}) custom-call(f32[184,128]{1,0:T(8,128)S(1)} %copy-done.1, bf16[2048,128]{1,0:T(8,128)(2,1)S(1)} %get-tuple-element.27.refs_0_, bf16[128,1024]{1,0:T(8,128)(2,1)S(1)} %copy-done, ...), custom_call_target="tpu_custom_call" | custom-call | flops 11500000 | tf_op jit(solution)/shard_map/attend_part/pallas_call | solution.py:439
  12.0 1.7 %collective-permute-done.4.refs_0_ = bf16[128,1024]{1,0:T(8,128)(2,1)S(1)} collective-permute-done((bf16[128,1024]{1,0:T(8,128)(2,1)}, bf16[128,1024]{1,0:T(8,128)(2,1)S(1)}, u32[]{:S(2)}, u32[]{:S(2)}) %collective-permute-start.4) | collective-permute-done | bytes 262176 | tf_op jit(solution)/shard_map/ppermute | solution.py:35
  13.8 0.3 collective-permute-start.5
  14.1 0.0 collective-permute-start.2
  14.1 3.8 %collective-permute-start.3 = (bf16[128,1024]{1,0:T(8,128)(2,1)S(1)}, bf16[128,1024]{1,0:T(8,128)(2,1)S(1)}, u32[]{:S(2)}, u32[]{:S(2)}) collective-permute-start(bf16[128,1024]{1,0:T(8,128)(2,1)S(1)} %after.2.refs_2_.rest_ref.refs_3_.refs_0_), channel_id=1, source_target_pairs={{0,4},{2,6},{4,8},{6,10},{8,12},{10,14},{12,16},{14,18},{16,20},{1... | collective-permute-start | bytes 786440 | tf_op jit(solution)/shard_map/ppermute | solution.py:40
  17.8 0.0 copy-done.3
  17.8 2.0 %pages.1 = (bf16[24,16,4,256]{3,2,1,0:T(4,128)(2,1)}, bf16[16,4,256]{2,1,0:T(4,128)(2,1)S(1)}) custom-call(f32[184,128]{1,0:T(8,128)S(1)} %copy-done.1, s32[1,24]{1,0:T(1,128)S(1)} %copy-done.3, bf16[128,1024]{1,0:T(8,128)(2,1)S(1)} %copy-done, bf16[128,1024]{1,0:T(8,128)(2,1)S(1)} %after.2.refs_2_.rest_ref.refs_3_.refs_0_), custom_call_target="tpu_custom_call" | custom-call | flops 11500000 | tf_op jit(solution)/shard_map/pages/pallas_call | solution.py:545
  19.9 0.0 collective-permute-done.5.refs_2_.refs_5_
  19.9 0.1 pick.4.refs_9_
  19.9 5.0 %collective-permute-start.7 = (bf16[256,1024]{1,0:T(8,128)(2,1)S(1)}, bf16[256,1024]{1,0:T(8,128)(2,1)S(1)}, u32[]{:S(2)}, u32[]{:S(2)}) collective-permute-start(bf16[256,1024]{1,0:T(8,128)(2,1)S(1)} %pick.4.refs_9_), channel_id=1, source_target_pairs={{0,2},{2,0},{4,6},{6,4},{8,10},{10,8},{12,14},{14,12},{16,18},{18,... | collective-permute-start | bytes 1572872 | tf_op jit(solution)/shard_map/ppermute | solution.py:45
  25.0 0.0 collective-permute-done.refs_1_
  25.0 2.7 %attend_part.4 = (f32[1,4,1,512]{3,2,1,0:T(1,128)S(1)}, f32[1,4,1,512]{3,2,1,0:T(1,128)S(1)}, f32[1,4,128,512]{3,2,1,0:T(8,128)S(1)}, f32[1,4,1,512]{3,2,1,0:T(1...) custom-call(f32[184,128]{1,0:T(8,128)S(1)} %copy-done.1, ...), custom_call_target="tpu_custom_call" | custom-call | flops 11500000 | tf_op jit(solution)/shard_map/attend_part/pallas_call | solution.py:439
  27.7 0.0 collective-permute-done.2.refs_1_.refs_2_
  27.7 0.0 collective-permute-done.3.refs_2_.refs_3_
  27.7 0.1 pick.5.refs_11_
  27.8 0.5 %collective-permute-start.6 = (bf16[256,1024]{1,0:T(8,128)(2,1)S(1)}, bf16[256,1024]{1,0:T(8,128)(2,1)S(1)}, u32[]{:S(2)}, u32[]{:S(2)}) collective-permute-start(bf16[256,1024]{1,0:T(8,128)(2,1)S(1)} %pick.5.refs_11_), channel_id=1, source_target_pairs={{0,2},{2,0},{4,6},{6,4},{8,10},{10,8},{12,14},{14,12},{16,18},{18,... | collective-permute-start | bytes 1572872 | tf_op jit(solution)/shard_map/ppermute | solution.py:45
  28.3 0.0 collective-permute-done.7.refs_4_.refs_10_
  28.3 3.4 %attend_part.5 = (f32[1,4,1,512]{3,2,1,0:T(1,128)S(1)}, f32[1,4,1,512]{3,2,1,0:T(1,128)S(1)}, f32[1,4,128,512]{3,2,1,0:T(8,128)S(1)}, f32[1,4,1,512]{3,2,1,0:T(1...) custom-call(f32[184,128]{1,0:T(8,128)S(1)} %copy-done.1, ...), custom_call_target="tpu_custom_call" | custom-call | flops 11500000 | tf_op jit(solution)/shard_map/attend_part/pallas_call | solution.py:439
  31.7 0.0 collective-permute-done.6.refs_2_
  31.7 3.1 %attend_last.1 = (bf16[256,2048]{1,0:T(8,128)(2,1)}, bf16[24,16,4,256]{3,2,1,0:T(4,128)(2,1)}) custom-call(f32[184,128]{1,0:T(8,128)S(1)} %copy-done.1, bf16[2048,128]{1,0:T(8,128)(2,1)S(1)} %get-tuple-element.27.refs_0_, bf16[2048,128]{1,0:T(8,128)(2,1)S(1)} %collective-permute-done.refs_1_, ...), custom_call_target="tpu_custom_call", output_to_operand_aliasing={{1}: (13, {})} | custom-call | flops 11500000 | tf_op jit(solution)/shard_map/attend_last/pallas_call | solution.py:439
  (4 shorter events, 0.0 us)
Async XLA Ops:
  3.5 7.5 %collective-permute-start.1 = (bf16[128,1024]{1,0:T(8,128)(2,1)}, bf16[128,1024]{1,0:T(8,128)(2,1)S(1)}, u32[]{:S(2)}, u32[]{:S(2)}) collective-permute-start(bf16[128,1024]{1,0:T(8,128)(2,1)} %get-tuple-element.29), channel_id=1, source_target_pairs={{0,1},{1,0},{2,3},{3,2},{4,5},{5,4},{6,7},{7,6},{8,9},{9,8},{10,11... | collective-permute-start | bytes 786440 | tf_op jit(solution)/shard_map/ppermute | solution.py:35
  4.7 9.0 %collective-permute-start.4 = (bf16[128,1024]{1,0:T(8,128)(2,1)}, bf16[128,1024]{1,0:T(8,128)(2,1)S(1)}, u32[]{:S(2)}, u32[]{:S(2)}) collective-permute-start(bf16[128,1024]{1,0:T(8,128)(2,1)} %get-tuple-element.26.own_ref.refs_1_.refs_0_.refs_2_), channel_id=1, source_target_pairs={{0,8},{2,10},{4,12},{6,14},{8,16},{10,18},{12,20},{14,22},{16,24},... | collective-permute-start | bytes 786440 | tf_op jit(solution)/shard_map/ppermute | solution.py:35
  6.0 1.0 %copy-start = (bf16[128,1024]{1,0:T(8,128)(2,1)S(1)}, bf16[128,1024]{1,0:T(8,128)(2,1)}, u32[]{:S(2)}) copy-start(bf16[128,1024]{1,0:T(8,128)(2,1)} %get-tuple-element.26.own_ref.refs_1_.refs_0_.refs_2_) | copy-start | bytes 786436
  7.0 0.9 %copy-start.1 = (f32[184,128]{1,0:T(8,128)S(1)}, f32[184,128]{1,0:T(8,128)}, u32[]{:S(2)}) copy-start(f32[184,128]{1,0:T(8,128)} %get-tuple-element.25.table_ref.table) | copy-start | bytes 282628
  7.9 1.2 %copy-start.2 = (bf16[128,4096]{1,0:T(8,128)(2,1)S(1)}, bf16[128,4096]{1,0:T(8,128)(2,1)}, u32[]{:S(2)}) copy-start(bf16[128,4096]{1,0:T(8,128)(2,1)} %q_ref.1) | copy-start | bytes 3145732
  9.9 15.0 %collective-permute-start = (bf16[2048,128]{1,0:T(8,128)(2,1)S(1)}, bf16[2048,128]{1,0:T(8,128)(2,1)S(1)}, u32[]{:S(2)}, u32[]{:S(2)}) collective-permute-start(bf16[2048,128]{1,0:T(8,128)(2,1)S(1)} %get-tuple-element.28), channel_id=1, source_target_pairs={{0,1},{1,0},{2,3},{3,2},{4,5},{5,4},{6,7},{7,6},{8,9},{9,8},{10,11... | collective-permute-start | bytes 1572872 | tf_op jit(solution)/shard_map/ppermute | solution.py:35
  13.7 4.1 %copy-start.3 = (s32[1,24]{1,0:T(1,128)S(1)}, s32[1,24]{1,0:T(1,128)}, u32[]{:S(2)}) copy-start(s32[1,24]{1,0:T(1,128)} %refs_9_.1) | copy-start | bytes 292
  13.8 6.1 %collective-permute-start.5 = (bf16[128,1024]{1,0:T(8,128)(2,1)S(1)}, bf16[128,1024]{1,0:T(8,128)(2,1)S(1)}, u32[]{:S(2)}, u32[]{:S(2)}) collective-permute-start(bf16[128,1024]{1,0:T(8,128)(2,1)S(1)} %pick.3), channel_id=1, source_target_pairs={{0,4},{2,6},{4,0},{6,2},{8,12},{10,14},{12,8},{14,10},{16,20},{18,... | collective-permute-start | bytes 786440 | tf_op jit(solution)/shard_map/ppermute | solution.py:45
  14.1 13.7 %collective-permute-start.2 = (bf16[128,1024]{1,0:T(8,128)(2,1)S(1)}, bf16[128,1024]{1,0:T(8,128)(2,1)S(1)}, u32[]{:S(2)}, u32[]{:S(2)}) collective-permute-start(bf16[128,1024]{1,0:T(8,128)(2,1)S(1)} %after.2.refs_2_.rest_ref.refs_3_.refs_0_), channel_id=1, source_target_pairs={{0,8},{2,10},{4,12},{6,14},{8,16},{10,18},{12,20},{14,22},{16,24},... | collective-permute-start | bytes 786440 | tf_op jit(solution)/shard_map/ppermute | solution.py:35
  14.1 13.7 %collective-permute-start.3 = (bf16[128,1024]{1,0:T(8,128)(2,1)S(1)}, bf16[128,1024]{1,0:T(8,128)(2,1)S(1)}, u32[]{:S(2)}, u32[]{:S(2)}) collective-permute-start(bf16[128,1024]{1,0:T(8,128)(2,1)S(1)} %after.2.refs_2_.rest_ref.refs_3_.refs_0_), channel_id=1, source_target_pairs={{0,4},{2,6},{4,8},{6,10},{8,12},{10,14},{12,16},{14,18},{16,20},{1... | collective-permute-start | bytes 786440 | tf_op jit(solution)/shard_map/ppermute | solution.py:40
  19.9 8.3 %collective-permute-start.7 = (bf16[256,1024]{1,0:T(8,128)(2,1)S(1)}, bf16[256,1024]{1,0:T(8,128)(2,1)S(1)}, u32[]{:S(2)}, u32[]{:S(2)}) collective-permute-start(bf16[256,1024]{1,0:T(8,128)(2,1)S(1)} %pick.4.refs_9_), channel_id=1, source_target_pairs={{0,2},{2,0},{4,6},{6,4},{8,10},{10,8},{12,14},{14,12},{16,18},{18,... | collective-permute-start | bytes 1572872 | tf_op jit(solution)/shard_map/ppermute | solution.py:45
  27.8 3.9 %collective-permute-start.6 = (bf16[256,1024]{1,0:T(8,128)(2,1)S(1)}, bf16[256,1024]{1,0:T(8,128)(2,1)S(1)}, u32[]{:S(2)}, u32[]{:S(2)}) collective-permute-start(bf16[256,1024]{1,0:T(8,128)(2,1)S(1)} %pick.5.refs_11_), channel_id=1, source_target_pairs={{0,2},{2,0},{4,6},{6,4},{8,10},{10,8},{12,14},{14,12},{16,18},{18,... | collective-permute-start | bytes 1572872 | tf_op jit(solution)/shard_map/ppermute | solution.py:45

commit v5 on v4

--- a/solution.py
+++ b/solution.py
@@ -136,9 +136,9 @@
         peer = lax.rem(x + d, heads)
         for j in range(kvl):
             head = peer * kvl + j
-            key = k_ref[:, at(head * D)].astype(jnp.float32).T
-            key = rotate(key, cos_gain, sin_gain).T
-            outs[d][:, 2 * j * D : (2 * j + 1) * D] = key.astype(jnp.bfloat16)
+            key = k_ref[:, at(head * D)].T.astype(jnp.float32)
+            key = rotate(key, cos_gain, sin_gain).astype(jnp.bfloat16)
+            outs[d][:, 2 * j * D : (2 * j + 1) * D] = key.T
             value = v_ref[:, at(head * D)]
             outs[d][:, (2 * j + 1) * D : (2 * j + 2) * D] = value.T
 
@@ -177,7 +177,7 @@
     for d in reversed(range(heads)):
         peer = lax.rem(x + d, heads)
         for j in range(ql):
-            query = q_ref[:, at((peer * ql + j) * D)].astype(jnp.float32).T
+            query = q_ref[:, at((peer * ql + j) * D)].T.astype(jnp.float32)
             outs[d][j * D : (j + 1) * D, :] = rotate(query, cos_gain, sin_gain).astype(
                 jnp.bfloat16
             )
@@ -346,6 +346,8 @@
                 job, c = chunks[slot]
                 mix((i - 2) % bufs, job, c, g, origins[slot], tops[i - 2], totals[i - 2])
 
+    if last:
+        before, slot = partial_place(heads, query_begin, query_end, earlier[0])
     if max(job[2] for job in jobs) == 1:
         sweep([(job, 0) for job in range(len(jobs))])
     else:
@@ -356,24 +358,26 @@
 
             lax.fori_loop(0, jobs[job][2], body, 0)
     if last:
-        slots, own_s, head_ref, _ = earlier
-        first_page = (slots, own_s, kv_refs[0], head_ref, outs[1], *page)
-        finish = partial_page(heads, query_begin, query_end, *first_page)
+        _, own_s, head_ref, _ = earlier
+        finish = partial_page(heads, before, slot, own_s, kv_refs[0], head_ref, outs[1], *page)
         for origin in range(heads):
             for g in range(kvl):
                 out_part(origin, g).wait()
         finish()
 
 
-def partial_page(heads, begins, ends, slots, own_s, rest_s, head_ref, pool_ref, page, sem):
-    x = lax.axis_index("head")
-    tok = lax.axis_index("tok")
-    core = lax.rem(tok, 2)
-    base = tok * heads * D
+def partial_place(heads, begins, ends, slots):
+    base = lax.axis_index("tok") * heads * D
     here = (begins <= base) & (base < ends)
     first = jnp.max(jnp.where(here, begins.astype(jnp.float32), 0.0)).astype(jnp.int32)
     before = lax.rem(base - first, PAGE)
     slot = jnp.max(slots[:, :1].astype(jnp.float32)).astype(jnp.int32)
+    return before, slot
+
+
+def partial_page(heads, before, slot, own_s, rest_s, head_ref, pool_ref, page, sem):
+    x = lax.axis_index("head")
+    core = lax.rem(lax.axis_index("tok"), 2)
     kvl = head_ref.shape[1]
     d = lax.rem(x + 1, heads)
     lane = lax.broadcasted_iota(jnp.int32, (PAGE, PAGE), 1)

time: 35.2 us -> 34.7 us (0.986)
  Pallas kernels: 16.1 us -> 15.5 us
    pallas_call x1, Pallas kernels: 2.83 us -> 2.31 us  [kv_prep(): pl.pallas_call(functools.partial(kv_prep_body, heads, lengths.shape[0]),...]
where the time goes in v5:
time: 34.7 us; the launch traced here: 34.3 us
  Pallas kernels  15.5 us (45%)
  starting transfers between devices  12.5 us (36%)
  local copies, waits for them, and re-layouts  3.1 us (9%)
  waiting for transfers between devices  2.49 us (7%)
  between operations  0.75 us (2%)
    pallas_call x4, Pallas kernels, attend(): pl.pallas_call(functools.partial(attend_body, heads, segs, tuple(plan), l...  10.3 us
    ppermute x3, starting transfers between devices, swap(): return lax.ppermute(x, 'tok', [(i, i ^ bit) for i in range(peers)])  5.81 us
    ppermute x1, starting transfers between devices, onward(): return lax.ppermute(x, axis, [(i, i + by) for i in range(peers - by)])  3.77 us
    unnamed x8, local copies, waits for them, and re-layouts  3.1 us
    ppermute x4, starting transfers between devices, around(): return lax.ppermute(x, axis, [(i, (i + by) % peers) for i in range(peers)])  2.9 us
    ppermute x4, waiting for transfers between devices, around(): return lax.ppermute(x, axis, [(i, (i + by) % peers) for i in range(peers)])  2.48 us
    pallas_call x1, Pallas kernels, kv_prep(): pl.pallas_call(functools.partial(kv_prep_body, heads, lengths.shape[0]),...  2.31 us
    pallas_call x1, Pallas kernels, pages(): pl.pallas_call(functools.partial(pages_body, heads, segs, pool), out_shap...  2.02 us
  transfers between devices with their start and end apart: 8, of which 2 were waited for; matrix products, arithmetic and copies ran while one was open for 0% of the time, Pallas kernels for 29%

profile of v5, /device:TPU:5, one launch (start us, length us, event | category | flops | bytes accessed | tf_op | source)
XLA Modules:
  0.0 34.3 jit_solution(5508668525140411492)
XLA Ops:
  0.6 2.3 %kv_prep.1 = (f32[184,128]{1,0:T(8,128)}, bf16[128,1024]{1,0:T(8,128)(2,1)}, bf16[128,1024]{1,0:T(8,128)(2,1)}) custom-call(s32[8]{0:T(128)} %lengths_in.1, bf16[128,1024]{1,0:T(8,128)(2,1)} %k_in.1, bf16[128,1024]{1,0:T(8,128)(2,1)} %v_in.1, f32[1,128]{1,0:T(1,128)} %bitcast.2, f32[1,128]{1,0:T(1,128)} %bitcast.3), custom_call_target="tpu_custom_call" | custom-call | flops 11500000 | tf_op jit(solution)/shard_map/kv_prep/pallas_call | solution.py:150
  3.0 1.3 %collective-permute-start.1 = (bf16[128,1024]{1,0:T(8,128)(2,1)}, bf16[128,1024]{1,0:T(8,128)(2,1)S(1)}, u32[]{:S(2)}, u32[]{:S(2)}) collective-permute-start(bf16[128,1024]{1,0:T(8,128)(2,1)} %get-tuple-element.29), channel_id=1, source_target_pairs={{0,1},{1,0},{2,3},{3,2},{4,5},{5,4},{6,7},{7,6},{8,9},{9,8},{10,11... | collective-permute-start | bytes 786440 | tf_op jit(solution)/shard_map/ppermute | solution.py:35
  4.2 1.3 %collective-permute-start.4 = (bf16[128,1024]{1,0:T(8,128)(2,1)}, bf16[128,1024]{1,0:T(8,128)(2,1)S(1)}, u32[]{:S(2)}, u32[]{:S(2)}) collective-permute-start(bf16[128,1024]{1,0:T(8,128)(2,1)} %get-tuple-element.26.own_ref.refs_1_.refs_0_.refs_2_), channel_id=1, source_target_pairs={{0,8},{2,10},{4,12},{6,14},{8,16},{10,18},{12,20},{14,22},{16,24},... | collective-permute-start | bytes 786440 | tf_op jit(solution)/shard_map/ppermute | solution.py:35
  5.5 0.0 copy-start
  5.5 1.0 %copy-done = bf16[128,1024]{1,0:T(8,128)(2,1)S(1)} copy-done((bf16[128,1024]{1,0:T(8,128)(2,1)S(1)}, bf16[128,1024]{1,0:T(8,128)(2,1)}, u32[]{:S(2)}) %copy-start) | copy-done | bytes 262168
  6.5 0.0 copy-start.1
  6.5 0.9 %copy-done.1 = f32[184,128]{1,0:T(8,128)S(1)} copy-done((f32[184,128]{1,0:T(8,128)S(1)}, f32[184,128]{1,0:T(8,128)}, u32[]{:S(2)}) %copy-start.1) | copy-done | bytes 94232
  7.4 0.0 copy-start.2
  7.4 1.2 %copy-done.2 = bf16[128,4096]{1,0:T(8,128)(2,1)S(1)} copy-done((bf16[128,4096]{1,0:T(8,128)(2,1)S(1)}, bf16[128,4096]{1,0:T(8,128)(2,1)}, u32[]{:S(2)}) %copy-start.2) | copy-done | bytes 1048600
  8.6 0.7 %q_prep.1 = (bf16[2048,128]{1,0:T(8,128)(2,1)S(1)}, bf16[2048,128]{1,0:T(8,128)(2,1)S(1)}, f32[8,128]{1,0:T(8,128)S(1)}) custom-call(bf16[128,4096]{1,0:T(8,128)(2,1)S(1)} %copy-done.2, f32[184,128]{1,0:T(8,128)S(1)} %copy-done.1, bf16[128,1024]{1,0:T(8,128)(2,1)S(1)} %copy-done), custom_call_target="tpu_custom_call" | custom-call | flops 11500000 | tf_op jit(solution)/shard_map/q_prep/pallas_call | solution.py:189
  9.3 0.3 collective-permute-start
  9.7 0.7 %collective-permute-done.1.refs_0_ = bf16[128,1024]{1,0:T(8,128)(2,1)S(1)} collective-permute-done((bf16[128,1024]{1,0:T(8,128)(2,1)}, bf16[128,1024]{1,0:T(8,128)(2,1)S(1)}, u32[]{:S(2)}, u32[]{:S(2)}) %collective-permute-start.1) | collective-permute-done | bytes 262176 | tf_op jit(solution)/shard_map/ppermute | solution.py:35
  10.4 1.1 %attend_part.3 = (f32[1,4,1,512]{3,2,1,0:T(1,128)S(1)}, f32[1,4,1,512]{3,2,1,0:T(1,128)S(1)}, f32[1,4,128,512]{3,2,1,0:T(8,128)S(1)}) custom-call(f32[184,128]{1,0:T(8,128)S(1)} %copy-done.1, bf16[2048,128]{1,0:T(8,128)(2,1)S(1)} %get-tuple-element.27.refs_0_, bf16[128,1024]{1,0:T(8,128)(2,1)S(1)} %copy-done, ...), custom_call_target="tpu_custom_call" | custom-call | flops 11500000 | tf_op jit(solution)/shard_map/attend_part/pallas_call | solution.py:443
  11.5 1.7 %collective-permute-done.4.refs_0_ = bf16[128,1024]{1,0:T(8,128)(2,1)S(1)} collective-permute-done((bf16[128,1024]{1,0:T(8,128)(2,1)}, bf16[128,1024]{1,0:T(8,128)(2,1)S(1)}, u32[]{:S(2)}, u32[]{:S(2)}) %collective-permute-start.4) | collective-permute-done | bytes 262176 | tf_op jit(solution)/shard_map/ppermute | solution.py:35
  13.2 0.3 collective-permute-start.5
  13.5 0.0 collective-permute-start.2
  13.5 3.8 %collective-permute-start.3 = (bf16[128,1024]{1,0:T(8,128)(2,1)S(1)}, bf16[128,1024]{1,0:T(8,128)(2,1)S(1)}, u32[]{:S(2)}, u32[]{:S(2)}) collective-permute-start(bf16[128,1024]{1,0:T(8,128)(2,1)S(1)} %after.2.refs_2_.rest_ref.refs_3_.refs_0_), channel_id=1, source_target_pairs={{0,4},{2,6},{4,8},{6,10},{8,12},{10,14},{12,16},{14,18},{16,20},{1... | collective-permute-start | bytes 786440 | tf_op jit(solution)/shard_map/ppermute | solution.py:40
  17.3 0.0 copy-done.3
  17.3 2.0 %pages.1 = (bf16[24,16,4,256]{3,2,1,0:T(4,128)(2,1)}, bf16[16,4,256]{2,1,0:T(4,128)(2,1)S(1)}) custom-call(f32[184,128]{1,0:T(8,128)S(1)} %copy-done.1, s32[1,24]{1,0:T(1,128)S(1)} %copy-done.3, bf16[128,1024]{1,0:T(8,128)(2,1)S(1)} %copy-done, bf16[128,1024]{1,0:T(8,128)(2,1)S(1)} %after.2.refs_2_.rest_ref.refs_3_.refs_0_), custom_call_target="tpu_custom_call" | custom-call | flops 11500000 | tf_op jit(solution)/shard_map/pages/pallas_call | solution.py:549
  19.4 0.0 collective-permute-done.5.refs_2_.refs_5_
  19.4 0.1 pick.4.refs_9_
  19.4 5.0 %collective-permute-start.7 = (bf16[256,1024]{1,0:T(8,128)(2,1)S(1)}, bf16[256,1024]{1,0:T(8,128)(2,1)S(1)}, u32[]{:S(2)}, u32[]{:S(2)}) collective-permute-start(bf16[256,1024]{1,0:T(8,128)(2,1)S(1)} %pick.4.refs_9_), channel_id=1, source_target_pairs={{0,2},{2,0},{4,6},{6,4},{8,10},{10,8},{12,14},{14,12},{16,18},{18,... | collective-permute-start | bytes 1572872 | tf_op jit(solution)/shard_map/ppermute | solution.py:45
  24.5 0.0 collective-permute-done.refs_1_
  24.5 2.7 %attend_part.4 = (f32[1,4,1,512]{3,2,1,0:T(1,128)S(1)}, f32[1,4,1,512]{3,2,1,0:T(1,128)S(1)}, f32[1,4,128,512]{3,2,1,0:T(8,128)S(1)}, f32[1,4,1,512]{3,2,1,0:T(1...) custom-call(f32[184,128]{1,0:T(8,128)S(1)} %copy-done.1, ...), custom_call_target="tpu_custom_call" | custom-call | flops 11500000 | tf_op jit(solution)/shard_map/attend_part/pallas_call | solution.py:443
  27.2 0.0 collective-permute-done.2.refs_1_.refs_2_
  27.2 0.0 collective-permute-done.3.refs_2_.refs_3_
  27.2 0.1 pick.5.refs_11_
  27.3 0.5 %collective-permute-start.6 = (bf16[256,1024]{1,0:T(8,128)(2,1)S(1)}, bf16[256,1024]{1,0:T(8,128)(2,1)S(1)}, u32[]{:S(2)}, u32[]{:S(2)}) collective-permute-start(bf16[256,1024]{1,0:T(8,128)(2,1)S(1)} %pick.5.refs_11_), channel_id=1, source_target_pairs={{0,2},{2,0},{4,6},{6,4},{8,10},{10,8},{12,14},{14,12},{16,18},{18,... | collective-permute-start | bytes 1572872 | tf_op jit(solution)/shard_map/ppermute | solution.py:45
  27.8 0.0 collective-permute-done.7.refs_4_.refs_10_
  27.8 3.4 %attend_part.5 = (f32[1,4,1,512]{3,2,1,0:T(1,128)S(1)}, f32[1,4,1,512]{3,2,1,0:T(1,128)S(1)}, f32[1,4,128,512]{3,2,1,0:T(8,128)S(1)}, f32[1,4,1,512]{3,2,1,0:T(1...) custom-call(f32[184,128]{1,0:T(8,128)S(1)} %copy-done.1, ...), custom_call_target="tpu_custom_call" | custom-call | flops 11500000 | tf_op jit(solution)/shard_map/attend_part/pallas_call | solution.py:443
  31.2 0.0 collective-permute-done.6.refs_2_
  31.2 3.1 %attend_last.1 = (bf16[256,2048]{1,0:T(8,128)(2,1)}, bf16[24,16,4,256]{3,2,1,0:T(4,128)(2,1)}) custom-call(f32[184,128]{1,0:T(8,128)S(1)} %copy-done.1, bf16[2048,128]{1,0:T(8,128)(2,1)S(1)} %get-tuple-element.27.refs_0_, bf16[2048,128]{1,0:T(8,128)(2,1)S(1)} %collective-permute-done.refs_1_, ...), custom_call_target="tpu_custom_call", output_to_operand_aliasing={{1}: (13, {})} | custom-call | flops 11500000 | tf_op jit(solution)/shard_map/attend_last/pallas_call | solution.py:443
  (4 shorter events, 0.0 us)
Async XLA Ops:
  3.0 7.5 %collective-permute-start.1 = (bf16[128,1024]{1,0:T(8,128)(2,1)}, bf16[128,1024]{1,0:T(8,128)(2,1)S(1)}, u32[]{:S(2)}, u32[]{:S(2)}) collective-permute-start(bf16[128,1024]{1,0:T(8,128)(2,1)} %get-tuple-element.29), channel_id=1, source_target_pairs={{0,1},{1,0},{2,3},{3,2},{4,5},{5,4},{6,7},{7,6},{8,9},{9,8},{10,11... | collective-permute-start | bytes 786440 | tf_op jit(solution)/shard_map/ppermute | solution.py:35
  4.2 9.0 %collective-permute-start.4 = (bf16[128,1024]{1,0:T(8,128)(2,1)}, bf16[128,1024]{1,0:T(8,128)(2,1)S(1)}, u32[]{:S(2)}, u32[]{:S(2)}) collective-permute-start(bf16[128,1024]{1,0:T(8,128)(2,1)} %get-tuple-element.26.own_ref.refs_1_.refs_0_.refs_2_), channel_id=1, source_target_pairs={{0,8},{2,10},{4,12},{6,14},{8,16},{10,18},{12,20},{14,22},{16,24},... | collective-permute-start | bytes 786440 | tf_op jit(solution)/shard_map/ppermute | solution.py:35
  5.5 1.0 %copy-start = (bf16[128,1024]{1,0:T(8,128)(2,1)S(1)}, bf16[128,1024]{1,0:T(8,128)(2,1)}, u32[]{:S(2)}) copy-start(bf16[128,1024]{1,0:T(8,128)(2,1)} %get-tuple-element.26.own_ref.refs_1_.refs_0_.refs_2_) | copy-start | bytes 786436
  6.5 0.9 %copy-start.1 = (f32[184,128]{1,0:T(8,128)S(1)}, f32[184,128]{1,0:T(8,128)}, u32[]{:S(2)}) copy-start(f32[184,128]{1,0:T(8,128)} %get-tuple-element.25.table_ref.table) | copy-start | bytes 282628
  7.4 1.2 %copy-start.2 = (bf16[128,4096]{1,0:T(8,128)(2,1)S(1)}, bf16[128,4096]{1,0:T(8,128)(2,1)}, u32[]{:S(2)}) copy-start(bf16[128,4096]{1,0:T(8,128)(2,1)} %q_ref.1) | copy-start | bytes 3145732
  9.3 15.1 %collective-permute-start = (bf16[2048,128]{1,0:T(8,128)(2,1)S(1)}, bf16[2048,128]{1,0:T(8,128)(2,1)S(1)}, u32[]{:S(2)}, u32[]{:S(2)}) collective-permute-start(bf16[2048,128]{1,0:T(8,128)(2,1)S(1)} %get-tuple-element.28), channel_id=1, source_target_pairs={{0,1},{1,0},{2,3},{3,2},{4,5},{5,4},{6,7},{7,6},{8,9},{9,8},{10,11... | collective-permute-start | bytes 1572872 | tf_op jit(solution)/shard_map/ppermute | solution.py:35
  13.2 4.1 %copy-start.3 = (s32[1,24]{1,0:T(1,128)S(1)}, s32[1,24]{1,0:T(1,128)}, u32[]{:S(2)}) copy-start(s32[1,24]{1,0:T(1,128)} %refs_9_.1) | copy-start | bytes 292
  13.2 6.1 %collective-permute-start.5 = (bf16[128,1024]{1,0:T(8,128)(2,1)S(1)}, bf16[128,1024]{1,0:T(8,128)(2,1)S(1)}, u32[]{:S(2)}, u32[]{:S(2)}) collective-permute-start(bf16[128,1024]{1,0:T(8,128)(2,1)S(1)} %pick.3), channel_id=1, source_target_pairs={{0,4},{2,6},{4,0},{6,2},{8,12},{10,14},{12,8},{14,10},{16,20},{18,... | collective-permute-start | bytes 786440 | tf_op jit(solution)/shard_map/ppermute | solution.py:45
  13.5 13.7 %collective-permute-start.2 = (bf16[128,1024]{1,0:T(8,128)(2,1)S(1)}, bf16[128,1024]{1,0:T(8,128)(2,1)S(1)}, u32[]{:S(2)}, u32[]{:S(2)}) collective-permute-start(bf16[128,1024]{1,0:T(8,128)(2,1)S(1)} %after.2.refs_2_.rest_ref.refs_3_.refs_0_), channel_id=1, source_target_pairs={{0,8},{2,10},{4,12},{6,14},{8,16},{10,18},{12,20},{14,22},{16,24},... | collective-permute-start | bytes 786440 | tf_op jit(solution)/shard_map/ppermute | solution.py:35
  13.5 13.7 %collective-permute-start.3 = (bf16[128,1024]{1,0:T(8,128)(2,1)S(1)}, bf16[128,1024]{1,0:T(8,128)(2,1)S(1)}, u32[]{:S(2)}, u32[]{:S(2)}) collective-permute-start(bf16[128,1024]{1,0:T(8,128)(2,1)S(1)} %after.2.refs_2_.rest_ref.refs_3_.refs_0_), channel_id=1, source_target_pairs={{0,4},{2,6},{4,8},{6,10},{8,12},{10,14},{12,16},{14,18},{16,20},{1... | collective-permute-start | bytes 786440 | tf_op jit(solution)/shard_map/ppermute | solution.py:40
  19.4 8.3 %collective-permute-start.7 = (bf16[256,1024]{1,0:T(8,128)(2,1)S(1)}, bf16[256,1024]{1,0:T(8,128)(2,1)S(1)}, u32[]{:S(2)}, u32[]{:S(2)}) collective-permute-start(bf16[256,1024]{1,0:T(8,128)(2,1)S(1)} %pick.4.refs_9_), channel_id=1, source_target_pairs={{0,2},{2,0},{4,6},{6,4},{8,10},{10,8},{12,14},{14,12},{16,18},{18,... | collective-permute-start | bytes 1572872 | tf_op jit(solution)/shard_map/ppermute | solution.py:45
  27.3 3.9 %collective-permute-start.6 = (bf16[256,1024]{1,0:T(8,128)(2,1)S(1)}, bf16[256,1024]{1,0:T(8,128)(2,1)S(1)}, u32[]{:S(2)}, u32[]{:S(2)}) collective-permute-start(bf16[256,1024]{1,0:T(8,128)(2,1)S(1)} %pick.5.refs_11_), channel_id=1, source_target_pairs={{0,2},{2,0},{4,6},{6,4},{8,10},{10,8},{12,14},{14,12},{16,18},{18,... | collective-permute-start | bytes 1572872 | tf_op jit(solution)/shard_map/ppermute | solution.py:45

commit v6 on v5

--- a/solution.py
+++ b/solution.py
@@ -631,10 +631,10 @@
     base = [(0, 0, "own", 0)] + [(1, d - 1, "own", d) for d in others]
     [own_state] = attend(table, [q_own], [own, rest], [(0, 0, None, base)], False, heads, segs)
 
-    own4 = after(own4, own_state[0])
+    own4 = after(own4, rest)
     own2 = swap(pick(2, ((0, 1),), own, own4), 2)
     page_pool, head_page = pages(table, slot_order, own, rest, heads, segs)
-    own_mixed = pick(1, ((0, 1), (2,)), own, own4, own2, head_page)
+    own_mixed = pick(1, ((0, 1), (2,)), own, own4, own2, head_page, own_state[0])
     own_s = swap(own_mixed, 1)
 
     qs = [q_own, q_rest]

time: 34.7 us -> 34.5 us (level)
  starting transfers between devices: 12.5 us -> 11.4 us
  waiting for transfers between devices: 2.49 us -> 3.58 us
    ppermute x4, waiting for transfers between devices: 2.48 us -> 3.57 us  [around(): return lax.ppermute(x, axis, [(i, (i + by) % peers) for i in range(peers)])]
    ppermute x3, starting transfers between devices: 5.81 us -> 4.96 us  [swap(): return lax.ppermute(x, 'tok', [(i, i ^ bit) for i in range(peers)])]
where the time goes in v6:
time: 34.5 us; the launch traced here: 34.3 us
  Pallas kernels  15.5 us (45%)
  starting transfers between devices  11.4 us (33%)
  waiting for transfers between devices  3.58 us (10%)
  local copies, waits for them, and re-layouts  3.1 us (9%)
  between operations  0.76 us (2%)
    pallas_call x4, Pallas kernels, attend(): pl.pallas_call(functools.partial(attend_body, heads, segs, tuple(plan), l...  10.3 us
    ppermute x3, starting transfers between devices, swap(): return lax.ppermute(x, 'tok', [(i, i ^ bit) for i in range(peers)])  4.96 us
    ppermute x4, waiting for transfers between devices, around(): return lax.ppermute(x, axis, [(i, (i + by) % peers) for i in range(peers)])  3.57 us
    ppermute x1, starting transfers between devices, onward(): return lax.ppermute(x, axis, [(i, i + by) for i in range(peers - by)])  3.51 us
    unnamed x8, local copies, waits for them, and re-layouts  3.1 us
    ppermute x4, starting transfers between devices, around(): return lax.ppermute(x, axis, [(i, (i + by) % peers) for i in range(peers)])  2.9 us
    pallas_call x1, Pallas kernels, kv_prep(): pl.pallas_call(functools.partial(kv_prep_body, heads, lengths.shape[0]),...  2.31 us
    pallas_call x1, Pallas kernels, pages(): pl.pallas_call(functools.partial(pages_body, heads, segs, pool), out_shap...  2.02 us
  transfers between devices with their start and end apart: 8, of which 2 were waited for; matrix products, arithmetic and copies ran while one was open for 0% of the time, Pallas kernels for 29%

profile of v6, /device:TPU:5, one launch (start us, length us, event | category | flops | bytes accessed | tf_op | source)
XLA Modules:
  0.0 34.3 jit_solution(987642282625045881)
XLA Ops:
  0.6 2.3 %kv_prep.1 = (f32[184,128]{1,0:T(8,128)}, bf16[128,1024]{1,0:T(8,128)(2,1)}, bf16[128,1024]{1,0:T(8,128)(2,1)}) custom-call(s32[8]{0:T(128)} %lengths_in.1, bf16[128,1024]{1,0:T(8,128)(2,1)} %k_in.1, bf16[128,1024]{1,0:T(8,128)(2,1)} %v_in.1, f32[1,128]{1,0:T(1,128)} %bitcast.2, f32[1,128]{1,0:T(1,128)} %bitcast.3), custom_call_target="tpu_custom_call" | custom-call | flops 11500000 | tf_op jit(solution)/shard_map/kv_prep/pallas_call | solution.py:150
  3.0 1.3 %collective-permute-start.1 = (bf16[128,1024]{1,0:T(8,128)(2,1)}, bf16[128,1024]{1,0:T(8,128)(2,1)S(1)}, u32[]{:S(2)}, u32[]{:S(2)}) collective-permute-start(bf16[128,1024]{1,0:T(8,128)(2,1)} %get-tuple-element.29), channel_id=1, source_target_pairs={{0,1},{1,0},{2,3},{3,2},{4,5},{5,4},{6,7},{7,6},{8,9},{9,8},{10,11... | collective-permute-start | bytes 786440 | tf_op jit(solution)/shard_map/ppermute | solution.py:35
  4.2 1.3 %collective-permute-start.4 = (bf16[128,1024]{1,0:T(8,128)(2,1)}, bf16[128,1024]{1,0:T(8,128)(2,1)S(1)}, u32[]{:S(2)}, u32[]{:S(2)}) collective-permute-start(bf16[128,1024]{1,0:T(8,128)(2,1)} %get-tuple-element.26.own_ref.refs_0_.refs_1_.refs_2_), channel_id=1, source_target_pairs={{0,8},{2,10},{4,12},{6,14},{8,16},{10,18},{12,20},{14,22},{16,24},... | collective-permute-start | bytes 786440 | tf_op jit(solution)/shard_map/ppermute | solution.py:35
  5.5 0.0 copy-start
  5.5 1.0 %copy-done = bf16[128,1024]{1,0:T(8,128)(2,1)S(1)} copy-done((bf16[128,1024]{1,0:T(8,128)(2,1)S(1)}, bf16[128,1024]{1,0:T(8,128)(2,1)}, u32[]{:S(2)}) %copy-start) | copy-done | bytes 262168
  6.5 0.0 copy-start.1
  6.5 0.9 %copy-done.1 = f32[184,128]{1,0:T(8,128)S(1)} copy-done((f32[184,128]{1,0:T(8,128)S(1)}, f32[184,128]{1,0:T(8,128)}, u32[]{:S(2)}) %copy-start.1) | copy-done | bytes 94232
  7.4 1.2 %copy-done.2 = bf16[128,4096]{1,0:T(8,128)(2,1)S(1)} copy-done((bf16[128,4096]{1,0:T(8,128)(2,1)S(1)}, bf16[128,4096]{1,0:T(8,128)(2,1)}, u32[]{:S(2)}) %copy-start.2) | copy-done | bytes 1048600
  8.6 0.7 %q_prep.1 = (bf16[2048,128]{1,0:T(8,128)(2,1)S(1)}, bf16[2048,128]{1,0:T(8,128)(2,1)S(1)}, f32[8,128]{1,0:T(8,128)S(1)}) custom-call(bf16[128,4096]{1,0:T(8,128)(2,1)S(1)} %copy-done.2, f32[184,128]{1,0:T(8,128)S(1)} %copy-done.1, bf16[128,1024]{1,0:T(8,128)(2,1)S(1)} %copy-done), custom_call_target="tpu_custom_call" | custom-call | flops 11500000 | tf_op jit(solution)/shard_map/q_prep/pallas_call | solution.py:189
  9.3 0.3 collective-permute-start
  9.7 0.7 %collective-permute-done.1.refs_0_ = bf16[128,1024]{1,0:T(8,128)(2,1)S(1)} collective-permute-done((bf16[128,1024]{1,0:T(8,128)(2,1)}, bf16[128,1024]{1,0:T(8,128)(2,1)S(1)}, u32[]{:S(2)}, u32[]{:S(2)}) %collective-permute-start.1) | collective-permute-done | bytes 262176 | tf_op jit(solution)/shard_map/ppermute | solution.py:35
  10.4 2.8 %collective-permute-done.4.refs_0_ = bf16[128,1024]{1,0:T(8,128)(2,1)S(1)} collective-permute-done((bf16[128,1024]{1,0:T(8,128)(2,1)}, bf16[128,1024]{1,0:T(8,128)(2,1)S(1)}, u32[]{:S(2)}, u32[]{:S(2)}) %collective-permute-start.4) | collective-permute-done | bytes 262176 | tf_op jit(solution)/shard_map/ppermute | solution.py:35
  13.2 0.3 collective-permute-start.5
  13.5 0.0 collective-permute-start.2
  13.5 3.5 %collective-permute-start.3 = (bf16[128,1024]{1,0:T(8,128)(2,1)S(1)}, bf16[128,1024]{1,0:T(8,128)(2,1)S(1)}, u32[]{:S(2)}, u32[]{:S(2)}) collective-permute-start(bf16[128,1024]{1,0:T(8,128)(2,1)S(1)} %after.2.refs_1_.refs_2_.rest_ref.refs_3_.refs_0_), channel_id=1, source_target_pairs={{0,4},{2,6},{4,8},{6,10},{8,12},{10,14},{12,16},{14,18},{16,20},{1... | collective-permute-start | bytes 786440 | tf_op jit(solution)/shard_map/ppermute | solution.py:40
  17.1 0.0 copy-start.3
  17.1 1.1 %attend_part.3 = (f32[1,4,1,512]{3,2,1,0:T(1,128)S(1)}, f32[1,4,1,512]{3,2,1,0:T(1,128)S(1)}, f32[1,4,128,512]{3,2,1,0:T(8,128)S(1)}) custom-call(f32[184,128]{1,0:T(8,128)S(1)} %copy-done.1, bf16[2048,128]{1,0:T(8,128)(2,1)S(1)} %get-tuple-element.27.refs_0_, bf16[128,1024]{1,0:T(8,128)(2,1)S(1)} %copy-done, ...), custom_call_target="tpu_custom_call" | custom-call | flops 11500000 | tf_op jit(solution)/shard_map/attend_part/pallas_call | solution.py:443
  18.2 0.0 copy-done.3
  18.2 2.0 %pages.1 = (bf16[24,16,4,256]{3,2,1,0:T(4,128)(2,1)}, bf16[16,4,256]{2,1,0:T(4,128)(2,1)S(1)}) custom-call(f32[184,128]{1,0:T(8,128)S(1)} %copy-done.1, s32[1,24]{1,0:T(1,128)S(1)} %copy-done.3, bf16[128,1024]{1,0:T(8,128)(2,1)S(1)} %copy-done, bf16[128,1024]{1,0:T(8,128)(2,1)S(1)} %after.2.refs_1_.refs_2_.rest_ref.refs_3_.refs_0_), custom_call_target="tpu_custom_call" | custom-call | flops 11500000 | tf_op jit(solution)/shard_map/pages/pallas_call | solution.py:549
  20.2 0.0 collective-permute-done.5.refs_2_.refs_5_
  20.2 0.1 pick.4.refs_9_
  20.3 4.2 %collective-permute-start.7 = (bf16[256,1024]{1,0:T(8,128)(2,1)S(1)}, bf16[256,1024]{1,0:T(8,128)(2,1)S(1)}, u32[]{:S(2)}, u32[]{:S(2)}) collective-permute-start(bf16[256,1024]{1,0:T(8,128)(2,1)S(1)} %pick.4.refs_9_), channel_id=1, source_target_pairs={{0,2},{2,0},{4,6},{6,4},{8,10},{10,8},{12,14},{14,12},{16,18},{18,... | collective-permute-start | bytes 1572872 | tf_op jit(solution)/shard_map/ppermute | solution.py:45
  24.5 0.0 collective-permute-done.refs_1_
  24.5 2.7 %attend_part.4 = (f32[1,4,1,512]{3,2,1,0:T(1,128)S(1)}, f32[1,4,1,512]{3,2,1,0:T(1,128)S(1)}, f32[1,4,128,512]{3,2,1,0:T(8,128)S(1)}, f32[1,4,1,512]{3,2,1,0:T(1...) custom-call(f32[184,128]{1,0:T(8,128)S(1)} %copy-done.1, ...), custom_call_target="tpu_custom_call" | custom-call | flops 11500000 | tf_op jit(solution)/shard_map/attend_part/pallas_call | solution.py:443
  27.2 0.0 collective-permute-done.2.refs_1_.refs_2_
  27.2 0.0 collective-permute-done.3.refs_2_.refs_3_
  27.2 0.1 pick.5.refs_11_
  27.3 0.5 %collective-permute-start.6 = (bf16[256,1024]{1,0:T(8,128)(2,1)S(1)}, bf16[256,1024]{1,0:T(8,128)(2,1)S(1)}, u32[]{:S(2)}, u32[]{:S(2)}) collective-permute-start(bf16[256,1024]{1,0:T(8,128)(2,1)S(1)} %pick.5.refs_11_), channel_id=1, source_target_pairs={{0,2},{2,0},{4,6},{6,4},{8,10},{10,8},{12,14},{14,12},{16,18},{18,... | collective-permute-start | bytes 1572872 | tf_op jit(solution)/shard_map/ppermute | solution.py:45
  27.8 0.0 collective-permute-done.7.refs_4_.refs_10_
  27.8 3.4 %attend_part.5 = (f32[1,4,1,512]{3,2,1,0:T(1,128)S(1)}, f32[1,4,1,512]{3,2,1,0:T(1,128)S(1)}, f32[1,4,128,512]{3,2,1,0:T(8,128)S(1)}, f32[1,4,1,512]{3,2,1,0:T(1...) custom-call(f32[184,128]{1,0:T(8,128)S(1)} %copy-done.1, ...), custom_call_target="tpu_custom_call" | custom-call | flops 11500000 | tf_op jit(solution)/shard_map/attend_part/pallas_call | solution.py:443
  31.2 0.0 collective-permute-done.6.refs_2_
  31.2 3.1 %attend_last.1 = (bf16[256,2048]{1,0:T(8,128)(2,1)}, bf16[24,16,4,256]{3,2,1,0:T(4,128)(2,1)}) custom-call(f32[184,128]{1,0:T(8,128)S(1)} %copy-done.1, bf16[2048,128]{1,0:T(8,128)(2,1)S(1)} %get-tuple-element.27.refs_0_, bf16[2048,128]{1,0:T(8,128)(2,1)S(1)} %collective-permute-done.refs_1_, ...), custom_call_target="tpu_custom_call", output_to_operand_aliasing={{1}: (13, {})} | custom-call | flops 11500000 | tf_op jit(solution)/shard_map/attend_last/pallas_call | solution.py:443
  (4 shorter events, 0.0 us)
Async XLA Ops:
  3.0 7.5 %collective-permute-start.1 = (bf16[128,1024]{1,0:T(8,128)(2,1)}, bf16[128,1024]{1,0:T(8,128)(2,1)S(1)}, u32[]{:S(2)}, u32[]{:S(2)}) collective-permute-start(bf16[128,1024]{1,0:T(8,128)(2,1)} %get-tuple-element.29), channel_id=1, source_target_pairs={{0,1},{1,0},{2,3},{3,2},{4,5},{5,4},{6,7},{7,6},{8,9},{9,8},{10,11... | collective-permute-start | bytes 786440 | tf_op jit(solution)/shard_map/ppermute | solution.py:35
  4.2 9.0 %collective-permute-start.4 = (bf16[128,1024]{1,0:T(8,128)(2,1)}, bf16[128,1024]{1,0:T(8,128)(2,1)S(1)}, u32[]{:S(2)}, u32[]{:S(2)}) collective-permute-start(bf16[128,1024]{1,0:T(8,128)(2,1)} %get-tuple-element.26.own_ref.refs_0_.refs_1_.refs_2_), channel_id=1, source_target_pairs={{0,8},{2,10},{4,12},{6,14},{8,16},{10,18},{12,20},{14,22},{16,24},... | collective-permute-start | bytes 786440 | tf_op jit(solution)/shard_map/ppermute | solution.py:35
  5.5 1.0 %copy-start = (bf16[128,1024]{1,0:T(8,128)(2,1)S(1)}, bf16[128,1024]{1,0:T(8,128)(2,1)}, u32[]{:S(2)}) copy-start(bf16[128,1024]{1,0:T(8,128)(2,1)} %get-tuple-element.26.own_ref.refs_0_.refs_1_.refs_2_) | copy-start | bytes 786436
  6.5 0.9 %copy-start.1 = (f32[184,128]{1,0:T(8,128)S(1)}, f32[184,128]{1,0:T(8,128)}, u32[]{:S(2)}) copy-start(f32[184,128]{1,0:T(8,128)} %get-tuple-element.25.table_ref.table) | copy-start | bytes 282628
  7.4 1.2 %copy-start.2 = (bf16[128,4096]{1,0:T(8,128)(2,1)S(1)}, bf16[128,4096]{1,0:T(8,128)(2,1)}, u32[]{:S(2)}) copy-start(bf16[128,4096]{1,0:T(8,128)(2,1)} %q_ref.1) | copy-start | bytes 3145732
  9.3 15.1 %collective-permute-start = (bf16[2048,128]{1,0:T(8,128)(2,1)S(1)}, bf16[2048,128]{1,0:T(8,128)(2,1)S(1)}, u32[]{:S(2)}, u32[]{:S(2)}) collective-permute-start(bf16[2048,128]{1,0:T(8,128)(2,1)S(1)} %get-tuple-element.28), channel_id=1, source_target_pairs={{0,1},{1,0},{2,3},{3,2},{4,5},{5,4},{6,7},{7,6},{8,9},{9,8},{10,11... | collective-permute-start | bytes 1572872 | tf_op jit(solution)/shard_map/ppermute | solution.py:35
  13.2 7.0 %collective-permute-start.5 = (bf16[128,1024]{1,0:T(8,128)(2,1)S(1)}, bf16[128,1024]{1,0:T(8,128)(2,1)S(1)}, u32[]{:S(2)}, u32[]{:S(2)}) collective-permute-start(bf16[128,1024]{1,0:T(8,128)(2,1)S(1)} %pick.3), channel_id=1, source_target_pairs={{0,4},{2,6},{4,0},{6,2},{8,12},{10,14},{12,8},{14,10},{16,20},{18,... | collective-permute-start | bytes 786440 | tf_op jit(solution)/shard_map/ppermute | solution.py:45
  13.5 13.7 %collective-permute-start.2 = (bf16[128,1024]{1,0:T(8,128)(2,1)S(1)}, bf16[128,1024]{1,0:T(8,128)(2,1)S(1)}, u32[]{:S(2)}, u32[]{:S(2)}) collective-permute-start(bf16[128,1024]{1,0:T(8,128)(2,1)S(1)} %after.2.refs_1_.refs_2_.rest_ref.refs_3_.refs_0_), channel_id=1, source_target_pairs={{0,8},{2,10},{4,12},{6,14},{8,16},{10,18},{12,20},{14,22},{16,24},... | collective-permute-start | bytes 786440 | tf_op jit(solution)/shard_map/ppermute | solution.py:35
  13.5 13.7 %collective-permute-start.3 = (bf16[128,1024]{1,0:T(8,128)(2,1)S(1)}, bf16[128,1024]{1,0:T(8,128)(2,1)S(1)}, u32[]{:S(2)}, u32[]{:S(2)}) collective-permute-start(bf16[128,1024]{1,0:T(8,128)(2,1)S(1)} %after.2.refs_1_.refs_2_.rest_ref.refs_3_.refs_0_), channel_id=1, source_target_pairs={{0,4},{2,6},{4,8},{6,10},{8,12},{10,14},{12,16},{14,18},{16,20},{1... | collective-permute-start | bytes 786440 | tf_op jit(solution)/shard_map/ppermute | solution.py:40
  17.1 1.1 %copy-start.3 = (s32[1,24]{1,0:T(1,128)S(1)}, s32[1,24]{1,0:T(1,128)}, u32[]{:S(2)}) copy-start(s32[1,24]{1,0:T(1,128)} %refs_9_.1) | copy-start | bytes 292
  20.3 7.5 %collective-permute-start.7 = (bf16[256,1024]{1,0:T(8,128)(2,1)S(1)}, bf16[256,1024]{1,0:T(8,128)(2,1)S(1)}, u32[]{:S(2)}, u32[]{:S(2)}) collective-permute-start(bf16[256,1024]{1,0:T(8,128)(2,1)S(1)} %pick.4.refs_9_), channel_id=1, source_target_pairs={{0,2},{2,0},{4,6},{6,4},{8,10},{10,8},{12,14},{14,12},{16,18},{18,... | collective-permute-start | bytes 1572872 | tf_op jit(solution)/shard_map/ppermute | solution.py:45
  27.3 3.9 %collective-permute-start.6 = (bf16[256,1024]{1,0:T(8,128)(2,1)S(1)}, bf16[256,1024]{1,0:T(8,128)(2,1)S(1)}, u32[]{:S(2)}, u32[]{:S(2)}) collective-permute-start(bf16[256,1024]{1,0:T(8,128)(2,1)S(1)} %pick.5.refs_11_), channel_id=1, source_target_pairs={{0,2},{2,0},{4,6},{6,4},{8,10},{10,8},{12,14},{14,12},{16,18},{18,... | collective-permute-start | bytes 1572872 | tf_op jit(solution)/shard_map/ppermute | solution.py:45

commit v7 on v6

--- a/solution.py
+++ b/solution.py
@@ -98,8 +98,9 @@
     return starts
 
 
-def kv_prep_body(heads, segs, lengths_in, k_in, v_in, gain_in, q_gain_in, table_ref, *refs):
-    outs, (lengths, k_ref, v_ref, gain_ref, q_gain_ref, sems) = refs[:heads], refs[heads:]
+def kv_prep_body(heads, segs, lengths_in, k_in, v_in, gain_in, q_gain_in, table_out, *refs):
+    results, refs = refs[:heads], refs[heads:]
+    lengths, k_ref, v_ref, gain_ref, q_gain_ref, sems, table_ref, *outs, out_sems = refs
     pairs = [(lengths_in, lengths), (gain_in, gain_ref), (k_in, k_ref), (v_in, v_ref)]
     pairs += [(q_gain_in, q_gain_ref)]
     copies = [pltpu.make_async_copy(a, b, sems.at[i]) for i, (a, b) in enumerate(pairs)]
@@ -128,6 +129,8 @@
     table_ref[along_end:gain_at] = end.astype(jnp.float32)
     copies[4].wait()
     table_ref[gain_at:stop] = jnp.broadcast_to(q_gain_ref[...], (8, D))
+    sends = [pltpu.make_async_copy(table_ref, table_out, out_sems.at[heads])]
+    sends[0].start()
     copies[1].wait()
     cos_gain, sin_gain = gain_tables(cosine, sine, gain_ref[...])
     copies[2].wait()
@@ -141,6 +144,10 @@
             outs[d][:, 2 * j * D : (2 * j + 1) * D] = key.T
             value = v_ref[:, at(head * D)]
             outs[d][:, (2 * j + 1) * D : (2 * j + 2) * D] = value.T
+        sends.append(pltpu.make_async_copy(outs[d], results[d], out_sems.at[d]))
+        sends[-1].start()
+    for send in sends:
+        send.wait()
 
 
 def kv_prep(lengths, keys, values, gain, q_gain, heads):
@@ -151,7 +158,7 @@
         functools.partial(kv_prep_body, heads, lengths.shape[0]),
         out_shape=[table] + [part] * heads,
         in_specs=[HBM] * 5,
-        out_specs=[VMEM] * (1 + heads),
+        out_specs=[HBM] * (1 + heads),
         scratch_shapes=[
             pltpu.SMEM(lengths.shape, jnp.int32),
             pltpu.VMEM(keys.shape, jnp.bfloat16),
@@ -159,6 +166,9 @@
             pltpu.VMEM(gain.shape, jnp.float32),
             pltpu.VMEM(gain.shape, jnp.float32),
             pltpu.SemaphoreType.DMA((5,)),
+            pltpu.VMEM(table.shape, jnp.float32),
+            *[pltpu.VMEM(part.shape, jnp.bfloat16)] * heads,
+            pltpu.SemaphoreType.DMA((heads + 1,)),
         ],
         compiler_params=params(62),
         cost_estimate=cost(0.01),

time: 34.5 us -> 34.5 us (level)
  no operation moved by 1% of the time
where the time goes in v7:
time: 34.5 us; the launch traced here: 34.2 us
  Pallas kernels  15.4 us (45%)
  starting transfers between devices  11.4 us (33%)
  waiting for transfers between devices  3.58 us (10%)
  local copies, waits for them, and re-layouts  3.1 us (9%)
  between operations  0.76 us (2%)
    pallas_call x4, Pallas kernels, attend(): pl.pallas_call(functools.partial(attend_body, heads, segs, tuple(plan), l...  10.3 us
    ppermute x3, starting transfers between devices, swap(): return lax.ppermute(x, 'tok', [(i, i ^ bit) for i in range(peers)])  4.95 us
    ppermute x4, waiting for transfers between devices, around(): return lax.ppermute(x, axis, [(i, (i + by) % peers) for i in range(peers)])  3.57 us
    ppermute x1, starting transfers between devices, onward(): return lax.ppermute(x, axis, [(i, i + by) for i in range(peers - by)])  3.51 us
    unnamed x8, local copies, waits for them, and re-layouts  3.1 us
    ppermute x4, starting transfers between devices, around(): return lax.ppermute(x, axis, [(i, (i + by) % peers) for i in range(peers)])  2.9 us
    pallas_call x1, Pallas kernels, kv_prep(): pl.pallas_call(functools.partial(kv_prep_body, heads, lengths.shape[0]),...  2.25 us
    pallas_call x1, Pallas kernels, pages(): pl.pallas_call(functools.partial(pages_body, heads, segs, pool), out_shap...  2.02 us
  transfers between devices with their start and end apart: 8, of which 2 were waited for; matrix products, arithmetic and copies ran while one was open for 0% of the time, Pallas kernels for 29%

profile of v7, /device:TPU:5, one launch (start us, length us, event | category | flops | bytes accessed | tf_op | source)
XLA Modules:
  0.0 34.2 jit_solution(7298585640241308739)
XLA Ops:
  0.6 2.3 %kv_prep.1 = (f32[184,128]{1,0:T(8,128)}, bf16[128,1024]{1,0:T(8,128)(2,1)}, bf16[128,1024]{1,0:T(8,128)(2,1)}) custom-call(s32[8]{0:T(128)} %lengths_in.1, bf16[128,1024]{1,0:T(8,128)(2,1)} %k_in.1, bf16[128,1024]{1,0:T(8,128)(2,1)} %v_in.1, f32[1,128]{1,0:T(1,128)} %bitcast.2, f32[1,128]{1,0:T(1,128)} %bitcast.3), custom_call_target="tpu_custom_call" | custom-call | flops 11500000 | tf_op jit(solution)/shard_map/kv_prep/pallas_call | solution.py:157
  2.9 1.3 %collective-permute-start.1 = (bf16[128,1024]{1,0:T(8,128)(2,1)}, bf16[128,1024]{1,0:T(8,128)(2,1)S(1)}, u32[]{:S(2)}, u32[]{:S(2)}) collective-permute-start(bf16[128,1024]{1,0:T(8,128)(2,1)} %get-tuple-element.29), channel_id=1, source_target_pairs={{0,1},{1,0},{2,3},{3,2},{4,5},{5,4},{6,7},{7,6},{8,9},{9,8},{10,11... | collective-permute-start | bytes 786440 | tf_op jit(solution)/shard_map/ppermute | solution.py:35
  4.2 1.3 %collective-permute-start.4 = (bf16[128,1024]{1,0:T(8,128)(2,1)}, bf16[128,1024]{1,0:T(8,128)(2,1)S(1)}, u32[]{:S(2)}, u32[]{:S(2)}) collective-permute-start(bf16[128,1024]{1,0:T(8,128)(2,1)} %get-tuple-element.26.own_ref.refs_0_.refs_1_.refs_2_), channel_id=1, source_target_pairs={{0,8},{2,10},{4,12},{6,14},{8,16},{10,18},{12,20},{14,22},{16,24},... | collective-permute-start | bytes 786440 | tf_op jit(solution)/shard_map/ppermute | solution.py:35
  5.5 0.0 copy-start
  5.5 1.0 %copy-done = bf16[128,1024]{1,0:T(8,128)(2,1)S(1)} copy-done((bf16[128,1024]{1,0:T(8,128)(2,1)S(1)}, bf16[128,1024]{1,0:T(8,128)(2,1)}, u32[]{:S(2)}) %copy-start) | copy-done | bytes 262168
  6.5 0.0 copy-start.1
  6.5 0.9 %copy-done.1 = f32[184,128]{1,0:T(8,128)S(1)} copy-done((f32[184,128]{1,0:T(8,128)S(1)}, f32[184,128]{1,0:T(8,128)}, u32[]{:S(2)}) %copy-start.1) | copy-done | bytes 94232
  7.3 1.2 %copy-done.2 = bf16[128,4096]{1,0:T(8,128)(2,1)S(1)} copy-done((bf16[128,4096]{1,0:T(8,128)(2,1)S(1)}, bf16[128,4096]{1,0:T(8,128)(2,1)}, u32[]{:S(2)}) %copy-start.2) | copy-done | bytes 1048600
  8.6 0.7 %q_prep.1 = (bf16[2048,128]{1,0:T(8,128)(2,1)S(1)}, bf16[2048,128]{1,0:T(8,128)(2,1)S(1)}, f32[8,128]{1,0:T(8,128)S(1)}) custom-call(bf16[128,4096]{1,0:T(8,128)(2,1)S(1)} %copy-done.2, f32[184,128]{1,0:T(8,128)S(1)} %copy-done.1, bf16[128,1024]{1,0:T(8,128)(2,1)S(1)} %copy-done), custom_call_target="tpu_custom_call" | custom-call | flops 11500000 | tf_op jit(solution)/shard_map/q_prep/pallas_call | solution.py:199
  9.3 0.3 collective-permute-start
  9.6 0.7 %collective-permute-done.1.refs_0_ = bf16[128,1024]{1,0:T(8,128)(2,1)S(1)} collective-permute-done((bf16[128,1024]{1,0:T(8,128)(2,1)}, bf16[128,1024]{1,0:T(8,128)(2,1)S(1)}, u32[]{:S(2)}, u32[]{:S(2)}) %collective-permute-start.1) | collective-permute-done | bytes 262176 | tf_op jit(solution)/shard_map/ppermute | solution.py:35
  10.3 2.8 %collective-permute-done.4.refs_0_ = bf16[128,1024]{1,0:T(8,128)(2,1)S(1)} collective-permute-done((bf16[128,1024]{1,0:T(8,128)(2,1)}, bf16[128,1024]{1,0:T(8,128)(2,1)S(1)}, u32[]{:S(2)}, u32[]{:S(2)}) %collective-permute-start.4) | collective-permute-done | bytes 262176 | tf_op jit(solution)/shard_map/ppermute | solution.py:35
  13.2 0.3 collective-permute-start.5
  13.5 0.0 collective-permute-start.2
  13.5 3.5 %collective-permute-start.3 = (bf16[128,1024]{1,0:T(8,128)(2,1)S(1)}, bf16[128,1024]{1,0:T(8,128)(2,1)S(1)}, u32[]{:S(2)}, u32[]{:S(2)}) collective-permute-start(bf16[128,1024]{1,0:T(8,128)(2,1)S(1)} %after.2.refs_1_.refs_2_.rest_ref.refs_3_.refs_0_), channel_id=1, source_target_pairs={{0,4},{2,6},{4,8},{6,10},{8,12},{10,14},{12,16},{14,18},{16,20},{1... | collective-permute-start | bytes 786440 | tf_op jit(solution)/shard_map/ppermute | solution.py:40
  17.0 0.0 copy-start.3
  17.0 1.1 %attend_part.3 = (f32[1,4,1,512]{3,2,1,0:T(1,128)S(1)}, f32[1,4,1,512]{3,2,1,0:T(1,128)S(1)}, f32[1,4,128,512]{3,2,1,0:T(8,128)S(1)}) custom-call(f32[184,128]{1,0:T(8,128)S(1)} %copy-done.1, bf16[2048,128]{1,0:T(8,128)(2,1)S(1)} %get-tuple-element.27.refs_0_, bf16[128,1024]{1,0:T(8,128)(2,1)S(1)} %copy-done, ...), custom_call_target="tpu_custom_call" | custom-call | flops 11500000 | tf_op jit(solution)/shard_map/attend_part/pallas_call | solution.py:453
  18.1 0.0 copy-done.3
  18.1 2.0 %pages.1 = (bf16[24,16,4,256]{3,2,1,0:T(4,128)(2,1)}, bf16[16,4,256]{2,1,0:T(4,128)(2,1)S(1)}) custom-call(f32[184,128]{1,0:T(8,128)S(1)} %copy-done.1, s32[1,24]{1,0:T(1,128)S(1)} %copy-done.3, bf16[128,1024]{1,0:T(8,128)(2,1)S(1)} %copy-done, bf16[128,1024]{1,0:T(8,128)(2,1)S(1)} %after.2.refs_1_.refs_2_.rest_ref.refs_3_.refs_0_), custom_call_target="tpu_custom_call" | custom-call | flops 11500000 | tf_op jit(solution)/shard_map/pages/pallas_call | solution.py:559
  20.2 0.0 collective-permute-done.5.refs_2_.refs_5_
  20.2 0.1 pick.4.refs_9_
  20.2 4.2 %collective-permute-start.7 = (bf16[256,1024]{1,0:T(8,128)(2,1)S(1)}, bf16[256,1024]{1,0:T(8,128)(2,1)S(1)}, u32[]{:S(2)}, u32[]{:S(2)}) collective-permute-start(bf16[256,1024]{1,0:T(8,128)(2,1)S(1)} %pick.4.refs_9_), channel_id=1, source_target_pairs={{0,2},{2,0},{4,6},{6,4},{8,10},{10,8},{12,14},{14,12},{16,18},{18,... | collective-permute-start | bytes 1572872 | tf_op jit(solution)/shard_map/ppermute | solution.py:45
  24.4 0.0 collective-permute-done.refs_1_
  24.4 2.7 %attend_part.4 = (f32[1,4,1,512]{3,2,1,0:T(1,128)S(1)}, f32[1,4,1,512]{3,2,1,0:T(1,128)S(1)}, f32[1,4,128,512]{3,2,1,0:T(8,128)S(1)}, f32[1,4,1,512]{3,2,1,0:T(1...) custom-call(f32[184,128]{1,0:T(8,128)S(1)} %copy-done.1, ...), custom_call_target="tpu_custom_call" | custom-call | flops 11500000 | tf_op jit(solution)/shard_map/attend_part/pallas_call | solution.py:453
  27.1 0.0 collective-permute-done.2.refs_1_.refs_2_
  27.1 0.0 collective-permute-done.3.refs_2_.refs_3_
  27.2 0.1 pick.5.refs_11_
  27.2 0.5 %collective-permute-start.6 = (bf16[256,1024]{1,0:T(8,128)(2,1)S(1)}, bf16[256,1024]{1,0:T(8,128)(2,1)S(1)}, u32[]{:S(2)}, u32[]{:S(2)}) collective-permute-start(bf16[256,1024]{1,0:T(8,128)(2,1)S(1)} %pick.5.refs_11_), channel_id=1, source_target_pairs={{0,2},{2,0},{4,6},{6,4},{8,10},{10,8},{12,14},{14,12},{16,18},{18,... | collective-permute-start | bytes 1572872 | tf_op jit(solution)/shard_map/ppermute | solution.py:45
  27.7 0.0 collective-permute-done.7.refs_4_.refs_10_
  27.7 3.4 %attend_part.5 = (f32[1,4,1,512]{3,2,1,0:T(1,128)S(1)}, f32[1,4,1,512]{3,2,1,0:T(1,128)S(1)}, f32[1,4,128,512]{3,2,1,0:T(8,128)S(1)}, f32[1,4,1,512]{3,2,1,0:T(1...) custom-call(f32[184,128]{1,0:T(8,128)S(1)} %copy-done.1, ...), custom_call_target="tpu_custom_call" | custom-call | flops 11500000 | tf_op jit(solution)/shard_map/attend_part/pallas_call | solution.py:453
  31.1 0.0 collective-permute-done.6.refs_2_
  31.1 3.1 %attend_last.1 = (bf16[256,2048]{1,0:T(8,128)(2,1)}, bf16[24,16,4,256]{3,2,1,0:T(4,128)(2,1)}) custom-call(f32[184,128]{1,0:T(8,128)S(1)} %copy-done.1, bf16[2048,128]{1,0:T(8,128)(2,1)S(1)} %get-tuple-element.27.refs_0_, bf16[2048,128]{1,0:T(8,128)(2,1)S(1)} %collective-permute-done.refs_1_, ...), custom_call_target="tpu_custom_call", output_to_operand_aliasing={{1}: (13, {})} | custom-call | flops 11500000 | tf_op jit(solution)/shard_map/attend_last/pallas_call | solution.py:453
  (4 shorter events, 0.0 us)
Async XLA Ops:
  2.9 7.5 %collective-permute-start.1 = (bf16[128,1024]{1,0:T(8,128)(2,1)}, bf16[128,1024]{1,0:T(8,128)(2,1)S(1)}, u32[]{:S(2)}, u32[]{:S(2)}) collective-permute-start(bf16[128,1024]{1,0:T(8,128)(2,1)} %get-tuple-element.29), channel_id=1, source_target_pairs={{0,1},{1,0},{2,3},{3,2},{4,5},{5,4},{6,7},{7,6},{8,9},{9,8},{10,11... | collective-permute-start | bytes 786440 | tf_op jit(solution)/shard_map/ppermute | solution.py:35
  4.2 9.0 %collective-permute-start.4 = (bf16[128,1024]{1,0:T(8,128)(2,1)}, bf16[128,1024]{1,0:T(8,128)(2,1)S(1)}, u32[]{:S(2)}, u32[]{:S(2)}) collective-permute-start(bf16[128,1024]{1,0:T(8,128)(2,1)} %get-tuple-element.26.own_ref.refs_0_.refs_1_.refs_2_), channel_id=1, source_target_pairs={{0,8},{2,10},{4,12},{6,14},{8,16},{10,18},{12,20},{14,22},{16,24},... | collective-permute-start | bytes 786440 | tf_op jit(solution)/shard_map/ppermute | solution.py:35
  5.5 1.0 %copy-start = (bf16[128,1024]{1,0:T(8,128)(2,1)S(1)}, bf16[128,1024]{1,0:T(8,128)(2,1)}, u32[]{:S(2)}) copy-start(bf16[128,1024]{1,0:T(8,128)(2,1)} %get-tuple-element.26.own_ref.refs_0_.refs_1_.refs_2_) | copy-start | bytes 786436
  6.5 0.9 %copy-start.1 = (f32[184,128]{1,0:T(8,128)S(1)}, f32[184,128]{1,0:T(8,128)}, u32[]{:S(2)}) copy-start(f32[184,128]{1,0:T(8,128)} %get-tuple-element.25.table_ref.table) | copy-start | bytes 282628
  7.3 1.2 %copy-start.2 = (bf16[128,4096]{1,0:T(8,128)(2,1)S(1)}, bf16[128,4096]{1,0:T(8,128)(2,1)}, u32[]{:S(2)}) copy-start(bf16[128,4096]{1,0:T(8,128)(2,1)} %q_ref.1) | copy-start | bytes 3145732
  9.3 15.1 %collective-permute-start = (bf16[2048,128]{1,0:T(8,128)(2,1)S(1)}, bf16[2048,128]{1,0:T(8,128)(2,1)S(1)}, u32[]{:S(2)}, u32[]{:S(2)}) collective-permute-start(bf16[2048,128]{1,0:T(8,128)(2,1)S(1)} %get-tuple-element.28), channel_id=1, source_target_pairs={{0,1},{1,0},{2,3},{3,2},{4,5},{5,4},{6,7},{7,6},{8,9},{9,8},{10,11... | collective-permute-start | bytes 1572872 | tf_op jit(solution)/shard_map/ppermute | solution.py:35
  13.2 7.0 %collective-permute-start.5 = (bf16[128,1024]{1,0:T(8,128)(2,1)S(1)}, bf16[128,1024]{1,0:T(8,128)(2,1)S(1)}, u32[]{:S(2)}, u32[]{:S(2)}) collective-permute-start(bf16[128,1024]{1,0:T(8,128)(2,1)S(1)} %pick.3), channel_id=1, source_target_pairs={{0,4},{2,6},{4,0},{6,2},{8,12},{10,14},{12,8},{14,10},{16,20},{18,... | collective-permute-start | bytes 786440 | tf_op jit(solution)/shard_map/ppermute | solution.py:45
  13.5 13.7 %collective-permute-start.2 = (bf16[128,1024]{1,0:T(8,128)(2,1)S(1)}, bf16[128,1024]{1,0:T(8,128)(2,1)S(1)}, u32[]{:S(2)}, u32[]{:S(2)}) collective-permute-start(bf16[128,1024]{1,0:T(8,128)(2,1)S(1)} %after.2.refs_1_.refs_2_.rest_ref.refs_3_.refs_0_), channel_id=1, source_target_pairs={{0,8},{2,10},{4,12},{6,14},{8,16},{10,18},{12,20},{14,22},{16,24},... | collective-permute-start | bytes 786440 | tf_op jit(solution)/shard_map/ppermute | solution.py:35
  13.5 13.7 %collective-permute-start.3 = (bf16[128,1024]{1,0:T(8,128)(2,1)S(1)}, bf16[128,1024]{1,0:T(8,128)(2,1)S(1)}, u32[]{:S(2)}, u32[]{:S(2)}) collective-permute-start(bf16[128,1024]{1,0:T(8,128)(2,1)S(1)} %after.2.refs_1_.refs_2_.rest_ref.refs_3_.refs_0_), channel_id=1, source_target_pairs={{0,4},{2,6},{4,8},{6,10},{8,12},{10,14},{12,16},{14,18},{16,20},{1... | collective-permute-start | bytes 786440 | tf_op jit(solution)/shard_map/ppermute | solution.py:40
  17.0 1.1 %copy-start.3 = (s32[1,24]{1,0:T(1,128)S(1)}, s32[1,24]{1,0:T(1,128)}, u32[]{:S(2)}) copy-start(s32[1,24]{1,0:T(1,128)} %refs_9_.1) | copy-start | bytes 292
  20.2 7.5 %collective-permute-start.7 = (bf16[256,1024]{1,0:T(8,128)(2,1)S(1)}, bf16[256,1024]{1,0:T(8,128)(2,1)S(1)}, u32[]{:S(2)}, u32[]{:S(2)}) collective-permute-start(bf16[256,1024]{1,0:T(8,128)(2,1)S(1)} %pick.4.refs_9_), channel_id=1, source_target_pairs={{0,2},{2,0},{4,6},{6,4},{8,10},{10,8},{12,14},{14,12},{16,18},{18,... | collective-permute-start | bytes 1572872 | tf_op jit(solution)/shard_map/ppermute | solution.py:45
  27.2 3.9 %collective-permute-start.6 = (bf16[256,1024]{1,0:T(8,128)(2,1)S(1)}, bf16[256,1024]{1,0:T(8,128)(2,1)S(1)}, u32[]{:S(2)}, u32[]{:S(2)}) collective-permute-start(bf16[256,1024]{1,0:T(8,128)(2,1)S(1)} %pick.5.refs_11_), channel_id=1, source_target_pairs={{0,2},{2,0},{4,6},{6,4},{8,10},{10,8},{12,14},{14,12},{16,18},{18,... | collective-permute-start | bytes 1572872 | tf_op jit(solution)/shard_map/ppermute | solution.py:45

commit v8 on v7

--- a/solution.py
+++ b/solution.py
@@ -644,7 +644,7 @@
     own4 = after(own4, rest)
     own2 = swap(pick(2, ((0, 1),), own, own4), 2)
     page_pool, head_page = pages(table, slot_order, own, rest, heads, segs)
-    own_mixed = pick(1, ((0, 1), (2,)), own, own4, own2, head_page, own_state[0])
+    own_mixed = pick(1, ((0, 1), (2,)), own, own4, own2, head_page)
     own_s = swap(own_mixed, 1)
 
     qs = [q_own, q_rest]

time: 34.5 us -> 35.7 us (1.035)
  the two profiles are of different devices: /device:TPU:5 before, /device:TPU:13 now
where the time goes in v8:
time: 35.7 us; the launch traced here: 35.4 us
  Pallas kernels  15.4 us (43%)
  starting transfers between devices  14.5 us (41%)
  local copies, waits for them, and re-layouts  3.1 us (9%)
  waiting for transfers between devices  1.66 us (5%)
  between operations  0.75 us (2%)
    pallas_call x4, Pallas kernels, attend(): pl.pallas_call(functools.partial(attend_body, heads, segs, tuple(plan), l...  10.3 us
    ppermute x3, starting transfers between devices, swap(): return lax.ppermute(x, 'tok', [(i, i ^ bit) for i in range(peers)])  6.12 us
    ppermute x4, starting transfers between devices, around(): return lax.ppermute(x, axis, [(i, (i + by) % peers) for i in range(peers)])  4.24 us
    ppermute x1, starting transfers between devices, onward(): return lax.ppermute(x, axis, [(i, i + by) for i in range(peers - by)])  4.14 us
    unnamed x8, local copies, waits for them, and re-layouts  3.1 us
    pallas_call x1, Pallas kernels, kv_prep(): pl.pallas_call(functools.partial(kv_prep_body, heads, lengths.shape[0]),...  2.25 us
    pallas_call x1, Pallas kernels, pages(): pl.pallas_call(functools.partial(pages_body, heads, segs, pool), out_shap...  2.01 us
    ppermute x4, waiting for transfers between devices, around(): return lax.ppermute(x, axis, [(i, (i + by) % peers) for i in range(peers)])  1.65 us
  transfers between devices with their start and end apart: 8, of which 2 were waited for; matrix products, arithmetic and copies ran while one was open for 0% of the time, Pallas kernels for 28%

profile of v8, /device:TPU:13, one launch (start us, length us, event | category | flops | bytes accessed | tf_op | source)
XLA Modules:
  0.0 35.4 jit_solution(1958153892215041023)
XLA Ops:
  0.6 2.3 %kv_prep.1 = (f32[184,128]{1,0:T(8,128)}, bf16[128,1024]{1,0:T(8,128)(2,1)}, bf16[128,1024]{1,0:T(8,128)(2,1)}) custom-call(s32[8]{0:T(128)} %lengths_in.1, bf16[128,1024]{1,0:T(8,128)(2,1)} %k_in.1, bf16[128,1024]{1,0:T(8,128)(2,1)} %v_in.1, f32[1,128]{1,0:T(1,128)} %bitcast.2, f32[1,128]{1,0:T(1,128)} %bitcast.3), custom_call_target="tpu_custom_call" | custom-call | flops 11500000 | tf_op jit(solution)/shard_map/kv_prep/pallas_call | solution.py:157
  2.9 1.3 %collective-permute-start.1 = (bf16[128,1024]{1,0:T(8,128)(2,1)}, bf16[128,1024]{1,0:T(8,128)(2,1)S(1)}, u32[]{:S(2)}, u32[]{:S(2)}) collective-permute-start(bf16[128,1024]{1,0:T(8,128)(2,1)} %get-tuple-element.29), channel_id=1, source_target_pairs={{0,1},{1,0},{2,3},{3,2},{4,5},{5,4},{6,7},{7,6},{8,9},{9,8},{10,11... | collective-permute-start | bytes 786440 | tf_op jit(solution)/shard_map/ppermute | solution.py:35
  4.2 1.3 %collective-permute-start.4 = (bf16[128,1024]{1,0:T(8,128)(2,1)}, bf16[128,1024]{1,0:T(8,128)(2,1)S(1)}, u32[]{:S(2)}, u32[]{:S(2)}) collective-permute-start(bf16[128,1024]{1,0:T(8,128)(2,1)} %get-tuple-element.26.own_ref.refs_0_.refs_1_.refs_2_), channel_id=1, source_target_pairs={{0,8},{2,10},{4,12},{6,14},{8,16},{10,18},{12,20},{14,22},{16,24},... | collective-permute-start | bytes 786440 | tf_op jit(solution)/shard_map/ppermute | solution.py:35
  5.5 0.0 copy-start
  5.5 1.0 %copy-done = bf16[128,1024]{1,0:T(8,128)(2,1)S(1)} copy-done((bf16[128,1024]{1,0:T(8,128)(2,1)S(1)}, bf16[128,1024]{1,0:T(8,128)(2,1)}, u32[]{:S(2)}) %copy-start) | copy-done | bytes 262168
  6.5 0.0 copy-start.1
  6.5 0.9 %copy-done.1 = f32[184,128]{1,0:T(8,128)S(1)} copy-done((f32[184,128]{1,0:T(8,128)S(1)}, f32[184,128]{1,0:T(8,128)}, u32[]{:S(2)}) %copy-start.1) | copy-done | bytes 94232
  7.3 0.0 copy-start.2
  7.3 1.2 %copy-done.2 = bf16[128,4096]{1,0:T(8,128)(2,1)S(1)} copy-done((bf16[128,4096]{1,0:T(8,128)(2,1)S(1)}, bf16[128,4096]{1,0:T(8,128)(2,1)}, u32[]{:S(2)}) %copy-start.2) | copy-done | bytes 1048600
  8.6 0.7 %q_prep.1 = (bf16[2048,128]{1,0:T(8,128)(2,1)S(1)}, bf16[2048,128]{1,0:T(8,128)(2,1)S(1)}, f32[8,128]{1,0:T(8,128)S(1)}) custom-call(bf16[128,4096]{1,0:T(8,128)(2,1)S(1)} %copy-done.2, f32[184,128]{1,0:T(8,128)S(1)} %copy-done.1, bf16[128,1024]{1,0:T(8,128)(2,1)S(1)} %copy-done), custom_call_target="tpu_custom_call" | custom-call | flops 11500000 | tf_op jit(solution)/shard_map/q_prep/pallas_call | solution.py:199
  9.3 0.3 collective-permute-start
  9.6 0.7 %collective-permute-done.1.refs_0_ = bf16[128,1024]{1,0:T(8,128)(2,1)S(1)} collective-permute-done((bf16[128,1024]{1,0:T(8,128)(2,1)}, bf16[128,1024]{1,0:T(8,128)(2,1)S(1)}, u32[]{:S(2)}, u32[]{:S(2)}) %collective-permute-start.1) | collective-permute-done | bytes 262176 | tf_op jit(solution)/shard_map/ppermute | solution.py:35
  10.3 0.9 %collective-permute-done.4.refs_0_ = bf16[128,1024]{1,0:T(8,128)(2,1)S(1)} collective-permute-done((bf16[128,1024]{1,0:T(8,128)(2,1)}, bf16[128,1024]{1,0:T(8,128)(2,1)S(1)}, u32[]{:S(2)}, u32[]{:S(2)}) %collective-permute-start.4) | collective-permute-done | bytes 262176 | tf_op jit(solution)/shard_map/ppermute | solution.py:35
  11.3 0.3 collective-permute-start.5
  11.6 4.1 %collective-permute-start.3 = (bf16[128,1024]{1,0:T(8,128)(2,1)S(1)}, bf16[128,1024]{1,0:T(8,128)(2,1)S(1)}, u32[]{:S(2)}, u32[]{:S(2)}) collective-permute-start(bf16[128,1024]{1,0:T(8,128)(2,1)S(1)} %after.2.refs_1_.refs_2_.rest_ref.refs_3_.refs_0_), channel_id=1, source_target_pairs={{0,4},{2,6},{4,8},{6,10},{8,12},{10,14},{12,16},{14,18},{16,20},{1... | collective-permute-start | bytes 786440 | tf_op jit(solution)/shard_map/ppermute | solution.py:40
  15.7 1.3 %collective-permute-start.2 = (bf16[128,1024]{1,0:T(8,128)(2,1)S(1)}, bf16[128,1024]{1,0:T(8,128)(2,1)S(1)}, u32[]{:S(2)}, u32[]{:S(2)}) collective-permute-start(bf16[128,1024]{1,0:T(8,128)(2,1)S(1)} %after.2.refs_1_.refs_2_.rest_ref.refs_3_.refs_0_), channel_id=1, source_target_pairs={{0,8},{2,10},{4,12},{6,14},{8,16},{10,18},{12,20},{14,22},{16,24},... | collective-permute-start | bytes 786440 | tf_op jit(solution)/shard_map/ppermute | solution.py:35
  17.1 0.0 copy-done.3
  17.1 2.0 %pages.1 = (bf16[24,16,4,256]{3,2,1,0:T(4,128)(2,1)}, bf16[16,4,256]{2,1,0:T(4,128)(2,1)S(1)}) custom-call(f32[184,128]{1,0:T(8,128)S(1)} %copy-done.1, s32[1,24]{1,0:T(1,128)S(1)} %copy-done.3, bf16[128,1024]{1,0:T(8,128)(2,1)S(1)} %copy-done, bf16[128,1024]{1,0:T(8,128)(2,1)S(1)} %after.2.refs_1_.refs_2_.rest_ref.refs_3_.refs_0_), custom_call_target="tpu_custom_call" | custom-call | flops 11500000 | tf_op jit(solution)/shard_map/pages/pallas_call | solution.py:559
  19.1 1.1 %attend_part.3 = (f32[1,4,1,512]{3,2,1,0:T(1,128)S(1)}, f32[1,4,1,512]{3,2,1,0:T(1,128)S(1)}, f32[1,4,128,512]{3,2,1,0:T(8,128)S(1)}) custom-call(f32[184,128]{1,0:T(8,128)S(1)} %copy-done.1, bf16[2048,128]{1,0:T(8,128)(2,1)S(1)} %get-tuple-element.27.refs_0_, bf16[128,1024]{1,0:T(8,128)(2,1)S(1)} %copy-done, ...), custom_call_target="tpu_custom_call" | custom-call | flops 11500000 | tf_op jit(solution)/shard_map/attend_part/pallas_call | solution.py:453
  20.2 0.0 collective-permute-done.5.refs_2_.refs_5_
  20.2 0.1 pick.4.refs_9_
  20.2 2.8 %collective-permute-start.7 = (bf16[256,1024]{1,0:T(8,128)(2,1)S(1)}, bf16[256,1024]{1,0:T(8,128)(2,1)S(1)}, u32[]{:S(2)}, u32[]{:S(2)}) collective-permute-start(bf16[256,1024]{1,0:T(8,128)(2,1)S(1)} %pick.4.refs_9_), channel_id=1, source_target_pairs={{0,2},{2,0},{4,6},{6,4},{8,10},{10,8},{12,14},{14,12},{16,18},{18,... | collective-permute-start | bytes 1572872 | tf_op jit(solution)/shard_map/ppermute | solution.py:45
  23.0 0.0 collective-permute-done.refs_1_
  23.0 2.7 %attend_part.4 = (f32[1,4,1,512]{3,2,1,0:T(1,128)S(1)}, f32[1,4,1,512]{3,2,1,0:T(1,128)S(1)}, f32[1,4,128,512]{3,2,1,0:T(8,128)S(1)}, f32[1,4,1,512]{3,2,1,0:T(1...) custom-call(f32[184,128]{1,0:T(8,128)S(1)} %copy-done.1, ...), custom_call_target="tpu_custom_call" | custom-call | flops 11500000 | tf_op jit(solution)/shard_map/attend_part/pallas_call | solution.py:453
  25.7 0.0 collective-permute-done.3.refs_2_.refs_3_
  25.8 0.0 collective-permute-done.2.refs_1_.refs_2_
  25.8 0.1 pick.5.refs_11_
  25.8 3.1 %collective-permute-start.6 = (bf16[256,1024]{1,0:T(8,128)(2,1)S(1)}, bf16[256,1024]{1,0:T(8,128)(2,1)S(1)}, u32[]{:S(2)}, u32[]{:S(2)}) collective-permute-start(bf16[256,1024]{1,0:T(8,128)(2,1)S(1)} %pick.5.refs_11_), channel_id=1, source_target_pairs={{0,2},{2,0},{4,6},{6,4},{8,10},{10,8},{12,14},{14,12},{16,18},{18,... | collective-permute-start | bytes 1572872 | tf_op jit(solution)/shard_map/ppermute | solution.py:45
  28.9 0.0 collective-permute-done.7.refs_4_.refs_10_
  28.9 3.4 %attend_part.5 = (f32[1,4,1,512]{3,2,1,0:T(1,128)S(1)}, f32[1,4,1,512]{3,2,1,0:T(1,128)S(1)}, f32[1,4,128,512]{3,2,1,0:T(8,128)S(1)}, f32[1,4,1,512]{3,2,1,0:T(1...) custom-call(f32[184,128]{1,0:T(8,128)S(1)} %copy-done.1, ...), custom_call_target="tpu_custom_call" | custom-call | flops 11500000 | tf_op jit(solution)/shard_map/attend_part/pallas_call | solution.py:453
  32.3 0.0 collective-permute-done.6.refs_2_
  32.3 3.1 %attend_last.1 = (bf16[256,2048]{1,0:T(8,128)(2,1)}, bf16[24,16,4,256]{3,2,1,0:T(4,128)(2,1)}) custom-call(f32[184,128]{1,0:T(8,128)S(1)} %copy-done.1, bf16[2048,128]{1,0:T(8,128)(2,1)S(1)} %get-tuple-element.27.refs_0_, bf16[2048,128]{1,0:T(8,128)(2,1)S(1)} %collective-permute-done.refs_1_, ...), custom_call_target="tpu_custom_call", output_to_operand_aliasing={{1}: (13, {})} | custom-call | flops 11500000 | tf_op jit(solution)/shard_map/attend_last/pallas_call | solution.py:453
  (4 shorter events, 0.0 us)
Async XLA Ops:
  2.9 7.5 %collective-permute-start.1 = (bf16[128,1024]{1,0:T(8,128)(2,1)}, bf16[128,1024]{1,0:T(8,128)(2,1)S(1)}, u32[]{:S(2)}, u32[]{:S(2)}) collective-permute-start(bf16[128,1024]{1,0:T(8,128)(2,1)} %get-tuple-element.29), channel_id=1, source_target_pairs={{0,1},{1,0},{2,3},{3,2},{4,5},{5,4},{6,7},{7,6},{8,9},{9,8},{10,11... | collective-permute-start | bytes 786440 | tf_op jit(solution)/shard_map/ppermute | solution.py:35
  4.2 7.1 %collective-permute-start.4 = (bf16[128,1024]{1,0:T(8,128)(2,1)}, bf16[128,1024]{1,0:T(8,128)(2,1)S(1)}, u32[]{:S(2)}, u32[]{:S(2)}) collective-permute-start(bf16[128,1024]{1,0:T(8,128)(2,1)} %get-tuple-element.26.own_ref.refs_0_.refs_1_.refs_2_), channel_id=1, source_target_pairs={{0,8},{2,10},{4,12},{6,14},{8,16},{10,18},{12,20},{14,22},{16,24},... | collective-permute-start | bytes 786440 | tf_op jit(solution)/shard_map/ppermute | solution.py:35
  5.5 1.0 %copy-start = (bf16[128,1024]{1,0:T(8,128)(2,1)S(1)}, bf16[128,1024]{1,0:T(8,128)(2,1)}, u32[]{:S(2)}) copy-start(bf16[128,1024]{1,0:T(8,128)(2,1)} %get-tuple-element.26.own_ref.refs_0_.refs_1_.refs_2_) | copy-start | bytes 786436
  6.5 0.9 %copy-start.1 = (f32[184,128]{1,0:T(8,128)S(1)}, f32[184,128]{1,0:T(8,128)}, u32[]{:S(2)}) copy-start(f32[184,128]{1,0:T(8,128)} %get-tuple-element.25.table_ref.table) | copy-start | bytes 282628
  7.3 1.2 %copy-start.2 = (bf16[128,4096]{1,0:T(8,128)(2,1)S(1)}, bf16[128,4096]{1,0:T(8,128)(2,1)}, u32[]{:S(2)}) copy-start(bf16[128,4096]{1,0:T(8,128)(2,1)} %q_ref.1) | copy-start | bytes 3145732
  9.3 13.7 %collective-permute-start = (bf16[2048,128]{1,0:T(8,128)(2,1)S(1)}, bf16[2048,128]{1,0:T(8,128)(2,1)S(1)}, u32[]{:S(2)}, u32[]{:S(2)}) collective-permute-start(bf16[2048,128]{1,0:T(8,128)(2,1)S(1)} %get-tuple-element.28), channel_id=1, source_target_pairs={{0,1},{1,0},{2,3},{3,2},{4,5},{5,4},{6,7},{7,6},{8,9},{9,8},{10,11... | collective-permute-start | bytes 1572872 | tf_op jit(solution)/shard_map/ppermute | solution.py:35
  11.2 5.8 %copy-start.3 = (s32[1,24]{1,0:T(1,128)S(1)}, s32[1,24]{1,0:T(1,128)}, u32[]{:S(2)}) copy-start(s32[1,24]{1,0:T(1,128)} %refs_9_.1) | copy-start | bytes 292
  11.3 8.9 %collective-permute-start.5 = (bf16[128,1024]{1,0:T(8,128)(2,1)S(1)}, bf16[128,1024]{1,0:T(8,128)(2,1)S(1)}, u32[]{:S(2)}, u32[]{:S(2)}) collective-permute-start(bf16[128,1024]{1,0:T(8,128)(2,1)S(1)} %pick.3), channel_id=1, source_target_pairs={{0,4},{2,6},{4,0},{6,2},{8,12},{10,14},{12,8},{14,10},{16,20},{18,... | collective-permute-start | bytes 786440 | tf_op jit(solution)/shard_map/ppermute | solution.py:45
  11.6 14.2 %collective-permute-start.3 = (bf16[128,1024]{1,0:T(8,128)(2,1)S(1)}, bf16[128,1024]{1,0:T(8,128)(2,1)S(1)}, u32[]{:S(2)}, u32[]{:S(2)}) collective-permute-start(bf16[128,1024]{1,0:T(8,128)(2,1)S(1)} %after.2.refs_1_.refs_2_.rest_ref.refs_3_.refs_0_), channel_id=1, source_target_pairs={{0,4},{2,6},{4,8},{6,10},{8,12},{10,14},{12,16},{14,18},{16,20},{1... | collective-permute-start | bytes 786440 | tf_op jit(solution)/shard_map/ppermute | solution.py:40
  15.7 10.0 %collective-permute-start.2 = (bf16[128,1024]{1,0:T(8,128)(2,1)S(1)}, bf16[128,1024]{1,0:T(8,128)(2,1)S(1)}, u32[]{:S(2)}, u32[]{:S(2)}) collective-permute-start(bf16[128,1024]{1,0:T(8,128)(2,1)S(1)} %after.2.refs_1_.refs_2_.rest_ref.refs_3_.refs_0_), channel_id=1, source_target_pairs={{0,8},{2,10},{4,12},{6,14},{8,16},{10,18},{12,20},{14,22},{16,24},... | collective-permute-start | bytes 786440 | tf_op jit(solution)/shard_map/ppermute | solution.py:35
  20.2 8.6 %collective-permute-start.7 = (bf16[256,1024]{1,0:T(8,128)(2,1)S(1)}, bf16[256,1024]{1,0:T(8,128)(2,1)S(1)}, u32[]{:S(2)}, u32[]{:S(2)}) collective-permute-start(bf16[256,1024]{1,0:T(8,128)(2,1)S(1)} %pick.4.refs_9_), channel_id=1, source_target_pairs={{0,2},{2,0},{4,6},{6,4},{8,10},{10,8},{12,14},{14,12},{16,18},{18,... | collective-permute-start | bytes 1572872 | tf_op jit(solution)/shard_map/ppermute | solution.py:45
  25.8 6.5 %collective-permute-start.6 = (bf16[256,1024]{1,0:T(8,128)(2,1)S(1)}, bf16[256,1024]{1,0:T(8,128)(2,1)S(1)}, u32[]{:S(2)}, u32[]{:S(2)}) collective-permute-start(bf16[256,1024]{1,0:T(8,128)(2,1)S(1)} %pick.5.refs_11_), channel_id=1, source_target_pairs={{0,2},{2,0},{4,6},{6,4},{8,10},{10,8},{12,14},{14,12},{16,18},{18,... | collective-permute-start | bytes 1572872 | tf_op jit(solution)/shard_map/ppermute | solution.py:45
